TPU v7x, 128 devices: a whole 4x4x4 slice. The times are simulated.
128 devices in a mesh: row: 8 (over y, z_lo), col: 16 (over z_hi, x, core).
Axes of the slice: x: 4, y: 4, z: 4 (z_hi: 2, z_lo: 2; z = z_hi * 2 + z_lo), core: 2. Of those that a mesh axis runs over, the one named last changes fastest.
Arguments:
- object_field: float32 [2, 4096, 8192], P(None, 'row', 'col'), may hold values from -6 to 6
- probe_field: float32 [2, 128, 128], replicated, may hold values from -1 to 1
- amplitudes: float32 [192, 128, 2048], P('row', None, 'col'), may hold values from 0 to 2
- positions: int32 [8, 16, 2, 24], P('row', 'col'), may hold values from -32 to 416
- counts: int32 [8, 16], P('row', 'col'), may hold values from 8 to 24, as said below
Outputs:
- estimate: float32 [2, 4096, 8192], P(None, 'row', 'col')
- correction: float32 [2, 4096, 8192], P(None, 'row', 'col')
Inputs may be any that keep to these rules, and one draw needn't show every extreme that they name: `counts`: between 8 and 24 live slots per tile; some tile has exactly 24 and some exactly 8; slots at or beyond a tile's count carry data that is not used.
All inputs are finite; a program needn't handle non-finite values.
Results may differ from a plain program's by a relative error of at most 0.0001.
Values sent between devices are 32-bit elements; how exact they have to be, the bound alone decides.
A program may use at most 128 MiB of HBM per device.

v0:
```python
import jax
import jax.numpy as jnp
from jax import lax
from jax.sharding import PartitionSpec as P

BORDER = 32
ITERS = 2


smoothing = 0.5
step_gain = 0.5
highest = lax.Precision.HIGHEST


def extended_2(cells, sides, width):
    for axis, dim in sides:
        count = lax.axis_size(axis)
        ends = count - 1
        head = lax.slice_in_dim(cells, 0, width, axis=dim)
        tail = lax.slice_in_dim(cells, cells.shape[dim] - width, cells.shape[dim], axis=dim)
        cells = jnp.concatenate(
            [
                lax.ppermute(tail, axis, [(i, (i + 1) % count) for i in range(ends)]),
                cells,
                lax.ppermute(head, axis, [((i + 1) % count, i) for i in range(ends)]),
            ],
            axis=dim,
        )
    return cells


def dft_tables(length):
    counter = jnp.arange(length, dtype=jnp.int32)
    product = counter[:, None] * counter[None, :] % length
    angles = 2.0 * jnp.pi / length * product.astype(jnp.float32)
    factor = 1.0 / jnp.sqrt(jnp.float32(length))
    return (jnp.cos(angles) * factor, -jnp.sin(angles) * factor)


def transform(real_part, imag_part, table_real, table_imag):
    left_real = jnp.einsum("kp,spq->skq", table_real, real_part, precision=highest) - jnp.einsum(
        "kp,spq->skq", table_imag, imag_part, precision=highest
    )
    left_imag = jnp.einsum("kp,spq->skq", table_real, imag_part, precision=highest) + jnp.einsum(
        "kp,spq->skq", table_imag, real_part, precision=highest
    )
    right_real = jnp.einsum("spq,qk->spk", left_real, table_real, precision=highest) - jnp.einsum(
        "spq,qk->spk", left_imag, table_imag, precision=highest
    )
    right_imag = jnp.einsum("spq,qk->spk", left_real, table_imag, precision=highest) + jnp.einsum(
        "spq,qk->spk", left_imag, table_real, precision=highest
    )
    return (right_real, right_imag)


def probe_gradient(patch_real, patch_imag, probe_field, amplitude, table_real, table_imag):
    probe_real = probe_field[0]
    probe_imag = probe_field[1]
    exit_real = probe_real * patch_real - probe_imag * patch_imag
    exit_imag = probe_real * patch_imag + probe_imag * patch_real
    wave_real, wave_imag = transform(exit_real, exit_imag, table_real, table_imag)
    modulus = jnp.sqrt(wave_real * wave_real + wave_imag * wave_imag + smoothing)
    shrink = amplitude / modulus - 1.0
    back_real, back_imag = transform(
        wave_real * shrink, wave_imag * shrink, table_real, -table_imag
    )
    grad_real = probe_real * back_real + probe_imag * back_imag
    grad_imag = probe_real * back_imag - probe_imag * back_real
    return (grad_real, grad_imag)


def on_device(object_field, probe_field, amplitudes, positions, counts):
    tile_size = object_field.shape[1]
    probe_size = probe_field.shape[1]
    slot_total = amplitudes.shape[0]
    extent = tile_size + 2 * BORDER
    table_real, table_imag = dft_tables(probe_size)
    step_rate = step_gain / (
        jnp.max(probe_field[0] * probe_field[0] + probe_field[1] * probe_field[1]) + 1e-06
    )
    row_start = positions[0, 0, 0] + BORDER
    col_start = positions[0, 0, 1] + BORDER
    live_count = counts[0, 0]
    zero_index = jnp.zeros((), jnp.int32)
    correction = jnp.zeros_like(object_field)
    for iteration in range(ITERS):
        extended = extended_2(object_field + correction, (("row", 1), ("col", 2)), BORDER)
        empty_sum = jnp.zeros((2, extent, extent), jnp.float32)

        def cut_patch(start_row, start_col):
            return lax.dynamic_slice(
                extended, (zero_index, start_row, start_col), (2, probe_size, probe_size)
            )

        patches = jax.vmap(cut_patch)(row_start, col_start)
        grad_real, grad_imag = probe_gradient(
            patches[:, 0], patches[:, 1], probe_field, amplitudes, table_real, table_imag
        )
        live_mask = (jnp.arange(slot_total, dtype=jnp.int32) < live_count).astype(jnp.float32)[
            :, None, None
        ]
        gradient = jnp.stack([grad_real * live_mask, grad_imag * live_mask], axis=1)

        def accumulate(slot_index, partial_value):
            corner = (zero_index, row_start[slot_index], col_start[slot_index])
            current = lax.dynamic_slice(partial_value, corner, (2, probe_size, probe_size))
            return lax.dynamic_update_slice(partial_value, current + gradient[slot_index], corner)

        gradient_sum = lax.fori_loop(0, slot_total, accumulate, empty_sum)
        framed = extended_2(gradient_sum, (("row", 1), ("col", 2)), BORDER)
        rows_done = framed[:, 2 * BORDER : 2 * BORDER + tile_size, :]
        rows_done = rows_done.at[:, 0:BORDER, :].add(framed[:, 0:BORDER, :])
        rows_done = rows_done.at[:, tile_size - BORDER :, :].add(
            framed[:, tile_size + 3 * BORDER :, :]
        )
        folded = rows_done[:, :, 2 * BORDER : 2 * BORDER + tile_size]
        folded = folded.at[:, :, 0:BORDER].add(rows_done[:, :, 0:BORDER])
        folded = folded.at[:, :, tile_size - BORDER :].add(
            rows_done[:, :, tile_size + 3 * BORDER :]
        )
        correction = correction + step_rate * folded
    return (object_field + correction, correction)


def solution(mesh):
    placed = (
        P(None, "row", "col"),
        P(),
        P("row", None, "col"),
        P("row", "col", None, None),
        P("row", "col"),
    )
    return jax.shard_map(
        on_device,
        mesh=mesh,
        in_specs=placed,
        out_specs=(P(None, "row", "col"), P(None, "row", "col")),
        check_vma=False,
    )
```

profile of v0, /device:TPU:39, one launch (start us, length us, event | category | flops | bytes accessed | tf_op | source)
XLA Modules:
  0.0 910.9 jit_solution(9619204748696223492)
XLA Ops:
  9.0 19.9 %collective-permute-done = f32[2,32,512]{1,2,0:T(8,128)S(1)} collective-permute-done((f32[2,32,512]{1,2,0:T(8,128)S(1)}, f32[2,32,512]{1,2,0:T(8,128)S(1)}, u32[]{:S(2)}, u32[]{:S(2)}) %collective-permute-start) | collective-permute-done | bytes 131104 | tf_op jit(solution)/shard_map/ppermute | solution.py:23
  29.7 5.9 collective-permute-start.2
  38.2 8.0 collective-permute-done.3
  46.3 3.4 pad_maximum_fusion.4
  50.0 75.7 %while.38 = (s32[]{:T(128)}, f32[2,576,576]{1,2,0:T(8,128)}, s32[24,3]{0,1:T(4,128)S(1)}, f32[24,2,128,128]{3,2,0,1:T(8,128)S(1)}, s32[]{:T(128)}) while((s32[]{:T(128)}, f32[2,576,576]{1,2,0:T(8,128)}, s32[24,3]{0,1:T(4,128)S(1)}, f32[24,2,128,128]{3,2,0,1:T(8,128)S(1)}, s32[]{:T(128)}) %tuple.141), condition=%wide.while_cond.8, body=%wide.while_body.8.sunk | while | flops 2 | bytes 786549 | solution.py:91
  148.5 3.3 fusion.113
  177.0 236.4 %while.36 = (s32[]{:T(128)}, f32[2,576,576]{2,1,0:T(8,128)}, s32[24]{0:T(128)S(1)}, s32[24]{0:T(128)S(1)}, f32[24,2,128,128]{3,2,0,1:T(8,128)}, /*index=5*/s32[]{:T(128)}, s32[]{:T(128)}, s32[]{:T(128)}) while((s32[]{:T(128)}, f32[2,576,576]{2,1,0:T(8,128)}, s32[24]{0:T(128)S(1)}, s32[24]{0:T(128)S(1)}, f32[24,2,128,128]{3,2,0,1:T(8,128)}, ...), condition=%wide.region_2.3_spmd, body=%wide.region_1.2_spmd.sunk | while | flops 32776 | bytes 655553 | solution.py:109
  183.2 3.5 dynamic_update_slice.16
  193.0 3.7 dynamic_update_slice.16
  202.8 3.7 dynamic_update_slice.16
  212.7 3.7 dynamic_update_slice.16
  222.6 3.7 dynamic_update_slice.16
  232.5 3.7 dynamic_update_slice.16
  242.4 3.6 dynamic_update_slice.16
  252.2 3.4 dynamic_update_slice.16
  261.8 3.7 dynamic_update_slice.16
  271.7 3.7 dynamic_update_slice.16
  281.6 3.7 dynamic_update_slice.16
  291.5 3.7 dynamic_update_slice.16
  301.4 3.7 dynamic_update_slice.16
  311.3 3.7 dynamic_update_slice.16
  321.2 3.7 dynamic_update_slice.16
  331.1 3.7 dynamic_update_slice.16
  341.0 3.6 dynamic_update_slice.16
  350.8 3.6 dynamic_update_slice.16
  360.6 3.6 dynamic_update_slice.16
  370.5 3.6 dynamic_update_slice.16
  380.3 3.5 dynamic_update_slice.16
  390.0 3.7 dynamic_update_slice.16
  399.9 3.6 dynamic_update_slice.16
  409.8 3.7 dynamic_update_slice.16
  414.5 4.6 collective-permute-start.4
  421.1 3.5 copy.122
  434.2 7.0 collective-permute-done.7
  447.7 5.5 scatter-add.26
  455.0 5.8 scatter-add.29
  466.3 3.5 collective-permute-start.8
  471.7 16.0 %collective-permute-done.8 = f32[2,32,512]{1,2,0:T(8,128)S(1)} collective-permute-done((f32[2,32,512]{1,2,0:T(8,128)S(1)}, f32[2,32,512]{1,2,0:T(8,128)S(1)}, u32[]{:S(2)}, u32[]{:S(2)}) %collective-permute-start.8) | collective-permute-done | bytes 131104 | tf_op jit(solution)/shard_map/ppermute | solution.py:23
  487.9 3.4 collective-permute-start.10
  493.5 8.0 collective-permute-done.11
  501.5 4.1 pad_maximum_fusion.5
  507.7 87.3 %while.39 = (s32[]{:T(128)}, f32[2,576,576]{1,2,0:T(8,128)}, s32[24,3]{0,1:T(4,128)S(1)}, f32[24,2,128,128]{3,2,0,1:T(8,128)}, s32[]{:T(128)}) while((s32[]{:T(128)}, f32[2,576,576]{1,2,0:T(8,128)}, s32[24,3]{0,1:T(4,128)S(1)}, f32[24,2,128,128]{3,2,0,1:T(8,128)}, s32[]{:T(128)}) %tuple.153), condition=%wide.while_cond.9, body=%wide.while_body.9.sunk | while | flops 2 | bytes 787057 | solution.py:91
  594.9 4.8 fusion.74
  646.8 205.2 %while.37 = (s32[]{:T(128)}, f32[2,576,576]{2,1,0:T(8,128)S(1)}, s32[24]{0:T(128)S(1)}, s32[24]{0:T(128)S(1)}, f32[24,2,128,128]{3,2,0,1:T(8,128)}, /*index=5*/s32[]{:T(128)}, s32[]{:T(128)}, s32[]{:T(128)}) while((s32[]{:T(128)}, f32[2,576,576]{2,1,0:T(8,128)S(1)}, s32[24]{0:T(128)S(1)}, s32[24]{0:T(128)S(1)}, f32[24,2,128,128]{3,2,0,1:T(8,128)}, ...), condition=%wide.region_4.5_spmd, body=%wide.region_3.4_spmd.sunk | while | flops 32776 | bytes 655553 | solution.py:109
  852.8 5.2 collective-permute-start.12
  873.3 8.0 collective-permute-done.15
  885.9 5.6 scatter-add.34
  894.1 5.8 scatter-add.35
  (540 shorter events, 499.5 us)
Async XLA Ops:
  2.6 43.7 %copy-start.2 = (f32[2,512,512]{1,2,0:T(8,128)}, f32[2,512,512]{1,2,0:T(8,128)S(1)}, u32[]{:S(2)}) copy-start(f32[2,512,512]{1,2,0:T(8,128)S(1)} %copy.148) | copy-start | bytes 6291460
  2.6 5.7 copy-start.17
  2.6 5.7 copy-start.15
  2.8 26.1 %collective-permute-start = (f32[2,32,512]{1,2,0:T(8,128)S(1)}, f32[2,32,512]{1,2,0:T(8,128)S(1)}, u32[]{:S(2)}, u32[]{:S(2)}) collective-permute-start(f32[2,32,512]{1,2,0:T(8,128)S(1)} %get-tuple-element.414), channel_id=1, source_target_pairs={{0,16},{16,32},{32,48},{48,64},{64,80},{80,96},{96,112},{1,17},{17... | collective-permute-start | bytes 393224 | tf_op jit(solution)/shard_map/ppermute | solution.py:23
  5.7 23.2 %collective-permute-start.1 = (f32[2,32,512]{1,2,0:T(8,128)S(1)}, f32[2,32,512]{1,2,0:T(8,128)S(1)}, u32[]{:S(2)}, u32[]{:S(2)}) collective-permute-start(f32[2,32,512]{1,2,0:T(8,128)S(1)} %get-tuple-element.415), channel_id=1, source_target_pairs={{16,0},{32,16},{48,32},{64,48},{80,64},{96,80},{112,96},{17,1},{33... | collective-permute-start | bytes 393224 | tf_op jit(solution)/shard_map/ppermute | solution.py:25
  29.7 8.5 collective-permute-start.2
  35.7 10.6 %collective-permute-start.3 = (f32[2,576,32]{1,2,0:T(8,128)}, f32[2,576,32]{1,2,0:T(8,128)}, u32[]{:S(2)}, u32[]{:S(2)}) collective-permute-start(f32[2,576,32]{1,2,0:T(8,128)} %get-tuple-element.407), channel_id=1, source_target_pairs={{1,0},{2,1},{3,2},{4,3},{5,4},{6,5},{7,6},{8,7},{9,8},{10,9},{11,1... | collective-permute-start | bytes 442376 | tf_op jit(solution)/shard_map/ppermute | solution.py:25
  145.7 2.8 copy-start
  414.5 10.1 %collective-permute-start.4 = (f32[2,32,576]{2,1,0:T(8,128)S(1)}, f32[2,32,576]{2,1,0:T(8,128)S(1)}, u32[]{:S(2)}, u32[]{:S(2)}) collective-permute-start(f32[2,32,576]{2,1,0:T(8,128)S(1)} %get-tuple-element.410), channel_id=1, source_target_pairs={{0,16},{16,32},{32,48},{48,64},{64,80},{80,96},{96,112},{1,17},{17... | collective-permute-start | bytes 442376 | tf_op jit(solution)/shard_map/ppermute | solution.py:23
  419.1 7.0 collective-permute-start.5
  426.3 6.5 copy-start.16
  428.2 6.0 collective-permute-start.6
  430.9 10.3 %collective-permute-start.7 = (f32[2,640,32]{1,2,0:T(8,128)S(1)}, f32[2,640,32]{1,2,0:T(8,128)S(1)}, u32[]{:S(2)}, u32[]{:S(2)}) collective-permute-start(f32[2,640,32]{1,2,0:T(8,128)S(1)} %get-tuple-element.399), channel_id=1, source_target_pairs={{1,0},{2,1},{3,2},{4,3},{5,4},{6,5},{7,6},{8,7},{9,8},{10,9},{11,1... | collective-permute-start | bytes 491528 | tf_op jit(solution)/shard_map/ppermute | solution.py:25
  434.2 9.8 %copy-start.11 = (f32[2,640,32]{1,2,0:T(8,128)}, f32[2,640,32]{1,2,0:T(8,128)S(1)}, u32[]{:S(2)}) copy-start(f32[2,640,32]{1,2,0:T(8,128)S(1)} %collective-permute-done.6) | copy-start | bytes 491524
  441.2 2.9 copy-start.12
  444.1 2.2 copy-start.1
  460.8 3.9 copy-start.3
  464.7 1.4 copy-start.7
  466.1 21.8 %copy-start.6 = (f32[2,512,512]{1,2,0:T(8,128)}, f32[2,512,512]{1,2,0:T(8,128)S(1)}, u32[]{:S(2)}) copy-start(f32[2,512,512]{1,2,0:T(8,128)S(1)} %multiply_add_fusion.1) | copy-start | bytes 6291460
  466.3 21.4 %collective-permute-start.8 = (f32[2,32,512]{1,2,0:T(8,128)S(1)}, f32[2,32,512]{1,2,0:T(8,128)S(1)}, u32[]{:S(2)}, u32[]{:S(2)}) collective-permute-start(f32[2,32,512]{1,2,0:T(8,128)S(1)} %get-tuple-element.412), channel_id=1, source_target_pairs={{0,16},{16,32},{32,48},{48,64},{64,80},{80,96},{96,112},{1,17},{17... | collective-permute-start | bytes 393224 | tf_op jit(solution)/shard_map/ppermute | solution.py:23
  469.7 18.0 %collective-permute-start.9 = (f32[2,32,512]{1,2,0:T(8,128)S(1)}, f32[2,32,512]{1,2,0:T(8,128)S(1)}, u32[]{:S(2)}, u32[]{:S(2)}) collective-permute-start(f32[2,32,512]{1,2,0:T(8,128)S(1)} %get-tuple-element.413), channel_id=1, source_target_pairs={{16,0},{32,16},{48,32},{64,48},{80,64},{96,80},{112,96},{17,1},{33... | collective-permute-start | bytes 393224 | tf_op jit(solution)/shard_map/ppermute | solution.py:25
  487.9 5.6 collective-permute-start.10
  491.3 10.3 %collective-permute-start.11 = (f32[2,576,32]{1,2,0:T(8,128)S(1)}, f32[2,576,32]{1,2,0:T(8,128)S(1)}, u32[]{:S(2)}, u32[]{:S(2)}) collective-permute-start(f32[2,576,32]{1,2,0:T(8,128)S(1)} %get-tuple-element.405), channel_id=1, source_target_pairs={{1,0},{2,1},{3,2},{4,3},{5,4},{6,5},{7,6},{8,7},{9,8},{10,9},{11,1... | collective-permute-start | bytes 442376 | tf_op jit(solution)/shard_map/ppermute | solution.py:25
  594.9 4.9 copy-start.5
  852.0 6.0 copy-start.9
  852.8 9.5 %collective-permute-start.12 = (f32[2,32,576]{2,1,0:T(8,128)S(1)}, f32[2,32,576]{2,1,0:T(8,128)}, u32[]{:S(2)}, u32[]{:S(2)}) collective-permute-start(f32[2,32,576]{2,1,0:T(8,128)S(1)} %get-tuple-element.408), channel_id=1, source_target_pairs={{0,16},{16,32},{32,48},{48,64},{64,80},{80,96},{96,112},{1,17},{17... | collective-permute-start | bytes 442376 | tf_op jit(solution)/shard_map/ppermute | solution.py:23
  858.0 7.3 collective-permute-start.13
  867.2 14.1 %copy-start.10 = (f32[2,32,576]{1,2,0:T(8,128)S(1)}, f32[2,32,576]{1,2,0:T(8,128)}, u32[]{:S(2)}) copy-start(f32[2,32,576]{1,2,0:T(8,128)} %copy.147) | copy-start | bytes 442372
  868.2 5.1 collective-permute-start.14
  871.0 10.3 %collective-permute-start.15 = (f32[2,640,32]{1,2,0:T(8,128)S(1)}, f32[2,640,32]{1,2,0:T(8,128)S(1)}, u32[]{:S(2)}, u32[]{:S(2)}) collective-permute-start(f32[2,640,32]{1,2,0:T(8,128)S(1)} %get-tuple-element.397), channel_id=1, source_target_pairs={{1,0},{2,1},{3,2},{4,3},{5,4},{6,5},{7,6},{8,7},{9,8},{10,9},{11,1... | collective-permute-start | bytes 491528 | tf_op jit(solution)/shard_map/ppermute | solution.py:25
  873.3 11.2 %copy-start.13 = (f32[2,640,32]{1,2,0:T(8,128)}, f32[2,640,32]{1,2,0:T(8,128)S(1)}, u32[]{:S(2)}) copy-start(f32[2,640,32]{1,2,0:T(8,128)S(1)} %collective-permute-done.14) | copy-start | bytes 491524
  881.3 3.2 copy-start.14
  899.9 3.9 copy-start.4
  899.9 3.9 copy-start.8
where the time goes:
time: 923 us; the launch traced here: 911 us
  local copies, waits for them, and re-layouts  417 us (45%)
  loops' own time  190 us (21%)
  matrix products  97.3 us (11%)
  other arithmetic  85.2 us (9%)
  waiting for transfers between devices  71.3 us (8%)
  starting transfers between devices  47 us (5%)
    another operation x2, loops' own time, on_device(): gradient_sum = lax.fori_loop(0, slot_total, accumulate, empty_sum)  188 us
    gather x240, local copies, waits for them, and re-layouts  161 us
    dynamic_update_slice x48, local copies, waits for them, and re-layouts, accumulate(): lax.dynamic_update_slice(partial_value, current + gradient[slot_index], c...  145 us
    dynamic_slice x96, local copies, waits for them, and re-layouts, accumulate(): corner = (zero_index, row_start[slot_index], col_start[slot_index])  56.3 us
    add x48, other arithmetic, accumulate(): current + gradient[slot_index]  52.1 us
    ppermute x8, waiting for transfers between devices, extended_2(): lax.ppermute(tail, axis, [(i, (i + 1) % count) for i in range(ends)])  37.1 us
    ppermute x8, waiting for transfers between devices, extended_2(): lax.ppermute(head, axis, [((i + 1) % count, i) for i in range(ends)])  34.2 us
    ppermute x8, starting transfers between devices, extended_2(): lax.ppermute(tail, axis, [(i, (i + 1) % count) for i in range(ends)])  31 us
  transfers between devices with their start and end apart: 16, of which 11 were waited for; matrix products, arithmetic and copies ran while one was open for 1% of the time, Pallas kernels for 0%

commit v1 on v0

v1 whole, which is shorter than its diff:
```python
import functools

import jax
import jax.numpy as jnp
import ml_dtypes
import numpy as np
from jax import lax
from jax.experimental import pallas as pl
from jax.experimental.pallas import tpu as pltpu
from jax.sharding import PartitionSpec as P

BORDER = 32
PROBE = 128
TILE = 512
ROWS = TILE + 2 * BORDER
BLOCKS = 6
GROUP = 8
smoothing = 0.5
step_gain = 0.5
f32 = jnp.float32
bf16 = jnp.bfloat16
MESH = pl.DeviceIdType.MESH

DIRS = ((-1, 0), (1, 0), (0, -1), (0, 1), (-1, -1), (-1, 1), (1, -1), (1, 1))
OPP = (1, 0, 3, 2, 7, 6, 5, 4)


def tables():
    n = np.arange(PROBE)
    angle = 2.0 * np.pi / PROBE * (n[:, None] * n[None, :] % PROBE)
    real, imag = np.cos(angle) / np.sqrt(PROBE), -np.sin(angle) / np.sqrt(PROBE)
    whole = np.block([[real, -imag], [imag, real]]).astype(np.float32)

    def halves(matrix):
        high = matrix.astype(ml_dtypes.bfloat16)
        return high, (matrix - high.astype(np.float32)).astype(ml_dtypes.bfloat16)

    high, low = halves(whole)
    high_t, low_t = halves(whole.T.copy())
    return (
        np.concatenate([high, high, low], 1),
        np.concatenate([high_t, high_t, low_t], 0),
        np.concatenate([high_t, high_t, low_t], 1),
        np.concatenate([high, high, low], 0),
    )


def split(value):
    high = value.astype(bf16)
    return high, (value - high.astype(f32)).astype(bf16)


def dot(a, b):
    return jnp.dot(a, b, preferred_element_type=f32)


def left(table, pairs):
    parts = [split(jnp.concatenate([a, b], 0)) for a, b in pairs]
    high = jnp.concatenate([p[0] for p in parts], 1)
    low = jnp.concatenate([p[1] for p in parts], 1)
    out = dot(table[...], jnp.concatenate([high, low, high], 0))
    n = PROBE
    return [(out[:n, n * k : n * k + n], out[n:, n * k : n * k + n]) for k in range(len(pairs))]


def right(table, pairs):
    parts = [split(jnp.concatenate([a, b], 1)) for a, b in pairs]
    high = jnp.concatenate([p[0] for p in parts], 0)
    low = jnp.concatenate([p[1] for p in parts], 0)
    out = dot(jnp.concatenate([high, low, high], 1), table[...])
    n = PROBE
    return [(out[n * k : n * k + n, :n], out[n * k : n * k + n, n:]) for k in range(len(pairs))]


def lanes(rows=PROBE):
    return lax.broadcasted_iota(jnp.int32, (rows, 128), 1)


def cut(cur, row, col):
    block, lane = col >> 7, col & 127
    out = []
    for p in range(2):
        a = cur[p, block, pl.ds(row, PROBE), :]
        b = cur[p, block + 1, pl.ds(row, PROBE), :]
        out.append(pltpu.roll(jnp.where(lanes() >= lane, a, b), (128 - lane) & 127, 1))
    return out


def place(acc, grad, row, col):
    block, lane = col >> 7, col & 127
    for p in range(2):
        g = pltpu.roll(grad[p], lane, 1)
        acc[p, block, pl.ds(row, PROBE), :] += jnp.where(lanes() >= lane, g, 0.0)
        acc[p, block + 1, pl.ds(row, PROBE), :] += jnp.where(lanes() >= lane, 0.0, g)


def all_slots(count, pos, cur, acc, amps, probe, tabs):
    forward_left, forward_right, back_left, back_right = tabs
    pr, pi = probe[0], probe[1]

    def body(i, carry):
        slots = [i * GROUP + k for k in range(GROUP)]
        corners = [(pos[0, s] + BORDER, pos[1, s] + 128) for s in slots]
        pairs = []
        for row, col in corners:
            a, b = cut(cur, row, col)
            pairs.append((pr * a - pi * b, pr * b + pi * a))
        waves = left(forward_left, right(forward_right, pairs))
        shrunk = []
        for (a, b), s in zip(waves, slots):
            k = amps[s] * lax.rsqrt(a * a + b * b + smoothing) - 1.0
            k = k * jnp.where(s < count, 1.0, 0.0)
            shrunk.append((a * k, b * k))
        backs = right(back_right, left(back_left, shrunk))
        for (a, b), (row, col) in zip(backs, corners):
            place(acc, (pr * a + pi * b, pr * b - pi * a), row, col)
        return carry

    lax.fori_loop(0, lax.div(count + GROUP - 1, GROUP), body, 0)


def step_of(probe):
    return step_gain / (jnp.max(probe[0] * probe[0] + probe[1] * probe[1]) + 1e-06)


def neighbours():
    rows, cols = lax.axis_size("row"), lax.axis_size("col")
    row, col = lax.axis_index("row"), lax.axis_index("col")
    out = []
    for dr, dc in DIRS:
        there = None
        for cond in (
            [row > 0] if dr < 0 else [row < rows - 1] if dr > 0 else []
        ) + ([col > 0] if dc < 0 else [col < cols - 1] if dc > 0 else []):
            there = cond if there is None else jnp.logical_and(there, cond)
        out.append((there, (row + dr, col + dc)))
    return out


def greet(near):
    barrier = pltpu.get_barrier_semaphore()
    total = 0
    for there, where in near:
        @pl.when(there)
        def _():
            pl.semaphore_signal(barrier, inc=1, device_id=where, device_id_type=MESH)
        total = total + there.astype(jnp.int32)
    pl.semaphore_wait(barrier, total)


def remote(k, near, sources, targets, send, recv):
    return pltpu.make_async_remote_copy(
        src_ref=sources[k],
        dst_ref=targets[OPP[k]],
        send_sem=send.at[k],
        recv_sem=recv.at[OPP[k]],
        device_id=near[k][1],
        device_id_type=MESH,
    )


def start_all(near, sources, targets, send, recv, which=range(8)):
    for k in which:
        @pl.when(near[k][0])
        def _():
            remote(k, near, sources, targets, send, recv).start()


def finish_all(near, sources, targets, send, recv):
    for k in range(8):
        @pl.when(near[k][0])
        def _():
            remote(k, near, sources, targets, send, recv).wait_send()
            pltpu.make_async_remote_copy(
                src_ref=sources[k],
                dst_ref=targets[k],
                send_sem=send.at[k],
                recv_sem=recv.at[k],
                device_id=near[k][1],
                device_id_type=MESH,
            ).wait_recv()


def split_refs(v, c, d):
    return [v.at[0], v.at[1], c.at[0], c.at[1]] + [d.at[k] for k in range(4)]


def pack(pieces, start):
    lane = lanes()
    out = None
    for q, piece in enumerate(pieces):
        turned = pltpu.roll(piece, (32 * q - start) % 128, 1)
        out = turned if out is None else jnp.where(lane >= 32 * q, turned, out)
    return out


def unpack(value, start):
    return [pltpu.roll(value, (start - 32 * q) % 128, 1) if (start - 32 * q) % 128 else value for q in range(4)]


def halo_kernel(obj, v, c, d, edge, corner, packed, send, recv, load):
    near = neighbours()
    loads = [
        pltpu.make_async_copy(obj.at[:, :, pl.ds(384 * k, 128)], edge.at[k], load.at[k]) for k in range(2)
    ]
    for copy in loads:
        copy.start()
    greet(near)
    targets = split_refs(v, c, d)
    sources = [obj.at[:, pl.ds(0, 32), :], obj.at[:, pl.ds(TILE - 32, 32), :], packed.at[0], packed.at[1]] + [
        corner.at[k] for k in range(4)
    ]
    start_all(near, sources, targets, send, recv, (0, 1))
    for k in range(2):
        loads[k].wait()
        for p in range(2):
            packed[k, p] = pack([edge[k, p, 128 * q : 128 * q + 128, :] for q in range(4)], 96 * k)
            for up in range(2):
                corner[2 * up + k, p] = edge[k, p, (TILE - 32) * up : (TILE - 32) * up + 32, :]
        start_all(near, sources, targets, send, recv, (2 + k, 4 + k, 6 + k))
    finish_all(near, sources, targets, send, recv)


def swap_kernel(sv, sc, sd, v, c, d, send, recv):
    near = neighbours()
    greet(near)
    sources, targets = split_refs(sv, sc, sd), split_refs(v, c, d)
    start_all(near, sources, targets, send, recv)
    finish_all(near, sources, targets, send, recv)


def present(near, k, value):
    return jnp.where(near[k][0], value, 0.0)


def first_kernel(count, pos, obj, hv, hc, hd, amps_hbm, probe, t0, t1, t2, t3, cur, acc, sv, sc, sd, amps, sems):
    near = neighbours()
    copies = [
        pltpu.make_async_copy(
            obj.at[:, :, pl.ds(128 * j, 128)], cur.at[:, j + 1, pl.ds(BORDER, TILE), :], sems.at[j]
        )
        for j in range(4)
    ] + [pltpu.make_async_copy(amps_hbm, amps, sems.at[4])]
    for copy in copies:
        copy.start()
    acc[...] = jnp.zeros_like(acc)
    for k, base in ((0, 0), (1, BORDER + TILE)):
        for j in range(4):
            for p in range(2):
                cur[p, j + 1, base : base + 32, :] = present(near, k, hv[k, p, :, 128 * j : 128 * j + 128])
    for k, block in ((0, 0), (1, 5)):
        for p in range(2):
            for q, piece in enumerate(unpack(hc[k, p], 0 if k else 96)):
                cur[p, block, BORDER + 128 * q : BORDER + 128 * q + 128, :] = present(near, 2 + k, piece)
    for k in range(4):
        base, block = (BORDER + TILE) * (k // 2), 5 * (k % 2)
        for p in range(2):
            cur[p, block, base : base + 32, :] = present(near, 4 + k, hd[k, p])
    for copy in copies:
        copy.wait()
    all_slots(count[0, 0], pos, cur, acc, amps, probe, (t0, t1, t2, t3))
    edge = lanes(64) >= 96
    for p in range(2):
        for k in range(2):
            base = TILE * k
            for j in range(4):
                sv[k, p, j] = acc[p, j + 1, base : base + 64, :]
            sv[k, p, 4] = jnp.where(edge, acc[p, 0, base : base + 64, :], acc[p, 5, base : base + 64, :])
            for side in range(2):
                a, b = acc[p, 4 * side, base : base + 64, :], acc[p, 4 * side + 1, base : base + 64, :]
                sd[2 * k + side, p] = jnp.where(edge, a, b)
        for side in range(2):
            a, b = acc[p, 4 * side], acc[p, 4 * side + 1]
            strip = jnp.where(lanes(ROWS) >= 96, a, b)
            low, high = strip[: ROWS // 2], pltpu.roll(strip[ROWS // 2 :], 64, 1)
            lane = lanes(ROWS // 2)
            middle = jnp.logical_and(lane >= 32, lane < 96)
            sc[side, p] = jnp.where(middle, high, low)


def second_kernel(
    count, pos, cur_in, acc_in, rv, rc, rd, amps_hbm, probe, t0, t1, t2, t3, corr, inner, fv, fc, fd, cur, acc, amps, sems
):
    near = neighbours()
    load = pltpu.make_async_copy(amps_hbm, amps, sems.at[0])
    load.start()
    step = step_of(probe)
    acc[...] = acc_in[...]
    edge = lanes(64) >= 96
    half = ROWS // 2
    for p in range(2):
        for k in range(2):
            base = TILE * k
            for j in range(4):
                acc[p, j + 1, base : base + 64, :] += present(near, k, rv[k, p, j])
            for side in range(2):
                mine = edge if side == 0 else jnp.logical_not(edge)
                acc[p, 5 * side, base : base + 64, :] += jnp.where(mine, present(near, k, rv[k, p, 4]), 0.0)
                both = present(near, 4 + 2 * k + side, rd[2 * k + side, p])
                acc[p, 4 * side, base : base + 64, :] += jnp.where(edge, both, 0.0)
                acc[p, 4 * side + 1, base : base + 64, :] += jnp.where(edge, 0.0, both)
        for side in range(2):
            both = present(near, 2 + side, rc[side, p])
            for q, piece in enumerate((both, pltpu.roll(both, 64, 1))):
                lane = lanes(half)
                acc[p, 4 * side, half * q : half * q + half, :] += jnp.where(lane >= 96, piece, 0.0)
                acc[p, 4 * side + 1, half * q : half * q + half, :] += jnp.where(lane < 32, piece, 0.0)
    cur[...] = cur_in[...] + step * acc[...]
    for k, base in ((0, 0), (1, BORDER + TILE)):
        cur[:, :, base : base + 32, :] = present(near, k, cur[:, :, base : base + 32, :])
    for k, block in ((0, 0), (1, 5)):
        cur[:, block] = present(near, 2 + k, cur[:, block])
    corr[...] = step * acc[:, 1:5, BORDER : BORDER + TILE, :]
    acc[...] = jnp.zeros_like(acc)
    load.wait()
    all_slots(count[0, 0], pos, cur, acc, amps, probe, (t0, t1, t2, t3))
    for p in range(2):
        for k in range(2):
            base = (BORDER + TILE) * k
            for j in range(4):
                fv[k, p, j] = acc[p, j + 1, base : base + 32, :]
            for side in range(2):
                fd[2 * k + side, p] = acc[p, 5 * side, base : base + 32, :]
        for side in range(2):
            fc[side, p] = pack(
                [acc[p, 5 * side, BORDER + 128 * q : BORDER + 128 * q + 128, :] for q in range(4)], 0 if side else 96
            )
    inner[...] = acc[:, 1:5, BORDER : BORDER + TILE, :]


def last_kernel(obj, corr, inner_in, gv, gc, gd, probe, est_out, corr_out, est, total, inner, sems):
    near = neighbours()
    loads = [
        pltpu.make_async_copy(obj.at[:, :, pl.ds(128 * j, 128)], est.at[:, j], sems.at[j]) for j in range(4)
    ]
    for load in loads:
        load.start()
    step = step_of(probe)
    inner[...] = inner_in[...]
    for p in range(2):
        for k in range(2):
            base = (TILE - 32) * k
            for j in range(4):
                inner[p, j, base : base + 32, :] += present(near, k, gv[k, p, j])
            for side in range(2):
                lane = lanes(32)
                mine = lane < 32 if side == 0 else lane >= 96
                both = present(near, 4 + 2 * k + side, gd[2 * k + side, p])
                inner[p, 3 * side, base : base + 32, :] += jnp.where(mine, both, 0.0)
        for side in range(2):
            lane = lanes()
            mine = lane < 32 if side == 0 else lane >= 96
            for q, piece in enumerate(unpack(gc[side, p], 96 if side else 0)):
                inner[p, 3 * side, 128 * q : 128 * q + 128, :] += jnp.where(mine, present(near, 2 + side, piece), 0.0)
    total[...] = corr[...] + step * inner[...]
    stores = []
    for j in range(4):
        stores.append(
            pltpu.make_async_copy(total.at[:, j], corr_out.at[:, :, pl.ds(128 * j, 128)], sems.at[4 + j])
        )
        stores[-1].start()
    for j in range(4):
        loads[j].wait()
        est[:, j] = est[:, j] + total[:, j]
        stores.append(pltpu.make_async_copy(est.at[:, j], est_out.at[:, :, pl.ds(128 * j, 128)], sems.at[8 + j]))
        stores[-1].start()
    for store in stores:
        store.wait()


VM = pl.BlockSpec(memory_space=pltpu.VMEM)
SM = pl.BlockSpec(memory_space=pltpu.SMEM)
ANY = pl.BlockSpec(memory_space=pl.ANY)


def shape(*dims):
    return jax.ShapeDtypeStruct(dims, f32)


def params(limit_mib=40, **kw):
    return pltpu.CompilerParams(vmem_limit_bytes=limit_mib * 2**20, **kw)


def on_device(object_field, probe_field, amplitudes, positions, counts):
    pos = positions[0, 0]
    tabs = [jnp.asarray(t) for t in tables()]
    dma = pltpu.SemaphoreType.DMA
    halo = (shape(2, 2, 32, TILE), shape(2, 2, 128, 128), shape(4, 2, 32, 128))
    hv, hc, hd = pl.pallas_call(
        halo_kernel,
        out_shape=halo,
        in_specs=[ANY],
        out_specs=[VM] * 3,
        scratch_shapes=[
            pltpu.VMEM((2, 2, TILE, 128), f32),
            pltpu.VMEM((4, 2, 32, 128), f32),
            pltpu.VMEM((2, 2, 128, 128), f32),
            dma((8,)),
            dma((8,)),
            dma((2,)),
        ],
        compiler_params=params(collective_id=0, has_side_effects=True),
        name="halo",
    )(object_field)
    ext = (2, BLOCKS, ROWS, 128)
    strips = (shape(2, 2, 5, 64, 128), shape(2, 2, ROWS // 2, 128), shape(4, 2, 64, 128))
    cur, acc, *sent = pl.pallas_call(
        first_kernel,
        out_shape=(shape(*ext), shape(*ext)) + strips,
        in_specs=[SM, SM, ANY, VM, VM, VM, ANY] + [VM] * 5,
        out_specs=[VM] * 5,
        scratch_shapes=[pltpu.VMEM((24, 128, 128), f32), dma((5,))],
        compiler_params=params(),
        name="first",
    )(counts, pos, object_field, hv, hc, hd, amplitudes, probe_field, *tabs)
    got = pl.pallas_call(
        swap_kernel,
        out_shape=strips,
        in_specs=[VM] * 3,
        out_specs=[VM] * 3,
        scratch_shapes=[dma((8,)), dma((8,))],
        compiler_params=params(collective_id=1, has_side_effects=True),
        name="strips",
    )(*sent)
    folds = (shape(2, 2, 4, 32, 128), shape(2, 2, 128, 128), shape(4, 2, 32, 128))
    tile = (2, 4, TILE, 128)
    corr, inner, *sent = pl.pallas_call(
        second_kernel,
        out_shape=(shape(*tile), shape(*tile)) + folds,
        in_specs=[SM, SM, VM, VM, VM, VM, VM, ANY] + [VM] * 5,
        out_specs=[VM] * 5,
        scratch_shapes=[
            pltpu.VMEM(ext, f32),
            pltpu.VMEM(ext, f32),
            pltpu.VMEM((24, 128, 128), f32),
            dma((1,)),
        ],
        compiler_params=params(),
        name="second",
    )(counts, pos, cur, acc, *got, amplitudes, probe_field, *tabs)
    got = pl.pallas_call(
        swap_kernel,
        out_shape=folds,
        in_specs=[VM] * 3,
        out_specs=[VM] * 3,
        scratch_shapes=[dma((8,)), dma((8,))],
        compiler_params=params(collective_id=2, has_side_effects=True),
        name="folds",
    )(*sent)
    return pl.pallas_call(
        last_kernel,
        out_shape=(shape(2, TILE, TILE), shape(2, TILE, TILE)),
        in_specs=[ANY] + [VM] * 6,
        out_specs=[ANY] * 2,
        scratch_shapes=[pltpu.VMEM(tile, f32)] * 3 + [dma((12,))],
        compiler_params=params(),
        name="last",
    )(object_field, corr, inner, *got, probe_field)


def solution(mesh):
    placed = (
        P(None, "row", "col"),
        P(),
        P("row", None, "col"),
        P("row", "col", None, None),
        P("row", "col"),
    )
    return jax.shard_map(
        on_device,
        mesh=mesh,
        in_specs=placed,
        out_specs=(P(None, "row", "col"), P(None, "row", "col")),
        check_vma=False,
    )
```

time: 923 us -> 81.7 us (0.09)
  the two profiles are of different devices: /device:TPU:39 before, /device:TPU:8 now
where the time goes in v1:
time: 81.7 us; the launch traced here: 81.1 us
  Pallas kernels  75.1 us (92%)
  local copies, waits for them, and re-layouts  4.6 us (6%)
  between operations  1.42 us (2%)
    pallas_call x1, Pallas kernels, on_device(): pl.pallas_call(swap_kernel, out_shape=strips, in_specs=[VM] * 3, out_spec...  26.5 us
    pallas_call x1, Pallas kernels, on_device(): pl.pallas_call(halo_kernel, out_shape=halo, in_specs=[ANY], out_specs=[VM...  13.9 us
    pallas_call x1, Pallas kernels, on_device(): pl.pallas_call(swap_kernel, out_shape=folds, in_specs=[VM] * 3, out_specs...  13.6 us
    pallas_call x1, Pallas kernels, on_device(): pl.pallas_call(second_kernel, out_shape=(shape(*tile), shape(*tile)) + fo...  9.5 us
    pallas_call x1, Pallas kernels, on_device(): pl.pallas_call(first_kernel, out_shape=(shape(*ext), shape(*ext)) + strip...  8.66 us
    unnamed x22, local copies, waits for them, and re-layouts  4.6 us
    pallas_call x1, Pallas kernels, on_device(): pl.pallas_call(last_kernel, out_shape=(shape(2, TILE, TILE), shape(2, TIL...  2.96 us

profile of v1, /device:TPU:8, one launch (start us, length us, event | category | flops | bytes accessed | tf_op | source)
XLA Modules:
  0.0 81.1 jit_solution(7234303063186630166)
XLA Ops:
  0.6 0.0 copy-start.10
  1.3 0.0 copy-start
  1.3 1.6 %copy-done = f32[2,512,512]{2,1,0:T(8,128)S(1)} copy-done((f32[2,512,512]{2,1,0:T(8,128)S(1)}, f32[2,512,512]{2,1,0:T(8,128)}, u32[]{:S(2)}) %copy-start) | copy-done | bytes 2097176
  2.9 0.0 copy-start.2
  2.9 0.0 copy-start.3
  2.9 0.0 copy-start.9
  2.9 13.9 %halo.1 = (f32[2,2,32,512]{3,2,1,0:T(8,128)S(1)}, f32[2,2,128,128]{3,2,1,0:T(8,128)S(1)}, f32[4,2,32,128]{3,2,1,0:T(8,128)S(1)}) custom-call(f32[2,512,512]{2,1,0:T(8,128)S(1)} %copy-done), custom_call_target="tpu_custom_call" | custom-call | tf_op jit(solution)/shard_map/halo/pallas_call | solution.py:389
  16.8 0.0 copy-done.10
  16.8 0.0 copy-done.2
  16.8 0.0 copy-done.3
  16.8 0.0 copy-done.9
  16.8 0.0 copy-start.4
  16.9 1.0 %copy-done.4 = bf16[256,768]{1,0:T(8,128)(2,1)S(1)} copy-done((bf16[256,768]{1,0:T(8,128)(2,1)S(1)}, bf16[256,768]{1,0:T(8,128)(2,1)}, u32[]{:S(2)}) %copy-start.4) | copy-done | bytes 393240
  17.8 0.0 copy-start.6
  17.8 1.0 %copy-done.6 = bf16[768,256]{1,0:T(8,128)(2,1)S(1)} copy-done((bf16[768,256]{1,0:T(8,128)(2,1)S(1)}, bf16[768,256]{1,0:T(8,128)(2,1)}, u32[]{:S(2)}) %copy-start.6) | copy-done | bytes 393240
  18.8 0.0 copy-start.8
  18.8 1.0 %copy-done.8 = bf16[256,768]{1,0:T(8,128)(2,1)S(1)} copy-done((bf16[256,768]{1,0:T(8,128)(2,1)S(1)}, bf16[256,768]{1,0:T(8,128)(2,1)}, u32[]{:S(2)}) %copy-start.8) | copy-done | bytes 393240
  19.8 0.0 copy-start.5
  19.8 0.0 copy-start.7
  19.8 8.7 %first.1 = (f32[2,6,576,128]{3,2,1,0:T(8,128)S(1)}, f32[2,6,576,128]{3,2,1,0:T(8,128)}, f32[2,2,5,64,128]{4,3,2,1,0:T(8,128)S(1)}, f32[2,2,288,128]{3,2,1,0:T(8,128)S(1)}, f32[4,2,64,128]{3,2,1,0:T(8,128)S(1)}) custom-call(s32[1,1]{1,0:T(1,128)S(6)} %copy.11.count, s32[2,24]{1,0:T(2,128)S(1)} %bitcast.1, f32[2,512,512]{2,1,0:T(8,128)S(1)} %copy-done, ...), custom_call_target="tpu_custom_call" | custom-call | tf_op jit(solution)/shard_map/first/pallas_call | solution.py:407
  28.5 26.5 %strips.1 = (f32[2,2,5,64,128]{4,3,2,1,0:T(8,128)S(1)}, f32[2,2,288,128]{3,2,1,0:T(8,128)S(1)}, f32[4,2,64,128]{3,2,1,0:T(8,128)S(1)}) custom-call(f32[2,2,5,64,128]{4,3,2,1,0:T(8,128)S(1)} %get-tuple-element.26.sv, f32[2,2,288,128]{3,2,1,0:T(8,128)S(1)} %get-tuple-element.27.sc, f32[4,2,64,128]{3,2,1,0:T(8,128)S(1)} %get-tuple-element.28.sd), custom_call_target="tpu_custom_call" | custom-call | tf_op jit(solution)/shard_map/strips/pallas_call | solution.py:416
  55.0 0.0 copy-done.5
  55.0 0.0 copy-done.7
  55.0 0.0 copy-start.1
  55.0 9.5 %second.1 = (f32[2,4,512,128]{3,2,1,0:T(8,128)S(1)}, f32[2,4,512,128]{3,2,1,0:T(8,128)S(1)}, f32[2,2,4,32,128]{4,3,2,1,0:T(8,128)S(1)}, f32[2,2,128,128]{3,2,1,0:T(8,128)S(1)}, f32[4,2,32,128]{3,2,1,0:T(8,128)S(1)}) custom-call(s32[1,1]{1,0:T(1,128)S(6)} %copy.11.count, s32[2,24]{1,0:T(2,128)S(1)} %bitcast.2, ...), custom_call_target="tpu_custom_call" | custom-call | tf_op jit(solution)/shard_map/second/pallas_call | solution.py:427
  64.5 13.6 %folds.1 = (f32[2,2,4,32,128]{4,3,2,1,0:T(8,128)S(1)}, f32[2,2,128,128]{3,2,1,0:T(8,128)S(1)}, f32[4,2,32,128]{3,2,1,0:T(8,128)S(1)}) custom-call(f32[2,2,4,32,128]{4,3,2,1,0:T(8,128)S(1)} %get-tuple-element.34.sv, f32[2,2,128,128]{3,2,1,0:T(8,128)S(1)} %get-tuple-element.35.sc, f32[4,2,32,128]{3,2,1,0:T(8,128)S(1)} %get-tuple-element.36.sd), custom_call_target="tpu_custom_call" | custom-call | tf_op jit(solution)/shard_map/folds/pallas_call | solution.py:441
  78.1 0.0 copy-done.1
  78.1 3.0 %last.1 = (f32[2,512,512]{2,1,0:T(8,128)}, f32[2,512,512]{2,1,0:T(8,128)}) custom-call(f32[2,512,512]{2,1,0:T(8,128)S(1)} %copy-done.1, f32[2,4,512,128]{3,2,1,0:T(8,128)S(1)} %get-tuple-element.32.corr, f32[2,4,512,128]{3,2,1,0:T(8,128)S(1)} %get-tuple-element.33.inner_in, f32[2,2,4,32,128]{4,3,2,1,0:T(8,128)S(1)} %get-tuple-element.37.gv, ...), custom_call_target="tpu_custom_call" | custom-call | tf_op jit(solution)/shard_map/last/pallas_call | solution.py:450
Async XLA Ops:
  0.6 16.2 %copy-start.10 = (s32[1,1,2,24]{3,2,1,0:T(2,128)S(1)}, s32[1,1,2,24]{3,2,1,0:T(2,128)}, u32[]{:S(2)}) copy-start(s32[1,1,2,24]{3,2,1,0:T(2,128)} %param.12) | copy-start | bytes 580
  1.3 1.6 %copy-start = (f32[2,512,512]{2,1,0:T(8,128)S(1)}, f32[2,512,512]{2,1,0:T(8,128)}, u32[]{:S(2)}) copy-start(f32[2,512,512]{2,1,0:T(8,128)} %obj.5) | copy-start | bytes 6291460
  2.9 13.9 %copy-start.2 = (f32[24,128,128]{2,1,0:T(8,128)S(1)}, f32[24,128,128]{2,1,0:T(8,128)}, u32[]{:S(2)}) copy-start(f32[24,128,128]{2,1,0:T(8,128)} %amps_hbm.3) | copy-start | bytes 4718596
  2.9 13.9 %copy-start.3 = (bf16[768,256]{1,0:T(8,128)(2,1)S(1)}, bf16[768,256]{1,0:T(8,128)(2,1)}, u32[]{:S(2)}) copy-start(bf16[768,256]{1,0:T(8,128)(2,1)} %constant.11.clone.t3) | copy-start | bytes 1179652
  2.9 13.9 %copy-start.9 = (f32[2,128,128]{2,1,0:T(8,128)S(1)}, f32[2,128,128]{2,1,0:T(8,128)}, u32[]{:S(2)}) copy-start(f32[2,128,128]{2,1,0:T(8,128)} %probe.5) | copy-start | bytes 393220
  16.8 1.0 %copy-start.4 = (bf16[256,768]{1,0:T(8,128)(2,1)S(1)}, bf16[256,768]{1,0:T(8,128)(2,1)}, u32[]{:S(2)}) copy-start(bf16[256,768]{1,0:T(8,128)(2,1)} %constant.10.clone.t2) | copy-start | bytes 1179652
  17.8 1.0 %copy-start.6 = (bf16[768,256]{1,0:T(8,128)(2,1)S(1)}, bf16[768,256]{1,0:T(8,128)(2,1)}, u32[]{:S(2)}) copy-start(bf16[768,256]{1,0:T(8,128)(2,1)} %constant.9.clone.t1) | copy-start | bytes 1179652
  18.8 1.0 %copy-start.8 = (bf16[256,768]{1,0:T(8,128)(2,1)S(1)}, bf16[256,768]{1,0:T(8,128)(2,1)}, u32[]{:S(2)}) copy-start(bf16[256,768]{1,0:T(8,128)(2,1)} %constant.8.clone.t0) | copy-start | bytes 1179652
  19.8 35.2 %copy-start.5 = (bf16[256,768]{1,0:T(8,128)(2,1)S(1)}, bf16[256,768]{1,0:T(8,128)(2,1)}, u32[]{:S(2)}) copy-start(bf16[256,768]{1,0:T(8,128)(2,1)} %constant.10.clone.t2) | copy-start | bytes 1179652
  19.8 35.2 %copy-start.7 = (bf16[768,256]{1,0:T(8,128)(2,1)S(1)}, bf16[768,256]{1,0:T(8,128)(2,1)}, u32[]{:S(2)}) copy-start(bf16[768,256]{1,0:T(8,128)(2,1)} %constant.9.clone.t1) | copy-start | bytes 1179652
  55.0 23.1 %copy-start.1 = (f32[2,512,512]{2,1,0:T(8,128)S(1)}, f32[2,512,512]{2,1,0:T(8,128)}, u32[]{:S(2)}) copy-start(f32[2,512,512]{2,1,0:T(8,128)} %obj.5) | copy-start | bytes 6291460

commit v2 on v1

v2 whole, which is shorter than its diff:
```python
import functools

import jax
import jax.numpy as jnp
import ml_dtypes
import numpy as np
from jax import lax
from jax.experimental import pallas as pl
from jax.experimental.pallas import tpu as pltpu
from jax.sharding import PartitionSpec as P

BORDER = 32
PROBE = 128
TILE = 512
PMAX = 24
ROWS = TILE + 2 * BORDER
BLOCKS = 6
GROUP = 8
smoothing = 0.5
step_gain = 0.5
f32 = jnp.float32
bf16 = jnp.bfloat16
MESH = pl.DeviceIdType.MESH

DIRS = ((-1, 0), (1, 0), (0, -1), (0, 1), (-1, -1), (-1, 1), (1, -1), (1, 1))
OPP = (1, 0, 3, 2, 7, 6, 5, 4)


def tables():
    n = np.arange(PROBE)
    angle = 2.0 * np.pi / PROBE * (n[:, None] * n[None, :] % PROBE)
    real, imag = np.cos(angle) / np.sqrt(PROBE), -np.sin(angle) / np.sqrt(PROBE)
    whole = np.block([[real, -imag], [imag, real]]).astype(np.float32)

    def halves(matrix):
        high = matrix.astype(ml_dtypes.bfloat16)
        return high, (matrix - high.astype(np.float32)).astype(ml_dtypes.bfloat16)

    return np.stack(halves(whole)), np.stack(halves(whole.T.copy()))


def split(value):
    high = value.astype(bf16)
    return high, (value - high.astype(f32)).astype(bf16)


def dot(a, b):
    return jnp.dot(a, b, preferred_element_type=f32)


def left(table, pairs):
    parts = [split(jnp.concatenate([a, b], 0)) for a, b in pairs]
    high = jnp.concatenate([p[0] for p in parts], 1)
    low = jnp.concatenate([p[1] for p in parts], 1)
    wide = jnp.concatenate([table[0], table[0], table[1]], 1)
    out = dot(wide, jnp.concatenate([high, low, high], 0))
    n = PROBE
    return [(out[:n, n * k : n * k + n], out[n:, n * k : n * k + n]) for k in range(len(pairs))]


def right(table, pairs):
    parts = [split(jnp.concatenate([a, b], 1)) for a, b in pairs]
    high = jnp.concatenate([p[0] for p in parts], 0)
    low = jnp.concatenate([p[1] for p in parts], 0)
    tall = jnp.concatenate([table[0], table[0], table[1]], 0)
    out = dot(jnp.concatenate([high, low, high], 1), tall)
    n = PROBE
    return [(out[n * k : n * k + n, :n], out[n * k : n * k + n, n:]) for k in range(len(pairs))]


def lanes(rows=PROBE):
    return lax.broadcasted_iota(jnp.int32, (rows, 128), 1)


def cut(cur, row, col):
    block, lane = col >> 7, col & 127
    out = []
    for p in range(2):
        a = cur[p, block, pl.ds(row, PROBE), :]
        b = cur[p, block + 1, pl.ds(row, PROBE), :]
        out.append(pltpu.roll(jnp.where(lanes() >= lane, a, b), (128 - lane) & 127, 1))
    return out


def place(acc, grad, row, col):
    block, lane = col >> 7, col & 127
    for p in range(2):
        g = pltpu.roll(grad[p], lane, 1)
        acc[p, block, pl.ds(row, PROBE), :] += jnp.where(lanes() >= lane, g, 0.0)
        acc[p, block + 1, pl.ds(row, PROBE), :] += jnp.where(lanes() >= lane, 0.0, g)


def gradients(cur, amps, probe, tabs, pos, slots, scale=None):
    forward, backward = tabs
    pr, pi = probe[0], probe[1]
    pairs = []
    for s in slots:
        a, b = cut(cur, *corner_of(pos, s))
        pairs.append((pr * a - pi * b, pr * b + pi * a))
    waves = left(forward, right(backward, pairs))
    shrunk = []
    for k, ((a, b), s) in enumerate(zip(waves, slots)):
        gain = amps[s] * lax.rsqrt(a * a + b * b + smoothing) - 1.0
        if scale is not None:
            gain = gain * scale[k]
        shrunk.append((a * gain, b * gain))
    backs = right(forward, left(backward, shrunk))
    return [(pr * a + pi * b, pr * b - pi * a) for a, b in backs]


def corner_of(pos, s):
    return pos[0, s] + BORDER, pos[1, s] + 128


def inside(pos, s, low, high):
    r, c = pos[0, s], pos[1, s]
    return jnp.logical_and(
        jnp.logical_and(r >= low, r <= high), jnp.logical_and(c >= low, c <= high)
    )


def listed_slots(amount, todo, pos, cur, acc, amps, probe, tabs):
    def body(i, carry):
        at = [i * GROUP + k for k in range(GROUP)]
        slots = [jnp.where(j < amount, todo[j], 0) for j in at]
        scale = [jnp.where(j < amount, 1.0, 0.0) for j in at]
        grads = gradients(cur, amps, probe, tabs, pos, slots, scale)
        for grad, s in zip(grads, slots):
            place(acc, grad, *corner_of(pos, s))
        return carry

    lax.fori_loop(0, lax.div(amount + GROUP - 1, GROUP), body, 0)


def step_of(probe):
    return step_gain / (jnp.max(probe[0] * probe[0] + probe[1] * probe[1]) + 1e-06)


def neighbours():
    rows, cols = lax.axis_size("row"), lax.axis_size("col")
    row, col = lax.axis_index("row"), lax.axis_index("col")
    out = []
    for dr, dc in DIRS:
        there = None
        for cond in (
            [row > 0] if dr < 0 else [row < rows - 1] if dr > 0 else []
        ) + ([col > 0] if dc < 0 else [col < cols - 1] if dc > 0 else []):
            there = cond if there is None else jnp.logical_and(there, cond)
        out.append((there, (row + dr, col + dc)))
    return out


def greet(near):
    barrier = pltpu.get_barrier_semaphore()
    total = 0
    for there, where in near:
        @pl.when(there)
        def _():
            pl.semaphore_signal(barrier, inc=1, device_id=where, device_id_type=MESH)
        total = total + there.astype(jnp.int32)
    pl.semaphore_wait(barrier, total)


def remote(k, near, source, target, send, recv, n):
    return pltpu.make_async_remote_copy(
        src_ref=source,
        dst_ref=target,
        send_sem=send.at[n],
        recv_sem=recv.at[n],
        device_id=near[k][1],
        device_id_type=MESH,
    )


class Post:
    def __init__(self, near, send, recv):
        self.near, self.send, self.recv = near, send, recv
        self.count, self.waits = 0, []

    def pair(self, k, outs, intos):
        for i, way in enumerate((k, OPP[k])):
            n = self.count + i
            @pl.when(self.near[way][0])
            def _(i=i, way=way, n=n):
                remote(way, self.near, outs[i], intos[1 - i], self.send, self.recv, n).start()

        def wait(base=self.count):
            for i, way in enumerate((k, OPP[k])):
                @pl.when(self.near[way][0])
                def _(i=i, way=way):
                    remote(way, self.near, outs[i], intos[i], self.send, self.recv, base + i).wait_send()
                    remote(way, self.near, outs[i], intos[i], self.send, self.recv, base + 1 - i).wait_recv()

        self.count += 2
        return wait


def pack(pieces, start):
    lane = lanes(pieces[0].shape[0])
    out = None
    for q, piece in enumerate(pieces):
        turn = (32 * q - start) % 128
        turned = pltpu.roll(piece, turn, 1) if turn else piece
        out = turned if out is None else jnp.where(lane >= 32 * q, turned, out)
    return out


def unpack(value, start):
    turns = [(start - 32 * q) % 128 for q in range(4)]
    return [pltpu.roll(value, turn, 1) if turn else value for turn in turns]


def pack_two(value):
    half = value.shape[0] // 2
    lane = lanes(half)
    middle = jnp.logical_and(lane >= 32, lane < 96)
    return jnp.where(middle, pltpu.roll(value[half:], 64, 1), value[:half])


def unpack_two(value):
    return jnp.concatenate([value, pltpu.roll(value, 64, 1)], 0)


def seam(a, b):
    return jnp.where(lanes(a.shape[0]) >= 96, a, b)


def present(near, k, value):
    return jnp.where(near[k][0], value, 0.0)


EARLY = 16
LATE = 8


def halo_kernel(
    count, pos, obj, amps_hbm, probe, t0, t1, cur, early, order, amps, hv, hc, hd, sc, sd, follow, send, recv, sems
):
    near = neighbours()
    tile_at = [
        pltpu.make_async_copy(
            obj.at[:, :, pl.ds(128 * j, 128)], cur.at[:, j + 1, pl.ds(BORDER, TILE), :], sems.at[j]
        )
        for j in range(4)
    ]
    for j in (0, 3, 1, 2):
        tile_at[j].start()
    measured = pltpu.make_async_copy(amps_hbm, amps, sems.at[4])
    measured.start()
    greet(near)
    post = Post(near, send, recv)
    waits = [post.pair(0, [obj.at[:, pl.ds(0, 32), :], obj.at[:, pl.ds(TILE - 32, 32), :]], [hv.at[0], hv.at[1]])]
    for side in range(2):
        tile_at[3 * side].wait()
        block, start = 1 + 3 * side, 96 * side
        for p in range(2):
            sc[side, p] = pack(
                [cur[p, block, BORDER + 128 * q : BORDER + 128 * q + 128, :] for q in range(4)], start
            )
            for ud in range(2):
                base = BORDER + (TILE - 32) * ud
                sd[2 * ud + side, p] = pack(
                    [cur[p, block, base + 8 * q : base + 8 * q + 8, :] for q in range(4)], start
                )
    waits.append(post.pair(4, [sd.at[0], sd.at[3]], [hd.at[0], hd.at[3]]))
    waits.append(post.pair(5, [sd.at[1], sd.at[2]], [hd.at[1], hd.at[2]]))
    waits.append(post.pair(2, [sc.at[0], sc.at[1]], [hc.at[0], hc.at[1]]))
    coming = jnp.int32(PMAX)
    follow[PMAX] = coming
    for s in range(PMAX - 1, -1, -1):
        keep = jnp.logical_and(s < count[0, 0], inside(pos, s, 0, TILE - PROBE))
        coming = jnp.where(keep, s, coming)
        follow[s] = coming
    coming = follow[0]
    for k in range(EARLY):
        order[k] = coming
        coming = follow[jnp.minimum(coming + 1, PMAX)]
    zeros = jnp.zeros((2, BLOCKS, BORDER, 128), f32)
    cur[:, :, 0:BORDER, :] = zeros
    cur[:, :, BORDER + TILE :, :] = zeros
    cur[:, 0] = jnp.zeros((2, ROWS, 128), f32)
    cur[:, 5] = jnp.zeros((2, ROWS, 128), f32)
    tile_at[1].wait()
    tile_at[2].wait()
    measured.wait()

    def body(i, carry):
        slots = [jnp.minimum(order[i * GROUP + k], PMAX - 1) for k in range(GROUP)]
        for k, (a, b) in enumerate(gradients(cur, amps, probe, (t0, t1), pos, slots)):
            early[i * GROUP + k, 0] = a
            early[i * GROUP + k, 1] = b
        return carry

    lax.fori_loop(0, EARLY // GROUP, body, 0)
    for wait in waits:
        wait()
    for p in range(2):
        for k in range(2):
            base = (BORDER + TILE) * k
            for j in range(4):
                cur[p, j + 1, base : base + 32, :] = present(near, k, hv[k, p, :, 128 * j : 128 * j + 128])
            for side in range(2):
                for q, piece in enumerate(unpack(hd[2 * k + side, p], 96 - 96 * side)):
                    cur[p, 5 * side, base + 8 * q : base + 8 * q + 8, :] = present(near, 4 + 2 * k + side, piece)
        for side in range(2):
            for q, piece in enumerate(unpack(hc[side, p], 96 - 96 * side)):
                at = BORDER + 128 * q
                cur[p, 5 * side, at : at + 128, :] = present(near, 2 + side, piece)


def first_kernel(count, pos, order, cur, early, amps, probe, t0, t1, acc, after, todo):
    live = count[0, 0]
    acc[...] = jnp.zeros_like(acc)

    def sort(s, carry):
        amount, kept = carry
        keep = inside(pos, s, 0, TILE - PROBE)
        done = jnp.logical_and(keep, kept < EARLY)

        @pl.when(jnp.logical_not(done))
        def _():
            todo[amount] = s

        return amount + jnp.where(done, 0, 1), kept + jnp.where(keep, 1, 0)

    amount, kept = lax.fori_loop(0, live, sort, (jnp.int32(0), jnp.int32(0)))

    def put(k, carry):
        place(acc, (early[k, 0], early[k, 1]), *corner_of(pos, order[k]))
        return carry

    lax.fori_loop(0, jnp.minimum(kept, EARLY), put, 0)
    listed_slots(amount, todo, pos, cur, acc, amps, probe, (t0, t1))
    after[...] = cur[...] + step_of(probe) * acc[...]


def strip_kernel(pos, acc, cur, amps, probe, t0, t1, grads, rv, rs, rc, rm, sv, ss, sc, sm, send, recv):
    near = neighbours()
    for p in range(2):
        for side in range(2):
            for ud in range(2):
                rows = pl.ds(TILE * ud, 64)
                sc[side, ud, p] = pack_two(seam(acc[p, 4 * side, rows, :], acc[p, 4 * side + 1, rows, :]))
    greet(near)
    post = Post(near, send, recv)
    corners = post.pair(2, [sc.at[0], sc.at[1]], [rc.at[0], rc.at[1]])
    waits = [
        post.pair(
            0,
            [acc.at[:, pl.ds(2, 2), pl.ds(TILE * ud, 64), :] for ud in range(2)],
            [rv.at[ud, :, pl.ds(1, 2)] for ud in range(2)],
        )
    ]
    for p in range(2):
        for side in range(2):
            sm[side, p] = pack_two(seam(acc[p, 4 * side, 64:TILE, :], acc[p, 4 * side + 1, 64:TILE, :]))
    waits.append(post.pair(2, [sm.at[0], sm.at[1]], [rm.at[0], rm.at[1]]))

    def body(i, carry):
        slots = [i * GROUP + k for k in range(GROUP)]
        for s, (a, b) in zip(slots, gradients(cur, amps, probe, (t0, t1), pos, slots)):
            grads[s, 0] = a
            grads[s, 1] = b
        return carry

    lax.fori_loop(0, 1, body, 0)
    corners()
    lane = lanes(64)
    for p in range(2):
        for ud in range(2):
            rows = pl.ds(TILE * ud, 64)
            west = present(near, 2, unpack_two(rc[0, ud, p]))
            east = present(near, 3, unpack_two(rc[1, ud, p]))
            sv[ud, p, 0] = acc[p, 1, rows, :] + jnp.where(lane < 32, west, 0.0)
            sv[ud, p, 1] = acc[p, 4, rows, :] + jnp.where(lane >= 96, east, 0.0)
            ss[ud, p] = pack_two(seam(acc[p, 0, rows, :] + west, acc[p, 5, rows, :] + east))
    for n, block in ((0, 0), (1, 3)):
        waits.append(
            post.pair(0, [sv.at[ud, :, n] for ud in range(2)], [rv.at[ud, :, block] for ud in range(2)])
        )
    waits.append(post.pair(0, [ss.at[0], ss.at[1]], [rs.at[0], rs.at[1]]))
    lax.fori_loop(1, PMAX // GROUP, body, 0)
    for wait in waits:
        wait()


def second_kernel(
    count, pos, acc_in, cur_in, rv, rs, rc, rm, grads, amps, probe, t0, t1, acc, cur, late, todo
):
    near = neighbours()
    step = step_of(probe)
    live = count[0, 0]
    acc[...] = acc_in[...]
    cur[...] = cur_in[...]

    def add(p, block, rows, value):
        acc[p, block, rows, :] += value
        cur[p, block, rows, :] += step * value

    for p in range(2):
        for ud in range(2):
            rows = pl.ds(TILE * ud, 64)
            for j in range(4):
                add(p, j + 1, rows, present(near, ud, rv[ud, p, j]))
            sides = present(near, ud, unpack_two(rs[ud, p]))
            lane = lanes(64)
            add(p, 0, rows, jnp.where(lane >= 96, sides, 0.0))
            add(p, 5, rows, jnp.where(lane < 32, sides, 0.0))
        for side in range(2):
            for rows, piece in (
                (pl.ds(0, 64), rc[side, 0, p]),
                (pl.ds(64, TILE - 64), rm[side, p]),
                (pl.ds(TILE, 64), rc[side, 1, p]),
            ):
                piece = present(near, 2 + side, unpack_two(piece))
                lane = lanes(piece.shape[0])
                add(p, 4 * side, rows, jnp.where(lane >= 96, piece, 0.0))
                add(p, 4 * side + 1, rows, jnp.where(lane < 32, piece, 0.0))
    for k in range(2):
        rows = pl.ds((BORDER + TILE) * k, BORDER)
        cur[:, :, rows, :] = present(near, k, cur[:, :, rows, :])
        cur[:, 5 * k] = present(near, 2 + k, cur[:, 5 * k])
        acc[:, :, rows, :] = jnp.zeros((2, BLOCKS, BORDER, 128), f32)
        acc[:, 5 * k] = jnp.zeros((2, ROWS, 128), f32)
    for k in range(LATE):
        late[k] = PMAX

    def sort(s, carry):
        amount, held = carry
        done = inside(pos, s, BORDER, TILE - PROBE - BORDER)
        hold = jnp.logical_and(
            jnp.logical_and(inside(pos, s, 0, TILE - PROBE), held < LATE), jnp.logical_not(done)
        )

        @pl.when(done)
        def _():
            place(acc, (grads[s, 0], grads[s, 1]), *corner_of(pos, s))

        @pl.when(hold)
        def _():
            late[held] = s

        now = jnp.logical_not(jnp.logical_or(done, hold))

        @pl.when(now)
        def _():
            todo[amount] = s

        return amount + jnp.where(now, 1, 0), held + jnp.where(hold, 1, 0)

    amount, _ = lax.fori_loop(0, live, sort, (jnp.int32(0), jnp.int32(0)))
    listed_slots(amount, todo, pos, cur, acc, amps, probe, (t0, t1))


def fold_kernel(pos, late, acc, cur, amps, probe, t0, t1, grads, gv, gc, gd, sc, sd, send, recv):
    near = neighbours()
    for p in range(2):
        for side in range(2):
            start = 96 - 96 * side
            for ud in range(2):
                base = (BORDER + TILE) * ud
                sd[2 * ud + side, p] = pack(
                    [acc[p, 5 * side, base + 8 * q : base + 8 * q + 8, :] for q in range(4)], start
                )
    greet(near)
    post = Post(near, send, recv)
    waits = [
        post.pair(
            0,
            [acc.at[:, pl.ds(1, 4), pl.ds((BORDER + TILE) * ud, BORDER), :] for ud in range(2)],
            [gv.at[0], gv.at[1]],
        ),
        post.pair(4, [sd.at[0], sd.at[3]], [gd.at[0], gd.at[3]]),
        post.pair(5, [sd.at[1], sd.at[2]], [gd.at[1], gd.at[2]]),
    ]
    for p in range(2):
        for side in range(2):
            sc[side, p] = pack(
                [acc[p, 5 * side, BORDER + 128 * q : BORDER + 128 * q + 128, :] for q in range(4)], 96 - 96 * side
            )
    waits.append(post.pair(2, [sc.at[0], sc.at[1]], [gc.at[0], gc.at[1]]))

    def body(i, carry):
        slots = [jnp.minimum(late[i * GROUP + k], PMAX - 1) for k in range(GROUP)]
        for k, (a, b) in enumerate(gradients(cur, amps, probe, (t0, t1), pos, slots)):
            grads[i * GROUP + k, 0] = a
            grads[i * GROUP + k, 1] = b
        return carry

    lax.fori_loop(0, LATE // GROUP, body, 0)
    for wait in waits:
        wait()


def last_kernel(
    pos, late, obj, acc_in, gv, gc, gd, grads, probe, est_out, corr_out, est, acc, sems
):
    near = neighbours()
    loads = [
        pltpu.make_async_copy(obj.at[:, :, pl.ds(128 * j, 128)], est.at[:, j], sems.at[j]) for j in range(4)
    ]
    for load in loads:
        load.start()
    step = step_of(probe)
    acc[...] = acc_in[...]

    def put(k, carry):
        s = late[k]

        @pl.when(s < PMAX)
        def _():
            place(acc, (grads[k, 0], grads[k, 1]), *corner_of(pos, s))

        return carry

    lax.fori_loop(0, LATE, put, 0)
    for p in range(2):
        for side in range(2):
            block, start = 1 + 3 * side, 96 * side

            def mine(rows):
                return lanes(rows) >= 96 if side else lanes(rows) < 32

            for q, piece in enumerate(unpack(gc[side, p], start)):
                at = BORDER + 128 * q
                acc[p, block, at : at + 128, :] += jnp.where(mine(128), present(near, 2 + side, piece), 0.0)
            for ud in range(2):
                base = BORDER + (TILE - 32) * ud
                for q, piece in enumerate(unpack(gd[2 * ud + side, p], start)):
                    at = base + 8 * q
                    piece = present(near, 4 + 2 * ud + side, piece)
                    acc[p, block, at : at + 8, :] += jnp.where(mine(8), piece, 0.0)
        for ud in range(2):
            base = BORDER + (TILE - 32) * ud
            for j in range(4):
                acc[p, j + 1, base : base + 32, :] += present(near, ud, gv[ud, p, j])
    stores = []
    inner = pl.ds(BORDER, TILE)
    for j in range(4):
        out = pl.ds(128 * j, 128)
        acc[:, j + 1, inner, :] = step * acc[:, j + 1, inner, :]
        stores.append(pltpu.make_async_copy(acc.at[:, j + 1, inner, :], corr_out.at[:, :, out], sems.at[4 + j]))
        stores[-1].start()
        loads[j].wait()
        est[:, j] = est[:, j] + acc[:, j + 1, inner, :]
        stores.append(pltpu.make_async_copy(est.at[:, j], est_out.at[:, :, out], sems.at[8 + j]))
        stores[-1].start()
    for store in stores:
        store.wait()


VM = pl.BlockSpec(memory_space=pltpu.VMEM)
SM = pl.BlockSpec(memory_space=pltpu.SMEM)
HBM = pl.BlockSpec(memory_space=pltpu.HBM)


def shape(*dims, dtype=f32):
    return jax.ShapeDtypeStruct(dims, dtype)


def params(limit_mib=14, **kw):
    return pltpu.CompilerParams(vmem_limit_bytes=limit_mib * 2**20, **kw)


def remote_params(which):
    return params(collective_id=which, has_side_effects=True)


def on_device(object_field, probe_field, amplitudes, positions, counts):
    pos = positions[0, 0]
    tabs = [jnp.asarray(t) for t in tables()]
    dma = pltpu.SemaphoreType.DMA
    tile = (2, BLOCKS, ROWS, 128)
    window = (2, PROBE, PROBE)
    measured = shape(PMAX, PROBE, PROBE)
    far = functools.partial(pltpu.with_memory_space_constraint, memory_space=pltpu.HBM)
    cur, early, order, amps = pl.pallas_call(
        halo_kernel,
        out_shape=(shape(*tile), shape(EARLY, *window), shape(EARLY, dtype=jnp.int32), measured),
        in_specs=[SM, SM, HBM, HBM, VM, VM, VM],
        out_specs=[VM, VM, SM, VM],
        scratch_shapes=[
            pltpu.VMEM((2, 2, 32, TILE), f32),
            pltpu.VMEM((2, 2, 128, 128), f32),
            pltpu.VMEM((4, 2, 8, 128), f32),
            pltpu.VMEM((2, 2, 128, 128), f32),
            pltpu.VMEM((4, 2, 8, 128), f32),
            pltpu.SMEM((PMAX + 1,), jnp.int32),
            dma((8,)),
            dma((8,)),
            dma((5,)),
        ],
        compiler_params=remote_params(0),
        name="halo",
    )(counts, pos, far(object_field), far(amplitudes), probe_field, *tabs)
    shared = (amps, probe_field, *tabs)
    acc, after = pl.pallas_call(
        first_kernel,
        out_shape=(shape(*tile), shape(*tile)),
        in_specs=[SM, SM, SM] + [VM] * 6,
        out_specs=[VM] * 2,
        scratch_shapes=[pltpu.SMEM((PMAX,), jnp.int32)],
        compiler_params=params(),
        name="first",
    )(counts, pos, order, cur, early, *shared)
    strips = ((2, 2, 4, 64, 128), (2, 2, 32, 128), (2, 2, 2, 32, 128), (2, 2, 224, 128))
    grads, *got = pl.pallas_call(
        strip_kernel,
        out_shape=(shape(PMAX, *window),) + tuple(shape(*s) for s in strips),
        in_specs=[SM] + [VM] * 6,
        out_specs=[VM] * 5,
        scratch_shapes=[
            pltpu.VMEM((2, 2, 2, 64, 128), f32),
            pltpu.VMEM((2, 2, 32, 128), f32),
            pltpu.VMEM((2, 2, 2, 32, 128), f32),
            pltpu.VMEM((2, 2, 224, 128), f32),
            dma((12,)),
            dma((12,)),
        ],
        compiler_params=remote_params(1),
        name="strips",
    )(pos, acc, after, *shared)
    acc, cur, late = pl.pallas_call(
        second_kernel,
        out_shape=(shape(*tile), shape(*tile), shape(LATE, dtype=jnp.int32)),
        in_specs=[SM, SM] + [VM] * 11,
        out_specs=[VM, VM, SM],
        scratch_shapes=[pltpu.SMEM((PMAX,), jnp.int32)],
        compiler_params=params(),
        name="second",
    )(counts, pos, acc, after, *got, grads, *shared)
    folds = ((2, 2, 4, 32, 128), (2, 2, 128, 128), (4, 2, 8, 128))
    grads, *got = pl.pallas_call(
        fold_kernel,
        out_shape=(shape(LATE, *window),) + tuple(shape(*s) for s in folds),
        in_specs=[SM, SM] + [VM] * 6,
        out_specs=[VM] * 4,
        scratch_shapes=[
            pltpu.VMEM((2, 2, 128, 128), f32),
            pltpu.VMEM((4, 2, 8, 128), f32),
            dma((8,)),
            dma((8,)),
        ],
        compiler_params=remote_params(2),
        name="folds",
    )(pos, late, acc, cur, *shared)
    return pl.pallas_call(
        last_kernel,
        out_shape=(shape(2, TILE, TILE), shape(2, TILE, TILE)),
        in_specs=[SM, SM, HBM] + [VM] * 6,
        out_specs=[HBM] * 2,
        scratch_shapes=[pltpu.VMEM((2, 4, TILE, 128), f32), pltpu.VMEM(tile, f32), dma((12,))],
        compiler_params=params(),
        name="last",
    )(pos, late, far(object_field), acc, *got, grads, probe_field)


def solution(mesh):
    placed = (
        P(None, "row", "col"),
        P(),
        P("row", None, "col"),
        P("row", "col", None, None),
        P("row", "col"),
    )
    return jax.shard_map(
        on_device,
        mesh=mesh,
        in_specs=placed,
        out_specs=(P(None, "row", "col"), P(None, "row", "col")),
        check_vma=False,
    )
```

time: 81.7 us -> 66.9 us (0.82)
  Pallas kernels: 75.1 us -> 61.7 us
  local copies, waits for them, and re-layouts: 4.6 us -> 3.48 us
    pallas_call x5, Pallas kernels: 72.1 us -> 57.5 us  [the longest x1 19.8 us: on_device(): pl.pallas_call(strip_kernel, out_shape=(shape(PMAX, *window),) + tuple((s...]
    pallas_call x1, Pallas kernels: 2.96 us -> 4.13 us  [on_device(): pl.pallas_call(last_kernel, out_shape=(shape(2, TILE, TILE), shape(2, TIL...]
    unnamed x22 -> x8, local copies, waits for them, and re-layouts: 4.6 us -> 3.48 us
where the time goes in v2:
time: 66.9 us; the launch traced here: 66.6 us
  Pallas kernels  61.7 us (92%)
  local copies, waits for them, and re-layouts  3.48 us (5%)
  between operations  1.48 us (2%)
    pallas_call x1, Pallas kernels, on_device(): pl.pallas_call(strip_kernel, out_shape=(shape(PMAX, *window),) + tuple((s...  19.8 us
    pallas_call x1, Pallas kernels, on_device(): pl.pallas_call(halo_kernel, out_shape=(shape(*tile), shape(EARLY, *window...  13.6 us
    pallas_call x1, Pallas kernels, on_device(): pl.pallas_call(fold_kernel, out_shape=(shape(LATE, *window),) + tuple((sh...  11.6 us
    pallas_call x1, Pallas kernels, on_device(): pl.pallas_call(first_kernel, out_shape=(shape(*tile), shape(*tile)), in_s...  6.43 us
    pallas_call x1, Pallas kernels, on_device(): pl.pallas_call(second_kernel, out_shape=(shape(*tile), shape(*tile), shap...  6.11 us
    pallas_call x1, Pallas kernels, on_device(): pl.pallas_call(last_kernel, out_shape=(shape(2, TILE, TILE), shape(2, TIL...  4.13 us
    unnamed x8, local copies, waits for them, and re-layouts  3.48 us

profile of v2, /device:TPU:8, one launch (start us, length us, event | category | flops | bytes accessed | tf_op | source)
XLA Modules:
  0.0 66.6 jit_solution(1277888439785501141)
XLA Ops:
  1.3 0.0 copy-start
  1.3 0.9 %copy-done = bf16[2,256,256]{2,1,0:T(8,128)(2,1)S(1)} copy-done((bf16[2,256,256]{2,1,0:T(8,128)(2,1)S(1)}, bf16[2,256,256]{2,1,0:T(8,128)(2,1)}, u32[]{:S(2)}) %copy-start) | copy-done | bytes 262168
  2.2 0.0 copy-start.1
  2.2 0.9 %copy-done.1 = bf16[2,256,256]{2,1,0:T(8,128)(2,1)S(1)} copy-done((bf16[2,256,256]{2,1,0:T(8,128)(2,1)S(1)}, bf16[2,256,256]{2,1,0:T(8,128)(2,1)}, u32[]{:S(2)}) %copy-start.1) | copy-done | bytes 262168
  3.2 0.0 copy-start.2
  3.2 0.9 %copy-done.2 = f32[2,128,128]{2,1,0:T(8,128)S(1)} copy-done((f32[2,128,128]{2,1,0:T(8,128)S(1)}, f32[2,128,128]{2,1,0:T(8,128)}, u32[]{:S(2)}) %copy-start.2) | copy-done | bytes 131096
  4.1 0.0 copy-start.3
  4.1 0.7 %copy-done.3 = s32[1,1,2,24]{3,2,1,0:T(2,128)S(1)} copy-done((s32[1,1,2,24]{3,2,1,0:T(2,128)S(1)}, s32[1,1,2,24]{3,2,1,0:T(2,128)}, u32[]{:S(2)}) %copy-start.3) | copy-done | bytes 216
  4.8 13.6 %halo.1 = (f32[2,6,576,128]{3,2,1,0:T(8,128)S(1)}, f32[16,2,128,128]{3,2,1,0:T(8,128)S(1)}, s32[16]{0:T(128)S(1)}, f32[24,128,128]{2,1,0:T(8,128)S(1)}) custom-call(s32[1,1]{1,0:T(1,128)S(6)} %copy.9.count, s32[2,24]{1,0:T(2,128)S(1)} %bitcast.1, f32[2,512,512]{2,1,0:T(8,128)} %obj.3, f32[24,128,128]{2,1,0:T(8,128)} %amps_hbm.1, ...), custom_call_target="tpu_custom_call" | custom-call | tf_op jit(solution)/shard_map/halo/pallas_call | solution.py:577
  18.4 6.4 %first.1 = (f32[2,6,576,128]{3,2,1,0:T(8,128)S(1)}, f32[2,6,576,128]{3,2,1,0:T(8,128)S(1)}) custom-call(s32[1,1]{1,0:T(1,128)S(6)} %copy.9.count, s32[2,24]{1,0:T(2,128)S(1)} %bitcast.2, s32[16]{0:T(128)S(1)} %get-tuple-element.20.order, f32[2,6,576,128]{3,2,1,0:T(8,128)S(1)} %get-tuple-element.21.cur, f32[16,2,128,128]{3,2,1,0:T(8,128)S(1)} %get-tuple-element.22.early, ...), custom_call_target="tpu_custom_call" | custom-call | tf_op jit(solution)/shard_map/first/pallas_call | solution.py:597
  24.8 19.8 %strips.1 = (f32[24,2,128,128]{3,2,1,0:T(8,128)S(1)}, f32[2,2,4,64,128]{4,3,2,1,0:T(8,128)S(1)}, f32[2,2,32,128]{3,2,1,0:T(8,128)S(1)}, f32[2,2,2,32,128]{4,3,2,1,0:T(8,128)S(1)}, f32[2,2,224,128]{3,2,1,0:T(8,128)S(1)}) custom-call(s32[2,24]{1,0:T(2,128)S(1)} %bitcast.3, f32[2,6,576,128]{3,2,1,0:T(8,128)S(1)} %get-tuple-element.24.acc.acc_in, ...), custom_call_target="tpu_custom_call" | custom-call | tf_op jit(solution)/shard_map/strips/pallas_call | solution.py:607
  44.6 6.1 %second.1 = (f32[2,6,576,128]{3,2,1,0:T(8,128)S(1)}, f32[2,6,576,128]{3,2,1,0:T(8,128)S(1)}, s32[8]{0:T(128)S(1)}) custom-call(s32[1,1]{1,0:T(1,128)S(6)} %copy.9.count, s32[2,24]{1,0:T(2,128)S(1)} %bitcast.4, f32[2,6,576,128]{3,2,1,0:T(8,128)S(1)} %get-tuple-element.24.acc.acc_in, f32[2,6,576,128]{3,2,1,0:T(8,128)S(1)} %get-tuple-element.25.cur.cur_in, ...), custom_call_target="tpu_custom_call" | custom-call | tf_op jit(solution)/shard_map/second/pallas_call | solution.py:623
  50.8 11.6 %folds.1 = (f32[8,2,128,128]{3,2,1,0:T(8,128)S(1)}, f32[2,2,4,32,128]{4,3,2,1,0:T(8,128)S(1)}, f32[2,2,128,128]{3,2,1,0:T(8,128)S(1)}, f32[4,2,8,128]{3,2,1,0:T(8,128)S(1)}) custom-call(s32[2,24]{1,0:T(2,128)S(1)} %bitcast.5, s32[8]{0:T(128)S(1)} %get-tuple-element.31.late, f32[2,6,576,128]{3,2,1,0:T(8,128)S(1)} %get-tuple-element.32.acc.acc_in, ...), custom_call_target="tpu_custom_call" | custom-call | tf_op jit(solution)/shard_map/folds/pallas_call | solution.py:633
  62.3 4.1 %last.1 = (f32[2,512,512]{2,1,0:T(8,128)}, f32[2,512,512]{2,1,0:T(8,128)}) custom-call(s32[2,24]{1,0:T(2,128)S(1)} %bitcast.6, s32[8]{0:T(128)S(1)} %get-tuple-element.31.late, f32[2,512,512]{2,1,0:T(8,128)} %obj.3, f32[2,6,576,128]{3,2,1,0:T(8,128)S(1)} %get-tuple-element.32.acc.acc_in, f32[2,2,4,32,128]{4,3,2,1,0:T(8,128)S(1)} %get-tuple-element.34.gv, ...), custom_call_target="tpu_custom_call" | custom-call | tf_op jit(solution)/shard_map/last/pallas_call | solution.py:647
Async XLA Ops:
  1.3 1.0 %copy-start = (bf16[2,256,256]{2,1,0:T(8,128)(2,1)S(1)}, bf16[2,256,256]{2,1,0:T(8,128)(2,1)}, u32[]{:S(2)}) copy-start(bf16[2,256,256]{2,1,0:T(8,128)(2,1)} %constant.5.clone.t1) | copy-start | bytes 786436
  2.2 0.9 %copy-start.1 = (bf16[2,256,256]{2,1,0:T(8,128)(2,1)S(1)}, bf16[2,256,256]{2,1,0:T(8,128)(2,1)}, u32[]{:S(2)}) copy-start(bf16[2,256,256]{2,1,0:T(8,128)(2,1)} %constant.4.clone.t0) | copy-start | bytes 786436
  3.2 0.9 %copy-start.2 = (f32[2,128,128]{2,1,0:T(8,128)S(1)}, f32[2,128,128]{2,1,0:T(8,128)}, u32[]{:S(2)}) copy-start(f32[2,128,128]{2,1,0:T(8,128)} %probe.11) | copy-start | bytes 393220
  4.1 0.7 %copy-start.3 = (s32[1,1,2,24]{3,2,1,0:T(2,128)S(1)}, s32[1,1,2,24]{3,2,1,0:T(2,128)}, u32[]{:S(2)}) copy-start(s32[1,1,2,24]{3,2,1,0:T(2,128)} %param.10) | copy-start | bytes 580

commit v3 on v2

--- a/solution.py
+++ b/solution.py
@@ -109,27 +109,40 @@
 
 
 def corner_of(pos, s):
-    return pos[0, s] + BORDER, pos[1, s] + 128
-
-
-def inside(pos, s, low, high):
-    r, c = pos[0, s], pos[1, s]
-    return jnp.logical_and(
-        jnp.logical_and(r >= low, r <= high), jnp.logical_and(c >= low, c <= high)
-    )
+    return pos[0, 0, 0, s] + BORDER, pos[0, 0, 1, s] + 128
+
+
+def within(start, margin):
+    return jnp.logical_and(start >= margin, start <= TILE - PROBE - margin)
+
+
+def rows_within(pos, s, margin):
+    return within(pos[0, 0, 0, s], margin)
+
+
+def columns_within(pos, s, margin):
+    return within(pos[0, 0, 1, s], margin)
 
 
 def listed_slots(amount, todo, pos, cur, acc, amps, probe, tabs):
-    def body(i, carry):
-        at = [i * GROUP + k for k in range(GROUP)]
+    def some(start, size):
+        at = [start + k for k in range(size)]
         slots = [jnp.where(j < amount, todo[j], 0) for j in at]
         scale = [jnp.where(j < amount, 1.0, 0.0) for j in at]
         grads = gradients(cur, amps, probe, tabs, pos, slots, scale)
         for grad, s in zip(grads, slots):
             place(acc, grad, *corner_of(pos, s))
+
+    def body(i, carry):
+        some(i * GROUP, GROUP)
         return carry
 
-    lax.fori_loop(0, lax.div(amount + GROUP - 1, GROUP), body, 0)
+    full = lax.div(amount + GROUP // 2 - 1, GROUP)
+    lax.fori_loop(0, full, body, 0)
+
+    @pl.when(amount > full * GROUP)
+    def _():
+        some(full * GROUP, GROUP // 2)
 
 
 def step_of(probe):
@@ -152,13 +165,17 @@
 
 def greet(near):
     barrier = pltpu.get_barrier_semaphore()
-    total = 0
     for there, where in near:
         @pl.when(there)
         def _():
             pl.semaphore_signal(barrier, inc=1, device_id=where, device_id_type=MESH)
+
+
+def greeted(near):
+    total = 0
+    for there, _ in near:
         total = total + there.astype(jnp.int32)
-    pl.semaphore_wait(barrier, total)
+    pl.semaphore_wait(pltpu.get_barrier_semaphore(), total)
 
 
 def remote(k, near, source, target, send, recv, n):
@@ -229,25 +246,43 @@
     return jnp.where(near[k][0], value, 0.0)
 
 
-EARLY = 16
 LATE = 8
 
 
+def keep_gradients(grads, cur, amps, probe, tabs, pos):
+    def body(i, carry):
+        slots = [i * GROUP + k for k in range(GROUP)]
+        for s, (a, b) in zip(slots, gradients(cur, amps, probe, tabs, pos, slots)):
+            grads[s, 0] = a
+            grads[s, 1] = b
+        return carry
+
+    return body
+
+
 def halo_kernel(
-    count, pos, obj, amps_hbm, probe, t0, t1, cur, early, order, amps, hv, hc, hd, sc, sd, follow, send, recv, sems
+    pos, obj, amps_far, probe_far, t0_far, t1_far, cur, grads, amps, probe, t0, t1, hv, hc, hd, sc, sd, send, recv, sems
 ):
     near = neighbours()
+    greet(near)
     tile_at = [
         pltpu.make_async_copy(
             obj.at[:, :, pl.ds(128 * j, 128)], cur.at[:, j + 1, pl.ds(BORDER, TILE), :], sems.at[j]
         )
         for j in range(4)
     ]
-    for j in (0, 3, 1, 2):
-        tile_at[j].start()
-    measured = pltpu.make_async_copy(amps_hbm, amps, sems.at[4])
-    measured.start()
-    greet(near)
+    others = [
+        pltpu.make_async_copy(there, here, sems.at[4 + n])
+        for n, (there, here) in enumerate(((probe_far, probe), (t0_far, t0), (t1_far, t1), (amps_far, amps)))
+    ]
+    for copy in [tile_at[j] for j in (0, 3, 1, 2)] + others:
+        copy.start()
+    zeros = jnp.zeros((2, BLOCKS, BORDER, 128), f32)
+    cur[:, :, 0:BORDER, :] = zeros
+    cur[:, :, BORDER + TILE :, :] = zeros
+    cur[:, 0] = jnp.zeros((2, ROWS, 128), f32)
+    cur[:, 5] = jnp.zeros((2, ROWS, 128), f32)
+    greeted(near)
     post = Post(near, send, recv)
     waits = [post.pair(0, [obj.at[:, pl.ds(0, 32), :], obj.at[:, pl.ds(TILE - 32, 32), :]], [hv.at[0], hv.at[1]])]
     for side in range(2):
@@ -262,36 +297,20 @@
                 sd[2 * ud + side, p] = pack(
                     [cur[p, block, base + 8 * q : base + 8 * q + 8, :] for q in range(4)], start
                 )
+    sideways = post.pair(2, [sc.at[0], sc.at[1]], [hc.at[0], hc.at[1]])
     waits.append(post.pair(4, [sd.at[0], sd.at[3]], [hd.at[0], hd.at[3]]))
     waits.append(post.pair(5, [sd.at[1], sd.at[2]], [hd.at[1], hd.at[2]]))
-    waits.append(post.pair(2, [sc.at[0], sc.at[1]], [hc.at[0], hc.at[1]]))
-    coming = jnp.int32(PMAX)
-    follow[PMAX] = coming
-    for s in range(PMAX - 1, -1, -1):
-        keep = jnp.logical_and(s < count[0, 0], inside(pos, s, 0, TILE - PROBE))
-        coming = jnp.where(keep, s, coming)
-        follow[s] = coming
-    coming = follow[0]
-    for k in range(EARLY):
-        order[k] = coming
-        coming = follow[jnp.minimum(coming + 1, PMAX)]
-    zeros = jnp.zeros((2, BLOCKS, BORDER, 128), f32)
-    cur[:, :, 0:BORDER, :] = zeros
-    cur[:, :, BORDER + TILE :, :] = zeros
-    cur[:, 0] = jnp.zeros((2, ROWS, 128), f32)
-    cur[:, 5] = jnp.zeros((2, ROWS, 128), f32)
-    tile_at[1].wait()
-    tile_at[2].wait()
-    measured.wait()
-
-    def body(i, carry):
-        slots = [jnp.minimum(order[i * GROUP + k], PMAX - 1) for k in range(GROUP)]
-        for k, (a, b) in enumerate(gradients(cur, amps, probe, (t0, t1), pos, slots)):
-            early[i * GROUP + k, 0] = a
-            early[i * GROUP + k, 1] = b
-        return carry
-
-    lax.fori_loop(0, EARLY // GROUP, body, 0)
+    for copy in [tile_at[1], tile_at[2]] + others:
+        copy.wait()
+    body = keep_gradients(grads, cur, amps, probe, (t0, t1), pos)
+    lax.fori_loop(0, 1, body, 0)
+    sideways()
+    for p in range(2):
+        for side in range(2):
+            for q, piece in enumerate(unpack(hc[side, p], 96 - 96 * side)):
+                at = BORDER + 128 * q
+                cur[p, 5 * side, at : at + 128, :] = present(near, 2 + side, piece)
+    lax.fori_loop(1, PMAX // GROUP, body, 0)
     for wait in waits:
         wait()
     for p in range(2):
@@ -302,46 +321,53 @@
             for side in range(2):
                 for q, piece in enumerate(unpack(hd[2 * k + side, p], 96 - 96 * side)):
                     cur[p, 5 * side, base + 8 * q : base + 8 * q + 8, :] = present(near, 4 + 2 * k + side, piece)
-        for side in range(2):
-            for q, piece in enumerate(unpack(hc[side, p], 96 - 96 * side)):
-                at = BORDER + 128 * q
-                cur[p, 5 * side, at : at + 128, :] = present(near, 2 + side, piece)
-
-
-def first_kernel(count, pos, order, cur, early, amps, probe, t0, t1, acc, after, todo):
-    live = count[0, 0]
+
+
+def first_kernel(count, pos, cur, grads, amps, probe, t0, t1, acc, after, todo):
     acc[...] = jnp.zeros_like(acc)
 
-    def sort(s, carry):
-        amount, kept = carry
-        keep = inside(pos, s, 0, TILE - PROBE)
-        done = jnp.logical_and(keep, kept < EARLY)
+    def sort(s, amount):
+        done = jnp.logical_and(
+            rows_within(pos, s, 0), jnp.logical_or(s >= GROUP, columns_within(pos, s, 0))
+        )
+
+        @pl.when(done)
+        def _():
+            place(acc, (grads[s, 0], grads[s, 1]), *corner_of(pos, s))
 
         @pl.when(jnp.logical_not(done))
         def _():
             todo[amount] = s
 
-        return amount + jnp.where(done, 0, 1), kept + jnp.where(keep, 1, 0)
-
-    amount, kept = lax.fori_loop(0, live, sort, (jnp.int32(0), jnp.int32(0)))
-
-    def put(k, carry):
-        place(acc, (early[k, 0], early[k, 1]), *corner_of(pos, order[k]))
-        return carry
-
-    lax.fori_loop(0, jnp.minimum(kept, EARLY), put, 0)
+        return amount + jnp.where(done, 0, 1)
+
+    amount = lax.fori_loop(0, count[0, 0], sort, jnp.int32(0))
     listed_slots(amount, todo, pos, cur, acc, amps, probe, (t0, t1))
     after[...] = cur[...] + step_of(probe) * acc[...]
 
 
-def strip_kernel(pos, acc, cur, amps, probe, t0, t1, grads, rv, rs, rc, rm, sv, ss, sc, sm, send, recv):
+def side_sums(near, rc, rm, side, p):
+    for rows, value in (
+        (pl.ds(0, 64), rc[side, 0, p]),
+        (pl.ds(64, TILE - 64), rm[side, p]),
+        (pl.ds(TILE, 64), rc[side, 1, p]),
+    ):
+        yield rows, present(near, 2 + side, unpack_two(value))
+
+
+def strip_kernel(
+    pos, acc, cur_in, amps, probe, t0, t1, grads, cur, rv, rs, rc, rm, sv, ss, sc, sm, send, recv, sems
+):
     near = neighbours()
+    greet(near)
+    same = pltpu.make_async_copy(cur_in, cur, sems.at[0])
+    same.start()
     for p in range(2):
         for side in range(2):
             for ud in range(2):
                 rows = pl.ds(TILE * ud, 64)
                 sc[side, ud, p] = pack_two(seam(acc[p, 4 * side, rows, :], acc[p, 4 * side + 1, rows, :]))
-    greet(near)
+    greeted(near)
     post = Post(near, send, recv)
     corners = post.pair(2, [sc.at[0], sc.at[1]], [rc.at[0], rc.at[1]])
     waits = [
@@ -354,16 +380,7 @@
     for p in range(2):
         for side in range(2):
             sm[side, p] = pack_two(seam(acc[p, 4 * side, 64:TILE, :], acc[p, 4 * side + 1, 64:TILE, :]))
-    waits.append(post.pair(2, [sm.at[0], sm.at[1]], [rm.at[0], rm.at[1]]))
-
-    def body(i, carry):
-        slots = [i * GROUP + k for k in range(GROUP)]
-        for s, (a, b) in zip(slots, gradients(cur, amps, probe, (t0, t1), pos, slots)):
-            grads[s, 0] = a
-            grads[s, 1] = b
-        return carry
-
-    lax.fori_loop(0, 1, body, 0)
+    middle = post.pair(2, [sm.at[0], sm.at[1]], [rm.at[0], rm.at[1]])
     corners()
     lane = lanes(64)
     for p in range(2):
@@ -379,7 +396,18 @@
             post.pair(0, [sv.at[ud, :, n] for ud in range(2)], [rv.at[ud, :, block] for ud in range(2)])
         )
     waits.append(post.pair(0, [ss.at[0], ss.at[1]], [rs.at[0], rs.at[1]]))
-    lax.fori_loop(1, PMAX // GROUP, body, 0)
+    same.wait()
+    middle()
+    step = step_of(probe)
+    for p in range(2):
+        for side in range(2):
+            for rows, value in side_sums(near, rc, rm, side, p):
+                lane = lanes(value.shape[0])
+                cur[p, 4 * side, rows, :] += step * jnp.where(lane >= 96, value, 0.0)
+                cur[p, 4 * side + 1, rows, :] += step * jnp.where(lane < 32, value, 0.0)
+    for side in range(2):
+        cur[:, 5 * side] = present(near, 2 + side, cur[:, 5 * side])
+    lax.fori_loop(0, PMAX // GROUP, keep_gradients(grads, cur, amps, probe, (t0, t1), pos), 0)
     for wait in waits:
         wait()
 
@@ -389,9 +417,7 @@
 ):
     near = neighbours()
     step = step_of(probe)
-    live = count[0, 0]
-    acc[...] = acc_in[...]
-    cur[...] = cur_in[...]
+    del acc_in, cur_in
 
     def add(p, block, rows, value):
         acc[p, block, rows, :] += value
@@ -407,19 +433,17 @@
             add(p, 0, rows, jnp.where(lane >= 96, sides, 0.0))
             add(p, 5, rows, jnp.where(lane < 32, sides, 0.0))
         for side in range(2):
-            for rows, piece in (
-                (pl.ds(0, 64), rc[side, 0, p]),
-                (pl.ds(64, TILE - 64), rm[side, p]),
-                (pl.ds(TILE, 64), rc[side, 1, p]),
-            ):
-                piece = present(near, 2 + side, unpack_two(piece))
-                lane = lanes(piece.shape[0])
-                add(p, 4 * side, rows, jnp.where(lane >= 96, piece, 0.0))
-                add(p, 4 * side + 1, rows, jnp.where(lane < 32, piece, 0.0))
+            block = 1 + 3 * side
+            for rows, value in side_sums(near, rc, rm, side, p):
+                lane = lanes(value.shape[0])
+                acc[p, block, rows, :] += jnp.where(lane >= 96 if side else lane < 32, value, 0.0)
     for k in range(2):
         rows = pl.ds((BORDER + TILE) * k, BORDER)
         cur[:, :, rows, :] = present(near, k, cur[:, :, rows, :])
-        cur[:, 5 * k] = present(near, 2 + k, cur[:, 5 * k])
+        for p in range(2):
+            for r in range(2):
+                at = pl.ds((BORDER + TILE) * r, BORDER)
+                cur[p, 5 * k, at, :] = present(near, 2 + k, cur[p, 5 * k, at, :])
         acc[:, :, rows, :] = jnp.zeros((2, BLOCKS, BORDER, 128), f32)
         acc[:, 5 * k] = jnp.zeros((2, ROWS, 128), f32)
     for k in range(LATE):
@@ -427,10 +451,9 @@
 
     def sort(s, carry):
         amount, held = carry
-        done = inside(pos, s, BORDER, TILE - PROBE - BORDER)
-        hold = jnp.logical_and(
-            jnp.logical_and(inside(pos, s, 0, TILE - PROBE), held < LATE), jnp.logical_not(done)
-        )
+        done = rows_within(pos, s, BORDER)
+        inner = jnp.logical_and(rows_within(pos, s, 0), columns_within(pos, s, 0))
+        hold = jnp.logical_and(jnp.logical_and(inner, held < LATE), jnp.logical_not(done))
 
         @pl.when(done)
         def _():
@@ -448,12 +471,13 @@
 
         return amount + jnp.where(now, 1, 0), held + jnp.where(hold, 1, 0)
 
-    amount, _ = lax.fori_loop(0, live, sort, (jnp.int32(0), jnp.int32(0)))
+    amount, _ = lax.fori_loop(0, count[0, 0], sort, (jnp.int32(0), jnp.int32(0)))
     listed_slots(amount, todo, pos, cur, acc, amps, probe, (t0, t1))
 
 
 def fold_kernel(pos, late, acc, cur, amps, probe, t0, t1, grads, gv, gc, gd, sc, sd, send, recv):
     near = neighbours()
+    greet(near)
     for p in range(2):
         for side in range(2):
             start = 96 - 96 * side
@@ -462,7 +486,7 @@
                 sd[2 * ud + side, p] = pack(
                     [acc[p, 5 * side, base + 8 * q : base + 8 * q + 8, :] for q in range(4)], start
                 )
-    greet(near)
+    greeted(near)
     post = Post(near, send, recv)
     waits = [
         post.pair(
@@ -492,17 +516,10 @@
         wait()
 
 
-def last_kernel(
-    pos, late, obj, acc_in, gv, gc, gd, grads, probe, est_out, corr_out, est, acc, sems
-):
+def last_kernel(pos, late, obj, acc_in, gv, gc, gd, grads, probe, est_out, corr_out, acc, est, sems):
     near = neighbours()
-    loads = [
-        pltpu.make_async_copy(obj.at[:, :, pl.ds(128 * j, 128)], est.at[:, j], sems.at[j]) for j in range(4)
-    ]
-    for load in loads:
-        load.start()
+    del acc_in
     step = step_of(probe)
-    acc[...] = acc_in[...]
 
     def put(k, carry):
         s = late[k]
@@ -539,11 +556,10 @@
     for j in range(4):
         out = pl.ds(128 * j, 128)
         acc[:, j + 1, inner, :] = step * acc[:, j + 1, inner, :]
-        stores.append(pltpu.make_async_copy(acc.at[:, j + 1, inner, :], corr_out.at[:, :, out], sems.at[4 + j]))
+        stores.append(pltpu.make_async_copy(acc.at[:, j + 1, inner, :], corr_out.at[:, :, out], sems.at[j]))
         stores[-1].start()
-        loads[j].wait()
-        est[:, j] = est[:, j] + acc[:, j + 1, inner, :]
-        stores.append(pltpu.make_async_copy(est.at[:, j], est_out.at[:, :, out], sems.at[8 + j]))
+        est[:, j] = obj[:, :, 128 * j : 128 * j + 128] + acc[:, j + 1, inner, :]
+        stores.append(pltpu.make_async_copy(est.at[:, j], est_out.at[:, :, out], sems.at[4 + j]))
         stores[-1].start()
     for store in stores:
         store.wait()
@@ -567,48 +583,47 @@
 
 
 def on_device(object_field, probe_field, amplitudes, positions, counts):
-    pos = positions[0, 0]
     tabs = [jnp.asarray(t) for t in tables()]
     dma = pltpu.SemaphoreType.DMA
-    tile = (2, BLOCKS, ROWS, 128)
-    window = (2, PROBE, PROBE)
-    measured = shape(PMAX, PROBE, PROBE)
-    far = functools.partial(pltpu.with_memory_space_constraint, memory_space=pltpu.HBM)
-    cur, early, order, amps = pl.pallas_call(
+    tile = shape(2, BLOCKS, ROWS, 128)
+    kept = shape(PMAX, 2, PROBE, PROBE)
+    far = [
+        pltpu.with_memory_space_constraint(x, pltpu.HBM)
+        for x in (object_field, amplitudes, probe_field, *tabs)
+    ]
+    cur, grads, *shared = pl.pallas_call(
         halo_kernel,
-        out_shape=(shape(*tile), shape(EARLY, *window), shape(EARLY, dtype=jnp.int32), measured),
-        in_specs=[SM, SM, HBM, HBM, VM, VM, VM],
-        out_specs=[VM, VM, SM, VM],
+        out_shape=[tile, kept] + [jax.ShapeDtypeStruct(x.shape, x.dtype) for x in (amplitudes, probe_field, *tabs)],
+        in_specs=[SM] + [HBM] * 5,
+        out_specs=[VM] * 6,
         scratch_shapes=[
             pltpu.VMEM((2, 2, 32, TILE), f32),
             pltpu.VMEM((2, 2, 128, 128), f32),
             pltpu.VMEM((4, 2, 8, 128), f32),
             pltpu.VMEM((2, 2, 128, 128), f32),
             pltpu.VMEM((4, 2, 8, 128), f32),
-            pltpu.SMEM((PMAX + 1,), jnp.int32),
             dma((8,)),
             dma((8,)),
-            dma((5,)),
+            dma((8,)),
         ],
         compiler_params=remote_params(0),
         name="halo",
-    )(counts, pos, far(object_field), far(amplitudes), probe_field, *tabs)
-    shared = (amps, probe_field, *tabs)
+    )(positions, *far)
     acc, after = pl.pallas_call(
         first_kernel,
-        out_shape=(shape(*tile), shape(*tile)),
-        in_specs=[SM, SM, SM] + [VM] * 6,
+        out_shape=(tile, tile),
+        in_specs=[SM, SM] + [VM] * 6,
         out_specs=[VM] * 2,
         scratch_shapes=[pltpu.SMEM((PMAX,), jnp.int32)],
         compiler_params=params(),
         name="first",
-    )(counts, pos, order, cur, early, *shared)
+    )(counts, positions, cur, grads, *shared)
     strips = ((2, 2, 4, 64, 128), (2, 2, 32, 128), (2, 2, 2, 32, 128), (2, 2, 224, 128))
-    grads, *got = pl.pallas_call(
+    grads, cur, *got = pl.pallas_call(
         strip_kernel,
-        out_shape=(shape(PMAX, *window),) + tuple(shape(*s) for s in strips),
+        out_shape=(kept, tile) + tuple(shape(*s) for s in strips),
         in_specs=[SM] + [VM] * 6,
-        out_specs=[VM] * 5,
+        out_specs=[VM] * 6,
         scratch_shapes=[
             pltpu.VMEM((2, 2, 2, 64, 128), f32),
             pltpu.VMEM((2, 2, 32, 128), f32),
@@ -616,23 +631,25 @@
             pltpu.VMEM((2, 2, 224, 128), f32),
             dma((12,)),
             dma((12,)),
+            dma((1,)),
         ],
         compiler_params=remote_params(1),
         name="strips",
-    )(pos, acc, after, *shared)
+    )(positions, acc, after, *shared)
     acc, cur, late = pl.pallas_call(
         second_kernel,
-        out_shape=(shape(*tile), shape(*tile), shape(LATE, dtype=jnp.int32)),
+        out_shape=(tile, tile, shape(LATE, dtype=jnp.int32)),
         in_specs=[SM, SM] + [VM] * 11,
         out_specs=[VM, VM, SM],
         scratch_shapes=[pltpu.SMEM((PMAX,), jnp.int32)],
+        input_output_aliases={2: 0, 3: 1},
         compiler_params=params(),
         name="second",
-    )(counts, pos, acc, after, *got, grads, *shared)
+    )(counts, positions, acc, cur, *got, grads, *shared)
     folds = ((2, 2, 4, 32, 128), (2, 2, 128, 128), (4, 2, 8, 128))
     grads, *got = pl.pallas_call(
         fold_kernel,
-        out_shape=(shape(LATE, *window),) + tuple(shape(*s) for s in folds),
+        out_shape=(shape(LATE, 2, PROBE, PROBE),) + tuple(shape(*s) for s in folds),
         in_specs=[SM, SM] + [VM] * 6,
         out_specs=[VM] * 4,
         scratch_shapes=[
@@ -643,16 +660,17 @@
         ],
         compiler_params=remote_params(2),
         name="folds",
-    )(pos, late, acc, cur, *shared)
+    )(positions, late, acc, cur, *shared)
     return pl.pallas_call(
         last_kernel,
-        out_shape=(shape(2, TILE, TILE), shape(2, TILE, TILE)),
-        in_specs=[SM, SM, HBM] + [VM] * 6,
-        out_specs=[HBM] * 2,
-        scratch_shapes=[pltpu.VMEM((2, 4, TILE, 128), f32), pltpu.VMEM(tile, f32), dma((12,))],
+        out_shape=(shape(2, TILE, TILE), shape(2, TILE, TILE), tile),
+        in_specs=[SM, SM] + [VM] * 7,
+        out_specs=[HBM, HBM, VM],
+        scratch_shapes=[pltpu.VMEM((2, 4, TILE, 128), f32), dma((8,))],
+        input_output_aliases={3: 2},
         compiler_params=params(),
         name="last",
-    )(pos, late, far(object_field), acc, *got, grads, probe_field)
+    )(positions, late, object_field, acc, *got, grads, shared[1])[:2]
 
 
 def solution(mesh):

time: 66.9 us -> 63.8 us (0.954)
  the two profiles are of different devices: /device:TPU:8 before, /device:TPU:15 now
where the time goes in v3:
time: 63.8 us; the launch traced here: 63.6 us
  Pallas kernels  61.5 us (96%)
  between operations  1.5 us (2%)
  local copies, waits for them, and re-layouts  0.68 us (1%)
    pallas_call x1, Pallas kernels, on_device(): pl.pallas_call(strip_kernel, out_shape=(kept, tile) + tuple((shape(*s) fo...  21.5 us
    pallas_call x1, Pallas kernels, on_device(): pl.pallas_call(halo_kernel, out_shape=[tile, kept] + [jax.ShapeDtypeStruc...  16.4 us
    pallas_call x1, Pallas kernels, on_device(): pl.pallas_call(fold_kernel, out_shape=(shape(LATE, 2, PROBE, PROBE),) + t...  9.39 us
    pallas_call x1, Pallas kernels, on_device(): pl.pallas_call(first_kernel, out_shape=(tile, tile), in_specs=[SM, SM] +...  5.43 us
    pallas_call x1, Pallas kernels, on_device(): pl.pallas_call(second_kernel, out_shape=(tile, tile, shape(LATE, dtype=jn...  5.27 us
    pallas_call x1, Pallas kernels, on_device(): pl.pallas_call(last_kernel, out_shape=(shape(2, TILE, TILE), shape(2, TIL...  3.4 us

profile of v3, /device:TPU:15, one launch (start us, length us, event | category | flops | bytes accessed | tf_op | source)
XLA Modules:
  0.0 63.6 jit_solution(17699768219908202972)
XLA Ops:
  1.3 0.0 copy-start.1
  1.3 0.7 %copy-done.1 = s32[1,1,2,24]{3,2,1,0:T(2,128)S(1)} copy-done((s32[1,1,2,24]{3,2,1,0:T(2,128)S(1)}, s32[1,1,2,24]{3,2,1,0:T(2,128)}, u32[]{:S(2)}) %copy-start.1) | copy-done | bytes 216
  2.0 16.4 %halo.1 = (f32[2,6,576,128]{3,2,1,0:T(8,128)S(1)}, f32[24,2,128,128]{3,2,1,0:T(8,128)S(1)}, f32[24,128,128]{2,1,0:T(8,128)S(1)}, f32[2,128,128]{2,1,0:T(8,128)S(...) custom-call(s32[1,1,2,24]{3,2,1,0:T(2,128)S(1)} %copy-done.1, f32[2,512,512]{2,1,0:T(8,128)} %obj.3, ...), custom_call_target="tpu_custom_call" | custom-call | tf_op jit(solution)/shard_map/halo/pallas_call | solution.py:594
  18.4 5.4 %first.1 = (f32[2,6,576,128]{3,2,1,0:T(8,128)S(1)}, f32[2,6,576,128]{3,2,1,0:T(8,128)S(1)}) custom-call(s32[1,1]{1,0:T(1,128)S(6)} %copy.15.count, s32[1,1,2,24]{3,2,1,0:T(2,128)S(1)} %copy-done.1, f32[2,6,576,128]{3,2,1,0:T(8,128)S(1)} %get-tuple-element.25.cur, f32[24,2,128,128]{3,2,1,0:T(8,128)S(1)} %get-tuple-element.26.grads, ...), custom_call_target="tpu_custom_call" | custom-call | tf_op jit(solution)/shard_map/first/pallas_call | solution.py:612
  23.8 21.5 %strips.1 = (f32[24,2,128,128]{3,2,1,0:T(8,128)S(1)}, f32[2,6,576,128]{3,2,1,0:T(8,128)S(1)}, f32[2,2,4,64,128]{4,3,2,1,0:T(8,128)S(1)}, f32[2,2,32,128]{3,2,1,0...) custom-call(s32[1,1,2,24]{3,2,1,0:T(2,128)S(1)} %copy-done.1, ...), custom_call_target="tpu_custom_call" | custom-call | tf_op jit(solution)/shard_map/strips/pallas_call | solution.py:622
  45.4 5.3 %second.1 = (f32[2,6,576,128]{3,2,1,0:T(8,128)S(1)}, f32[2,6,576,128]{3,2,1,0:T(8,128)S(1)}, s32[8]{0:T(128)S(1)}) custom-call(s32[1,1]{1,0:T(1,128)S(6)} %copy.15.count, s32[1,1,2,24]{3,2,1,0:T(2,128)S(1)} %copy-done.1, f32[2,6,576,128]{3,2,1,0:T(8,128)S(1)} %get-tuple-element.31.acc.acc_in, ...), custom_call_target="tpu_custom_call", output_to_operand_aliasing={{0}: (2, {}), {1}: (3, {})} | custom-call | tf_op jit(solution)/shard_map/second/pallas_call | solution.py:639
  50.6 0.0 copy-start
  50.7 9.4 %folds.1 = (f32[8,2,128,128]{3,2,1,0:T(8,128)S(1)}, f32[2,2,4,32,128]{4,3,2,1,0:T(8,128)S(1)}, f32[2,2,128,128]{3,2,1,0:T(8,128)S(1)}, f32[4,2,8,128]{3,2,1,0:T(8,128)S(1)}) custom-call(s32[1,1,2,24]{3,2,1,0:T(2,128)S(1)} %copy-done.1, s32[8]{0:T(128)S(1)} %get-tuple-element.39.late, f32[2,6,576,128]{3,2,1,0:T(8,128)S(1)} %get-tuple-element.40.acc.acc_in, ...), custom_call_target="tpu_custom_call" | custom-call | tf_op jit(solution)/shard_map/folds/pallas_call | solution.py:650
  60.1 0.0 copy-done
  60.1 3.4 %last.1 = (f32[2,512,512]{2,1,0:T(8,128)}, f32[2,512,512]{2,1,0:T(8,128)}, f32[2,6,576,128]{3,2,1,0:T(8,128)S(1)}) custom-call(s32[1,1,2,24]{3,2,1,0:T(2,128)S(1)} %copy-done.1, s32[8]{0:T(128)S(1)} %get-tuple-element.39.late, f32[2,512,512]{2,1,0:T(8,128)S(1)} %copy-done, ...), custom_call_target="tpu_custom_call", output_to_operand_aliasing={{2}: (3, {})} | custom-call | tf_op jit(solution)/shard_map/last/pallas_call | solution.py:664
Async XLA Ops:
  1.3 0.7 %copy-start.1 = (s32[1,1,2,24]{3,2,1,0:T(2,128)S(1)}, s32[1,1,2,24]{3,2,1,0:T(2,128)}, u32[]{:S(2)}) copy-start(s32[1,1,2,24]{3,2,1,0:T(2,128)} %pos.11) | copy-start | bytes 580
  50.6 9.4 %copy-start = (f32[2,512,512]{2,1,0:T(8,128)S(1)}, f32[2,512,512]{2,1,0:T(8,128)}, u32[]{:S(2)}) copy-start(f32[2,512,512]{2,1,0:T(8,128)} %obj.3) | copy-start | bytes 6291460

commit v4 on v3

--- a/solution.py
+++ b/solution.py
@@ -163,16 +163,34 @@
     return out
 
 
+def crossing():
+    cols, row, col = lax.axis_size("col"), lax.axis_index("row"), lax.axis_index("col")
+    middle = (cols // 2 - 1, cols // 2)
+    outer = (cols - 1, 0)
+    in_middle = jnp.logical_or(col == middle[0], col == middle[1])
+    in_outer = jnp.logical_or(col == outer[0], col == outer[1])
+    return row, col, middle, outer, in_middle, in_outer
+
+
 def greet(near):
     barrier = pltpu.get_barrier_semaphore()
-    for there, where in near:
+
+    def hail(there, where):
         @pl.when(there)
         def _():
             pl.semaphore_signal(barrier, inc=1, device_id=where, device_id_type=MESH)
 
+    for there, where in near:
+        hail(there, where)
+    row, _, middle, outer, in_middle, in_outer = crossing()
+    for k in range(2):
+        hail(in_middle, (row, outer[k]))
+        hail(in_outer, (row, middle[k]))
+
 
 def greeted(near):
-    total = 0
+    *_, in_middle, in_outer = crossing()
+    total = 2 * jnp.logical_or(in_middle, in_outer).astype(jnp.int32)
     for there, _ in near:
         total = total + there.astype(jnp.int32)
     pl.semaphore_wait(pltpu.get_barrier_semaphore(), total)
@@ -211,6 +229,72 @@
         self.count += 2
         return wait
 
+    def sideways(self, outs, intos, hop, hop_sem):
+        row, col, middle, outer, *_ = crossing()
+        n = self.count
+
+        def copy(source, target, i, sem, where):
+            return pltpu.make_async_remote_copy(
+                src_ref=source,
+                dst_ref=target,
+                send_sem=self.send.at[n + i],
+                recv_sem=sem,
+                device_id=(row, where),
+                device_id_type=MESH,
+            )
+
+        def direct(i):
+            there, (_, where) = self.near[2 + i]
+            cross = col == middle[1 - i]
+            return jnp.logical_and(there, jnp.logical_not(cross)), cross, where
+
+        for i in range(2):
+            there, cross, where = direct(i)
+
+            @pl.when(there)
+            def _(i=i, where=where):
+                copy(outs[i], intos[1 - i], i, self.recv.at[n + i], where).start()
+
+            @pl.when(cross)
+            def _(i=i):
+                copy(outs[i], hop, i, hop_sem, outer[1 - i]).start()
+
+        def forward():
+            for i in range(2):
+                @pl.when(col == outer[1 - i])
+                def _(i=i):
+                    copy(outs[i], hop, i, hop_sem, middle[i]).wait_recv()
+                    copy(hop, intos[1 - i], i, self.recv.at[n + i], middle[i]).start()
+
+        def wait():
+            for i in range(2):
+                there, cross, where = direct(i)
+
+                @pl.when(jnp.logical_or(there, cross))
+                def _(i=i, where=where):
+                    copy(outs[i], intos[1 - i], i, self.recv.at[n + i], where).wait_send()
+
+                @pl.when(col == outer[1 - i])
+                def _(i=i):
+                    copy(hop, intos[1 - i], i, self.recv.at[n + i], middle[i]).wait_send()
+
+                @pl.when(self.near[2 + i][0])
+                def _(i=i, where=where):
+                    copy(outs[i], intos[i], 1 - i, self.recv.at[n + 1 - i], where).wait_recv()
+
+        self.count += 2
+        return forward, wait
+
+
+def halves(ref, rows):
+    return [[ref.at[side, :, pl.ds(rows * h, rows)] for side in range(2)] for h in range(2)]
+
+
+def groups_before():
+    *_, in_middle, _ = crossing()
+    late = in_middle.astype(jnp.int32)
+    return 1 + late, late
+
 
 def pack(pieces, start):
     lane = lanes(pieces[0].shape[0])
@@ -261,7 +345,7 @@
 
 
 def halo_kernel(
-    pos, obj, amps_far, probe_far, t0_far, t1_far, cur, grads, amps, probe, t0, t1, hv, hc, hd, sc, sd, send, recv, sems
+    pos, obj, amps_far, probe_far, t0_far, t1_far, cur, acc, grads, amps, probe, t0, t1, hv, hc, hd, sc, sd, hop, send, recv, hop_sem, sems
 ):
     near = neighbours()
     greet(near)
@@ -282,6 +366,7 @@
     cur[:, :, BORDER + TILE :, :] = zeros
     cur[:, 0] = jnp.zeros((2, ROWS, 128), f32)
     cur[:, 5] = jnp.zeros((2, ROWS, 128), f32)
+    acc[...] = jnp.zeros_like(acc)
     greeted(near)
     post = Post(near, send, recv)
     waits = [post.pair(0, [obj.at[:, pl.ds(0, 32), :], obj.at[:, pl.ds(TILE - 32, 32), :]], [hv.at[0], hv.at[1]])]
@@ -297,20 +382,26 @@
                 sd[2 * ud + side, p] = pack(
                     [cur[p, block, base + 8 * q : base + 8 * q + 8, :] for q in range(4)], start
                 )
-    sideways = post.pair(2, [sc.at[0], sc.at[1]], [hc.at[0], hc.at[1]])
+    outs, intos = halves(sc, 64), halves(hc, 64)
+    forward, over = post.sideways(outs[1], intos[1], hop, hop_sem.at[0])
+    straight = post.pair(2, outs[0], intos[0])
     waits.append(post.pair(4, [sd.at[0], sd.at[3]], [hd.at[0], hd.at[3]]))
     waits.append(post.pair(5, [sd.at[1], sd.at[2]], [hd.at[1], hd.at[2]]))
     for copy in [tile_at[1], tile_at[2]] + others:
         copy.wait()
     body = keep_gradients(grads, cur, amps, probe, (t0, t1), pos)
+    before, _ = groups_before()
     lax.fori_loop(0, 1, body, 0)
-    sideways()
+    forward()
+    lax.fori_loop(1, before, body, 0)
+    straight()
+    over()
     for p in range(2):
         for side in range(2):
             for q, piece in enumerate(unpack(hc[side, p], 96 - 96 * side)):
                 at = BORDER + 128 * q
                 cur[p, 5 * side, at : at + 128, :] = present(near, 2 + side, piece)
-    lax.fori_loop(1, PMAX // GROUP, body, 0)
+    lax.fori_loop(before, PMAX // GROUP, body, 0)
     for wait in waits:
         wait()
     for p in range(2):
@@ -323,12 +414,13 @@
                     cur[p, 5 * side, base + 8 * q : base + 8 * q + 8, :] = present(near, 4 + 2 * k + side, piece)
 
 
-def first_kernel(count, pos, cur, grads, amps, probe, t0, t1, acc, after, todo):
-    acc[...] = jnp.zeros_like(acc)
+def first_kernel(count, pos, acc_in, cur, grads, amps, probe, t0, t1, acc, todo):
+    del acc_in
+    early = GROUP * groups_before()[0]
 
     def sort(s, amount):
         done = jnp.logical_and(
-            rows_within(pos, s, 0), jnp.logical_or(s >= GROUP, columns_within(pos, s, 0))
+            rows_within(pos, s, 0), jnp.logical_or(s >= early, columns_within(pos, s, 0))
         )
 
         @pl.when(done)
@@ -343,7 +435,6 @@
 
     amount = lax.fori_loop(0, count[0, 0], sort, jnp.int32(0))
     listed_slots(amount, todo, pos, cur, acc, amps, probe, (t0, t1))
-    after[...] = cur[...] + step_of(probe) * acc[...]
 
 
 def side_sums(near, rc, rm, side, p):
@@ -356,12 +447,10 @@
 
 
 def strip_kernel(
-    pos, acc, cur_in, amps, probe, t0, t1, grads, cur, rv, rs, rc, rm, sv, ss, sc, sm, send, recv, sems
+    pos, acc, cur_in, amps, probe, t0, t1, grads, cur, rv, rs, rc, rm, sv, ss, sc, sm, hop, send, recv, hop_sem
 ):
     near = neighbours()
     greet(near)
-    same = pltpu.make_async_copy(cur_in, cur, sems.at[0])
-    same.start()
     for p in range(2):
         for side in range(2):
             for ud in range(2):
@@ -380,7 +469,11 @@
     for p in range(2):
         for side in range(2):
             sm[side, p] = pack_two(seam(acc[p, 4 * side, 64:TILE, :], acc[p, 4 * side + 1, 64:TILE, :]))
-    middle = post.pair(2, [sm.at[0], sm.at[1]], [rm.at[0], rm.at[1]])
+    outs, intos = halves(sm, 112), halves(rm, 112)
+    forward, over = post.sideways(outs[1], intos[1], hop, hop_sem.at[0])
+    straight = post.pair(2, outs[0], intos[0])
+    step = step_of(probe)
+    cur[...] = cur_in[...] + step * acc[...]
     corners()
     lane = lanes(64)
     for p in range(2):
@@ -396,18 +489,21 @@
             post.pair(0, [sv.at[ud, :, n] for ud in range(2)], [rv.at[ud, :, block] for ud in range(2)])
         )
     waits.append(post.pair(0, [ss.at[0], ss.at[1]], [rs.at[0], rs.at[1]]))
-    same.wait()
-    middle()
-    step = step_of(probe)
+    for side in range(2):
+        cur[:, 5 * side] = present(near, 2 + side, cur[:, 5 * side])
+    forward()
+    body = keep_gradients(grads, cur, amps, probe, (t0, t1), pos)
+    _, before = groups_before()
+    lax.fori_loop(0, before, body, 0)
+    straight()
+    over()
     for p in range(2):
         for side in range(2):
             for rows, value in side_sums(near, rc, rm, side, p):
                 lane = lanes(value.shape[0])
-                cur[p, 4 * side, rows, :] += step * jnp.where(lane >= 96, value, 0.0)
-                cur[p, 4 * side + 1, rows, :] += step * jnp.where(lane < 32, value, 0.0)
-    for side in range(2):
-        cur[:, 5 * side] = present(near, 2 + side, cur[:, 5 * side])
-    lax.fori_loop(0, PMAX // GROUP, keep_gradients(grads, cur, amps, probe, (t0, t1), pos), 0)
+                for block, mine in ((4 * side, lane >= 96), (4 * side + 1, lane < 32)):
+                    cur[p, block, rows, :] += step * jnp.where(mine, value, 0.0)
+    lax.fori_loop(before, PMAX // GROUP, body, 0)
     for wait in waits:
         wait()
 
@@ -418,6 +514,7 @@
     near = neighbours()
     step = step_of(probe)
     del acc_in, cur_in
+    early = GROUP * groups_before()[1]
 
     def add(p, block, rows, value):
         acc[p, block, rows, :] += value
@@ -451,7 +548,9 @@
 
     def sort(s, carry):
         amount, held = carry
-        done = rows_within(pos, s, BORDER)
+        done = jnp.logical_and(
+            rows_within(pos, s, BORDER), jnp.logical_or(s >= early, columns_within(pos, s, BORDER))
+        )
         inner = jnp.logical_and(rows_within(pos, s, 0), columns_within(pos, s, 0))
         hold = jnp.logical_and(jnp.logical_and(inner, held < LATE), jnp.logical_not(done))
 
@@ -475,7 +574,7 @@
     listed_slots(amount, todo, pos, cur, acc, amps, probe, (t0, t1))
 
 
-def fold_kernel(pos, late, acc, cur, amps, probe, t0, t1, grads, gv, gc, gd, sc, sd, send, recv):
+def fold_kernel(pos, late, acc, cur, amps, probe, t0, t1, grads, gv, gc, gd, sc, sd, hop, send, recv, hop_sem):
     near = neighbours()
     greet(near)
     for p in range(2):
@@ -502,7 +601,10 @@
             sc[side, p] = pack(
                 [acc[p, 5 * side, BORDER + 128 * q : BORDER + 128 * q + 128, :] for q in range(4)], 96 - 96 * side
             )
-    waits.append(post.pair(2, [sc.at[0], sc.at[1]], [gc.at[0], gc.at[1]]))
+    outs, intos = halves(sc, 64), halves(gc, 64)
+    forward, over = post.sideways(outs[1], intos[1], hop, hop_sem.at[0])
+    waits.append(post.pair(2, outs[0], intos[0]))
+    waits.append(over)
 
     def body(i, carry):
         slots = [jnp.minimum(late[i * GROUP + k], PMAX - 1) for k in range(GROUP)]
@@ -512,6 +614,7 @@
         return carry
 
     lax.fori_loop(0, LATE // GROUP, body, 0)
+    forward()
     for wait in waits:
         wait()
 
@@ -591,33 +694,36 @@
         pltpu.with_memory_space_constraint(x, pltpu.HBM)
         for x in (object_field, amplitudes, probe_field, *tabs)
     ]
-    cur, grads, *shared = pl.pallas_call(
+    cur, acc, grads, *shared = pl.pallas_call(
         halo_kernel,
-        out_shape=[tile, kept] + [jax.ShapeDtypeStruct(x.shape, x.dtype) for x in (amplitudes, probe_field, *tabs)],
+        out_shape=[tile, tile, kept] + [jax.ShapeDtypeStruct(x.shape, x.dtype) for x in (amplitudes, probe_field, *tabs)],
         in_specs=[SM] + [HBM] * 5,
-        out_specs=[VM] * 6,
+        out_specs=[VM] * 7,
         scratch_shapes=[
             pltpu.VMEM((2, 2, 32, TILE), f32),
             pltpu.VMEM((2, 2, 128, 128), f32),
             pltpu.VMEM((4, 2, 8, 128), f32),
             pltpu.VMEM((2, 2, 128, 128), f32),
             pltpu.VMEM((4, 2, 8, 128), f32),
-            dma((8,)),
-            dma((8,)),
+            pltpu.VMEM((2, 64, 128), f32),
+            dma((10,)),
+            dma((10,)),
+            dma((1,)),
             dma((8,)),
         ],
         compiler_params=remote_params(0),
         name="halo",
     )(positions, *far)
-    acc, after = pl.pallas_call(
+    acc = pl.pallas_call(
         first_kernel,
-        out_shape=(tile, tile),
-        in_specs=[SM, SM] + [VM] * 6,
-        out_specs=[VM] * 2,
+        out_shape=tile,
+        in_specs=[SM, SM] + [VM] * 7,
+        out_specs=VM,
         scratch_shapes=[pltpu.SMEM((PMAX,), jnp.int32)],
+        input_output_aliases={2: 0},
         compiler_params=params(),
         name="first",
-    )(counts, positions, cur, grads, *shared)
+    )(counts, positions, acc, cur, grads, *shared)
     strips = ((2, 2, 4, 64, 128), (2, 2, 32, 128), (2, 2, 2, 32, 128), (2, 2, 224, 128))
     grads, cur, *got = pl.pallas_call(
         strip_kernel,
@@ -629,13 +735,14 @@
             pltpu.VMEM((2, 2, 32, 128), f32),
             pltpu.VMEM((2, 2, 2, 32, 128), f32),
             pltpu.VMEM((2, 2, 224, 128), f32),
-            dma((12,)),
-            dma((12,)),
+            pltpu.VMEM((2, 112, 128), f32),
+            dma((14,)),
+            dma((14,)),
             dma((1,)),
         ],
         compiler_params=remote_params(1),
         name="strips",
-    )(positions, acc, after, *shared)
+    )(positions, acc, cur, *shared)
     acc, cur, late = pl.pallas_call(
         second_kernel,
         out_shape=(tile, tile, shape(LATE, dtype=jnp.int32)),
@@ -655,8 +762,10 @@
         scratch_shapes=[
             pltpu.VMEM((2, 2, 128, 128), f32),
             pltpu.VMEM((4, 2, 8, 128), f32),
-            dma((8,)),
-            dma((8,)),
+            pltpu.VMEM((2, 64, 128), f32),
+            dma((10,)),
+            dma((10,)),
+            dma((1,)),
         ],
         compiler_params=remote_params(2),
         name="folds",

time: 63.8 us -> 75.9 us (1.19)
  the two profiles are of different devices: /device:TPU:15 before, /device:TPU:8 now
where the time goes in v4:
time: 75.9 us; the launch traced here: 74.6 us
  Pallas kernels  72.4 us (95%)
  between operations  1.52 us (2%)
    pallas_call x1, Pallas kernels, on_device(): pl.pallas_call(strip_kernel, out_shape=(kept, tile) + tuple((shape(*s) fo...  26 us
    pallas_call x1, Pallas kernels, on_device(): pl.pallas_call(halo_kernel, out_shape=[tile, tile, kept] + [jax.ShapeDtyp...  22.8 us
    pallas_call x1, Pallas kernels, on_device(): pl.pallas_call(fold_kernel, out_shape=(shape(LATE, 2, PROBE, PROBE),) + t...  11.6 us
    pallas_call x1, Pallas kernels, on_device(): pl.pallas_call(second_kernel, out_shape=(tile, tile, shape(LATE, dtype=jn...  4.65 us
    pallas_call x1, Pallas kernels, on_device(): pl.pallas_call(first_kernel, out_shape=tile, in_specs=[SM, SM] + [VM] * 7...  3.79 us
    pallas_call x1, Pallas kernels, on_device(): pl.pallas_call(last_kernel, out_shape=(shape(2, TILE, TILE), shape(2, TIL...  3.5 us

profile of v4, /device:TPU:8, one launch (start us, length us, event | category | flops | bytes accessed | tf_op | source)
XLA Modules:
  0.0 74.6 jit_solution(17860317472437397649)
XLA Ops:
  1.3 0.0 copy-start.1
  1.3 0.7 copy-done.1
  2.0 22.8 %halo.1 = (f32[2,6,576,128]{3,2,1,0:T(8,128)S(1)}, f32[2,6,576,128]{3,2,1,0:T(8,128)S(1)}, f32[24,2,128,128]{3,2,1,0:T(8,128)S(1)}, f32[24,128,128]{2,1,0:T(8,12...) custom-call(s32[1,1,2,24]{3,2,1,0:T(2,128)S(1)} %copy-done.1, ...), custom_call_target="tpu_custom_call" | custom-call | tf_op jit(solution)/shard_map/halo/pallas_call | solution.py:697
  24.8 3.8 %first.1.acc.acc_in = f32[2,6,576,128]{3,2,1,0:T(8,128)S(1)} custom-call(s32[1,1]{1,0:T(1,128)S(6)} %copy.17.count, s32[1,1,2,24]{3,2,1,0:T(2,128)S(1)} %copy-done.1, f32[2,6,576,128]{3,2,1,0:T(8,128)S(1)} %get-tuple-element.24.acc_in, f32[2,6,576,128]{3,2,1,0:T(8,128)S(1)} %get-tuple-element.25.cur.cur_in, ...), custom_call_target="tpu_custom_call", output_to_operand_aliasing={{}: (2, {})} | custom-call | tf_op jit(solution)/shard_map/first/pallas_call | solution.py:717
  28.6 26.0 %strips.1 = (f32[24,2,128,128]{3,2,1,0:T(8,128)S(1)}, f32[2,6,576,128]{3,2,1,0:T(8,128)S(1)}, f32[2,2,4,64,128]{4,3,2,1,0:T(8,128)S(1)}, f32[2,2,32,128]{3,2,1,0...) custom-call(s32[1,1,2,24]{3,2,1,0:T(2,128)S(1)} %copy-done.1, ...), custom_call_target="tpu_custom_call" | custom-call | tf_op jit(solution)/shard_map/strips/pallas_call | solution.py:728
  54.6 4.7 %second.1 = (f32[2,6,576,128]{3,2,1,0:T(8,128)S(1)}, f32[2,6,576,128]{3,2,1,0:T(8,128)S(1)}, s32[8]{0:T(128)S(1)}) custom-call(s32[1,1]{1,0:T(1,128)S(6)} %copy.17.count, s32[1,1,2,24]{3,2,1,0:T(2,128)S(1)} %copy-done.1, f32[2,6,576,128]{3,2,1,0:T(8,128)S(1)} %first.1.acc.acc_in, ...), custom_call_target="tpu_custom_call", output_to_operand_aliasing={{0}: (2, {}), {1}: (3, {})} | custom-call | tf_op jit(solution)/shard_map/second/pallas_call | solution.py:746
  59.3 0.0 copy-start
  59.3 11.6 %folds.1 = (f32[8,2,128,128]{3,2,1,0:T(8,128)S(1)}, f32[2,2,4,32,128]{4,3,2,1,0:T(8,128)S(1)}, f32[2,2,128,128]{3,2,1,0:T(8,128)S(1)}, f32[4,2,8,128]{3,2,1,0:T(8,128)S(1)}) custom-call(s32[1,1,2,24]{3,2,1,0:T(2,128)S(1)} %copy-done.1, s32[8]{0:T(128)S(1)} %get-tuple-element.37.late, f32[2,6,576,128]{3,2,1,0:T(8,128)S(1)} %get-tuple-element.38.acc.acc_in, ...), custom_call_target="tpu_custom_call" | custom-call | tf_op jit(solution)/shard_map/folds/pallas_call | solution.py:757
  70.9 0.0 copy-done
  70.9 3.5 %last.1 = (f32[2,512,512]{2,1,0:T(8,128)}, f32[2,512,512]{2,1,0:T(8,128)}, f32[2,6,576,128]{3,2,1,0:T(8,128)S(1)}) custom-call(s32[1,1,2,24]{3,2,1,0:T(2,128)S(1)} %copy-done.1, s32[8]{0:T(128)S(1)} %get-tuple-element.37.late, f32[2,512,512]{2,1,0:T(8,128)S(1)} %copy-done, ...), custom_call_target="tpu_custom_call", output_to_operand_aliasing={{2}: (3, {})} | custom-call | tf_op jit(solution)/shard_map/last/pallas_call | solution.py:773
Async XLA Ops:
  1.3 0.7 copy-start.1
  59.3 11.6 %copy-start = (f32[2,512,512]{2,1,0:T(8,128)S(1)}, f32[2,512,512]{2,1,0:T(8,128)}, u32[]{:S(2)}) copy-start(f32[2,512,512]{2,1,0:T(8,128)} %obj.3) | copy-start | bytes 6291460

commit v5 on v3

--- a/solution.py
+++ b/solution.py
@@ -212,6 +212,12 @@
         return wait
 
 
+def groups_before():
+    cols, col = lax.axis_size("col"), lax.axis_index("col")
+    late = jnp.logical_or(col == cols // 2 - 1, col == cols // 2).astype(jnp.int32)
+    return 1 + late, late
+
+
 def pack(pieces, start):
     lane = lanes(pieces[0].shape[0])
     out = None
@@ -261,7 +267,7 @@
 
 
 def halo_kernel(
-    pos, obj, amps_far, probe_far, t0_far, t1_far, cur, grads, amps, probe, t0, t1, hv, hc, hd, sc, sd, send, recv, sems
+    pos, obj, amps_far, probe_far, t0_far, t1_far, cur, acc, grads, amps, probe, t0, t1, hv, hc, hd, sc, sd, send, recv, sems
 ):
     near = neighbours()
     greet(near)
@@ -282,9 +288,7 @@
     cur[:, :, BORDER + TILE :, :] = zeros
     cur[:, 0] = jnp.zeros((2, ROWS, 128), f32)
     cur[:, 5] = jnp.zeros((2, ROWS, 128), f32)
-    greeted(near)
-    post = Post(near, send, recv)
-    waits = [post.pair(0, [obj.at[:, pl.ds(0, 32), :], obj.at[:, pl.ds(TILE - 32, 32), :]], [hv.at[0], hv.at[1]])]
+    acc[...] = jnp.zeros_like(acc)
     for side in range(2):
         tile_at[3 * side].wait()
         block, start = 1 + 3 * side, 96 * side
@@ -297,20 +301,24 @@
                 sd[2 * ud + side, p] = pack(
                     [cur[p, block, base + 8 * q : base + 8 * q + 8, :] for q in range(4)], start
                 )
+    greeted(near)
+    post = Post(near, send, recv)
     sideways = post.pair(2, [sc.at[0], sc.at[1]], [hc.at[0], hc.at[1]])
+    waits = [post.pair(0, [obj.at[:, pl.ds(0, 32), :], obj.at[:, pl.ds(TILE - 32, 32), :]], [hv.at[0], hv.at[1]])]
     waits.append(post.pair(4, [sd.at[0], sd.at[3]], [hd.at[0], hd.at[3]]))
     waits.append(post.pair(5, [sd.at[1], sd.at[2]], [hd.at[1], hd.at[2]]))
     for copy in [tile_at[1], tile_at[2]] + others:
         copy.wait()
     body = keep_gradients(grads, cur, amps, probe, (t0, t1), pos)
-    lax.fori_loop(0, 1, body, 0)
+    before, _ = groups_before()
+    lax.fori_loop(0, before, body, 0)
     sideways()
     for p in range(2):
         for side in range(2):
             for q, piece in enumerate(unpack(hc[side, p], 96 - 96 * side)):
                 at = BORDER + 128 * q
                 cur[p, 5 * side, at : at + 128, :] = present(near, 2 + side, piece)
-    lax.fori_loop(1, PMAX // GROUP, body, 0)
+    lax.fori_loop(before, PMAX // GROUP, body, 0)
     for wait in waits:
         wait()
     for p in range(2):
@@ -323,12 +331,13 @@
                     cur[p, 5 * side, base + 8 * q : base + 8 * q + 8, :] = present(near, 4 + 2 * k + side, piece)
 
 
-def first_kernel(count, pos, cur, grads, amps, probe, t0, t1, acc, after, todo):
-    acc[...] = jnp.zeros_like(acc)
+def first_kernel(count, pos, acc_in, cur, grads, amps, probe, t0, t1, acc, todo):
+    del acc_in
+    early = GROUP * groups_before()[0]
 
     def sort(s, amount):
         done = jnp.logical_and(
-            rows_within(pos, s, 0), jnp.logical_or(s >= GROUP, columns_within(pos, s, 0))
+            rows_within(pos, s, 0), jnp.logical_or(s >= early, columns_within(pos, s, 0))
         )
 
         @pl.when(done)
@@ -343,7 +352,6 @@
 
     amount = lax.fori_loop(0, count[0, 0], sort, jnp.int32(0))
     listed_slots(amount, todo, pos, cur, acc, amps, probe, (t0, t1))
-    after[...] = cur[...] + step_of(probe) * acc[...]
 
 
 def side_sums(near, rc, rm, side, p):
@@ -356,12 +364,10 @@
 
 
 def strip_kernel(
-    pos, acc, cur_in, amps, probe, t0, t1, grads, cur, rv, rs, rc, rm, sv, ss, sc, sm, send, recv, sems
+    pos, acc, cur_in, amps, probe, t0, t1, grads, cur, rv, rs, rc, rm, sv, ss, sc, sm, send, recv
 ):
     near = neighbours()
     greet(near)
-    same = pltpu.make_async_copy(cur_in, cur, sems.at[0])
-    same.start()
     for p in range(2):
         for side in range(2):
             for ud in range(2):
@@ -370,6 +376,10 @@
     greeted(near)
     post = Post(near, send, recv)
     corners = post.pair(2, [sc.at[0], sc.at[1]], [rc.at[0], rc.at[1]])
+    for p in range(2):
+        for side in range(2):
+            sm[side, p] = pack_two(seam(acc[p, 4 * side, 64:TILE, :], acc[p, 4 * side + 1, 64:TILE, :]))
+    middle = post.pair(2, [sm.at[0], sm.at[1]], [rm.at[0], rm.at[1]])
     waits = [
         post.pair(
             0,
@@ -377,10 +387,8 @@
             [rv.at[ud, :, pl.ds(1, 2)] for ud in range(2)],
         )
     ]
-    for p in range(2):
-        for side in range(2):
-            sm[side, p] = pack_two(seam(acc[p, 4 * side, 64:TILE, :], acc[p, 4 * side + 1, 64:TILE, :]))
-    middle = post.pair(2, [sm.at[0], sm.at[1]], [rm.at[0], rm.at[1]])
+    step = step_of(probe)
+    cur[...] = cur_in[...] + step * acc[...]
     corners()
     lane = lanes(64)
     for p in range(2):
@@ -396,18 +404,19 @@
             post.pair(0, [sv.at[ud, :, n] for ud in range(2)], [rv.at[ud, :, block] for ud in range(2)])
         )
     waits.append(post.pair(0, [ss.at[0], ss.at[1]], [rs.at[0], rs.at[1]]))
-    same.wait()
+    for side in range(2):
+        cur[:, 5 * side] = present(near, 2 + side, cur[:, 5 * side])
+    body = keep_gradients(grads, cur, amps, probe, (t0, t1), pos)
+    _, before = groups_before()
+    lax.fori_loop(0, before, body, 0)
     middle()
-    step = step_of(probe)
     for p in range(2):
         for side in range(2):
             for rows, value in side_sums(near, rc, rm, side, p):
                 lane = lanes(value.shape[0])
-                cur[p, 4 * side, rows, :] += step * jnp.where(lane >= 96, value, 0.0)
-                cur[p, 4 * side + 1, rows, :] += step * jnp.where(lane < 32, value, 0.0)
-    for side in range(2):
-        cur[:, 5 * side] = present(near, 2 + side, cur[:, 5 * side])
-    lax.fori_loop(0, PMAX // GROUP, keep_gradients(grads, cur, amps, probe, (t0, t1), pos), 0)
+                for block, mine in ((4 * side, lane >= 96), (4 * side + 1, lane < 32)):
+                    cur[p, block, rows, :] += step * jnp.where(mine, value, 0.0)
+    lax.fori_loop(before, PMAX // GROUP, body, 0)
     for wait in waits:
         wait()
 
@@ -418,6 +427,7 @@
     near = neighbours()
     step = step_of(probe)
     del acc_in, cur_in
+    early = GROUP * groups_before()[1]
 
     def add(p, block, rows, value):
         acc[p, block, rows, :] += value
@@ -451,7 +461,9 @@
 
     def sort(s, carry):
         amount, held = carry
-        done = rows_within(pos, s, BORDER)
+        done = jnp.logical_and(
+            rows_within(pos, s, BORDER), jnp.logical_or(s >= early, columns_within(pos, s, BORDER))
+        )
         inner = jnp.logical_and(rows_within(pos, s, 0), columns_within(pos, s, 0))
         hold = jnp.logical_and(jnp.logical_and(inner, held < LATE), jnp.logical_not(done))
 
@@ -486,23 +498,23 @@
                 sd[2 * ud + side, p] = pack(
                     [acc[p, 5 * side, base + 8 * q : base + 8 * q + 8, :] for q in range(4)], start
                 )
+    for p in range(2):
+        for side in range(2):
+            sc[side, p] = pack(
+                [acc[p, 5 * side, BORDER + 128 * q : BORDER + 128 * q + 128, :] for q in range(4)], 96 - 96 * side
+            )
     greeted(near)
     post = Post(near, send, recv)
-    waits = [
+    waits = [post.pair(2, [sc.at[0], sc.at[1]], [gc.at[0], gc.at[1]])]
+    waits.append(
         post.pair(
             0,
             [acc.at[:, pl.ds(1, 4), pl.ds((BORDER + TILE) * ud, BORDER), :] for ud in range(2)],
             [gv.at[0], gv.at[1]],
-        ),
-        post.pair(4, [sd.at[0], sd.at[3]], [gd.at[0], gd.at[3]]),
-        post.pair(5, [sd.at[1], sd.at[2]], [gd.at[1], gd.at[2]]),
-    ]
-    for p in range(2):
-        for side in range(2):
-            sc[side, p] = pack(
-                [acc[p, 5 * side, BORDER + 128 * q : BORDER + 128 * q + 128, :] for q in range(4)], 96 - 96 * side
-            )
-    waits.append(post.pair(2, [sc.at[0], sc.at[1]], [gc.at[0], gc.at[1]]))
+        )
+    )
+    waits.append(post.pair(4, [sd.at[0], sd.at[3]], [gd.at[0], gd.at[3]]))
+    waits.append(post.pair(5, [sd.at[1], sd.at[2]], [gd.at[1], gd.at[2]]))
 
     def body(i, carry):
         slots = [jnp.minimum(late[i * GROUP + k], PMAX - 1) for k in range(GROUP)]
@@ -591,11 +603,11 @@
         pltpu.with_memory_space_constraint(x, pltpu.HBM)
         for x in (object_field, amplitudes, probe_field, *tabs)
     ]
-    cur, grads, *shared = pl.pallas_call(
+    cur, acc, grads, *shared = pl.pallas_call(
         halo_kernel,
-        out_shape=[tile, kept] + [jax.ShapeDtypeStruct(x.shape, x.dtype) for x in (amplitudes, probe_field, *tabs)],
+        out_shape=[tile, tile, kept] + [jax.ShapeDtypeStruct(x.shape, x.dtype) for x in (amplitudes, probe_field, *tabs)],
         in_specs=[SM] + [HBM] * 5,
-        out_specs=[VM] * 6,
+        out_specs=[VM] * 7,
         scratch_shapes=[
             pltpu.VMEM((2, 2, 32, TILE), f32),
             pltpu.VMEM((2, 2, 128, 128), f32),
@@ -609,15 +621,16 @@
         compiler_params=remote_params(0),
         name="halo",
     )(positions, *far)
-    acc, after = pl.pallas_call(
+    acc = pl.pallas_call(
         first_kernel,
-        out_shape=(tile, tile),
-        in_specs=[SM, SM] + [VM] * 6,
-        out_specs=[VM] * 2,
+        out_shape=tile,
+        in_specs=[SM, SM] + [VM] * 7,
+        out_specs=VM,
         scratch_shapes=[pltpu.SMEM((PMAX,), jnp.int32)],
+        input_output_aliases={2: 0},
         compiler_params=params(),
         name="first",
-    )(counts, positions, cur, grads, *shared)
+    )(counts, positions, acc, cur, grads, *shared)
     strips = ((2, 2, 4, 64, 128), (2, 2, 32, 128), (2, 2, 2, 32, 128), (2, 2, 224, 128))
     grads, cur, *got = pl.pallas_call(
         strip_kernel,
@@ -631,11 +644,10 @@
             pltpu.VMEM((2, 2, 224, 128), f32),
             dma((12,)),
             dma((12,)),
-            dma((1,)),
         ],
         compiler_params=remote_params(1),
         name="strips",
-    )(positions, acc, after, *shared)
+    )(positions, acc, cur, *shared)
     acc, cur, late = pl.pallas_call(
         second_kernel,
         out_shape=(tile, tile, shape(LATE, dtype=jnp.int32)),

time: 63.8 us -> 60.8 us (0.953)
  the two profiles are of different devices: /device:TPU:15 before, /device:TPU:8 now
where the time goes in v5:
time: 60.8 us; the launch traced here: 60.3 us
  Pallas kernels  58.1 us (96%)
  between operations  1.5 us (2%)
  local copies, waits for them, and re-layouts  0.68 us (1%)
    pallas_call x1, Pallas kernels, on_device(): pl.pallas_call(strip_kernel, out_shape=(kept, tile) + tuple((shape(*s) fo...  20.8 us
    pallas_call x1, Pallas kernels, on_device(): pl.pallas_call(halo_kernel, out_shape=[tile, tile, kept] + [jax.ShapeDtyp...  13.5 us
    pallas_call x1, Pallas kernels, on_device(): pl.pallas_call(fold_kernel, out_shape=(shape(LATE, 2, PROBE, PROBE),) + t...  11.9 us
    pallas_call x1, Pallas kernels, on_device(): pl.pallas_call(second_kernel, out_shape=(tile, tile, shape(LATE, dtype=jn...  4.66 us
    pallas_call x1, Pallas kernels, on_device(): pl.pallas_call(first_kernel, out_shape=tile, in_specs=[SM, SM] + [VM] * 7...  3.7 us
    pallas_call x1, Pallas kernels, on_device(): pl.pallas_call(last_kernel, out_shape=(shape(2, TILE, TILE), shape(2, TIL...  3.5 us

profile of v5, /device:TPU:8, one launch (start us, length us, event | category | flops | bytes accessed | tf_op | source)
XLA Modules:
  0.0 60.3 jit_solution(15957615976491342291)
XLA Ops:
  1.3 0.0 copy-start.1
  1.3 0.7 %copy-done.1 = s32[1,1,2,24]{3,2,1,0:T(2,128)S(1)} copy-done((s32[1,1,2,24]{3,2,1,0:T(2,128)S(1)}, s32[1,1,2,24]{3,2,1,0:T(2,128)}, u32[]{:S(2)}) %copy-start.1) | copy-done | bytes 216
  2.0 13.5 %halo.1 = (f32[2,6,576,128]{3,2,1,0:T(8,128)S(1)}, f32[2,6,576,128]{3,2,1,0:T(8,128)S(1)}, f32[24,2,128,128]{3,2,1,0:T(8,128)S(1)}, f32[24,128,128]{2,1,0:T(8,12...) custom-call(s32[1,1,2,24]{3,2,1,0:T(2,128)S(1)} %copy-done.1, ...), custom_call_target="tpu_custom_call" | custom-call | tf_op jit(solution)/shard_map/halo/pallas_call | solution.py:606
  15.5 3.7 %first.1.acc.acc_in = f32[2,6,576,128]{3,2,1,0:T(8,128)S(1)} custom-call(s32[1,1]{1,0:T(1,128)S(6)} %copy.17.count, s32[1,1,2,24]{3,2,1,0:T(2,128)S(1)} %copy-done.1, f32[2,6,576,128]{3,2,1,0:T(8,128)S(1)} %get-tuple-element.24.acc_in, f32[2,6,576,128]{3,2,1,0:T(8,128)S(1)} %get-tuple-element.25.cur.cur_in, ...), custom_call_target="tpu_custom_call", output_to_operand_aliasing={{}: (2, {})} | custom-call | tf_op jit(solution)/shard_map/first/pallas_call | solution.py:624
  19.2 20.8 %strips.1 = (f32[24,2,128,128]{3,2,1,0:T(8,128)S(1)}, f32[2,6,576,128]{3,2,1,0:T(8,128)S(1)}, f32[2,2,4,64,128]{4,3,2,1,0:T(8,128)S(1)}, f32[2,2,32,128]{3,2,1,0...) custom-call(s32[1,1,2,24]{3,2,1,0:T(2,128)S(1)} %copy-done.1, ...), custom_call_target="tpu_custom_call" | custom-call | tf_op jit(solution)/shard_map/strips/pallas_call | solution.py:635
  40.0 4.7 %second.1 = (f32[2,6,576,128]{3,2,1,0:T(8,128)S(1)}, f32[2,6,576,128]{3,2,1,0:T(8,128)S(1)}, s32[8]{0:T(128)S(1)}) custom-call(s32[1,1]{1,0:T(1,128)S(6)} %copy.17.count, s32[1,1,2,24]{3,2,1,0:T(2,128)S(1)} %copy-done.1, f32[2,6,576,128]{3,2,1,0:T(8,128)S(1)} %first.1.acc.acc_in, ...), custom_call_target="tpu_custom_call", output_to_operand_aliasing={{0}: (2, {}), {1}: (3, {})} | custom-call | tf_op jit(solution)/shard_map/second/pallas_call | solution.py:651
  44.6 0.0 copy-start
  44.6 11.9 %folds.1 = (f32[8,2,128,128]{3,2,1,0:T(8,128)S(1)}, f32[2,2,4,32,128]{4,3,2,1,0:T(8,128)S(1)}, f32[2,2,128,128]{3,2,1,0:T(8,128)S(1)}, f32[4,2,8,128]{3,2,1,0:T(8,128)S(1)}) custom-call(s32[1,1,2,24]{3,2,1,0:T(2,128)S(1)} %copy-done.1, s32[8]{0:T(128)S(1)} %get-tuple-element.37.late, f32[2,6,576,128]{3,2,1,0:T(8,128)S(1)} %get-tuple-element.38.acc.acc_in, ...), custom_call_target="tpu_custom_call" | custom-call | tf_op jit(solution)/shard_map/folds/pallas_call | solution.py:662
  56.6 0.0 copy-done
  56.6 3.5 %last.1 = (f32[2,512,512]{2,1,0:T(8,128)}, f32[2,512,512]{2,1,0:T(8,128)}, f32[2,6,576,128]{3,2,1,0:T(8,128)S(1)}) custom-call(s32[1,1,2,24]{3,2,1,0:T(2,128)S(1)} %copy-done.1, s32[8]{0:T(128)S(1)} %get-tuple-element.37.late, f32[2,512,512]{2,1,0:T(8,128)S(1)} %copy-done, ...), custom_call_target="tpu_custom_call", output_to_operand_aliasing={{2}: (3, {})} | custom-call | tf_op jit(solution)/shard_map/last/pallas_call | solution.py:676
Async XLA Ops:
  1.3 0.7 %copy-start.1 = (s32[1,1,2,24]{3,2,1,0:T(2,128)S(1)}, s32[1,1,2,24]{3,2,1,0:T(2,128)}, u32[]{:S(2)}) copy-start(s32[1,1,2,24]{3,2,1,0:T(2,128)} %pos.11) | copy-start | bytes 580
  44.6 12.0 %copy-start = (f32[2,512,512]{2,1,0:T(8,128)S(1)}, f32[2,512,512]{2,1,0:T(8,128)}, u32[]{:S(2)}) copy-start(f32[2,512,512]{2,1,0:T(8,128)} %obj.3) | copy-start | bytes 6291460

commit v6 on v5

--- a/solution.py
+++ b/solution.py
@@ -82,12 +82,20 @@
     return out
 
 
-def place(acc, grad, row, col):
+def turned(grad, pos, s):
+    lane = corner_of(pos, s)[1] & 127
+    return [pltpu.roll(g, lane, 1) for g in grad]
+
+
+def place(acc, grad, pos, s):
+    row, col = corner_of(pos, s)
     block, lane = col >> 7, col & 127
-    for p in range(2):
-        g = pltpu.roll(grad[p], lane, 1)
-        acc[p, block, pl.ds(row, PROBE), :] += jnp.where(lanes() >= lane, g, 0.0)
-        acc[p, block + 1, pl.ds(row, PROBE), :] += jnp.where(lanes() >= lane, 0.0, g)
+    rows = pl.ds(row, PROBE)
+    first = lanes() >= lane
+    for p in range(2):
+        a, b = acc[p, block, rows, :], acc[p, block + 1, rows, :]
+        acc[p, block, rows, :] = a + jnp.where(first, grad[p], 0.0)
+        acc[p, block + 1, rows, :] = b + jnp.where(first, 0.0, grad[p])
 
 
 def gradients(cur, amps, probe, tabs, pos, slots, scale=None):
@@ -130,8 +138,9 @@
         slots = [jnp.where(j < amount, todo[j], 0) for j in at]
         scale = [jnp.where(j < amount, 1.0, 0.0) for j in at]
         grads = gradients(cur, amps, probe, tabs, pos, slots, scale)
+        grads = [turned(grad, pos, s) for grad, s in zip(grads, slots)]
         for grad, s in zip(grads, slots):
-            place(acc, grad, *corner_of(pos, s))
+            place(acc, grad, pos, s)
 
     def body(i, carry):
         some(i * GROUP, GROUP)
@@ -258,16 +267,15 @@
 def keep_gradients(grads, cur, amps, probe, tabs, pos):
     def body(i, carry):
         slots = [i * GROUP + k for k in range(GROUP)]
-        for s, (a, b) in zip(slots, gradients(cur, amps, probe, tabs, pos, slots)):
-            grads[s, 0] = a
-            grads[s, 1] = b
+        for s, grad in zip(slots, gradients(cur, amps, probe, tabs, pos, slots)):
+            grads[s, 0], grads[s, 1] = turned(grad, pos, s)
         return carry
 
     return body
 
 
 def halo_kernel(
-    pos, obj, amps_far, probe_far, t0_far, t1_far, cur, acc, grads, amps, probe, t0, t1, hv, hc, hd, sc, sd, send, recv, sems
+    pos_far, obj, amps_far, probe_far, t0_far, t1_far, cur, acc, grads, amps, probe, t0, t1, hv, hc, hd, sc, sd, pos, send, recv, sems
 ):
     near = neighbours()
     greet(near)
@@ -279,7 +287,9 @@
     ]
     others = [
         pltpu.make_async_copy(there, here, sems.at[4 + n])
-        for n, (there, here) in enumerate(((probe_far, probe), (t0_far, t0), (t1_far, t1), (amps_far, amps)))
+        for n, (there, here) in enumerate(
+            ((probe_far, probe), (t0_far, t0), (t1_far, t1), (amps_far, amps), (pos_far, pos))
+        )
     ]
     for copy in [tile_at[j] for j in (0, 3, 1, 2)] + others:
         copy.start()
@@ -342,7 +352,7 @@
 
         @pl.when(done)
         def _():
-            place(acc, (grads[s, 0], grads[s, 1]), *corner_of(pos, s))
+            place(acc, (grads[s, 0], grads[s, 1]), pos, s)
 
         @pl.when(jnp.logical_not(done))
         def _():
@@ -364,7 +374,7 @@
 
 
 def strip_kernel(
-    pos, acc, cur_in, amps, probe, t0, t1, grads, cur, rv, rs, rc, rm, sv, ss, sc, sm, send, recv
+    pos, acc, cur_in, amps, probe, t0, t1, grads, cur, sums, rv, rs, rc, rm, sv, ss, sc, sm, send, recv
 ):
     near = neighbours()
     greet(near)
@@ -404,8 +414,10 @@
             post.pair(0, [sv.at[ud, :, n] for ud in range(2)], [rv.at[ud, :, block] for ud in range(2)])
         )
     waits.append(post.pair(0, [ss.at[0], ss.at[1]], [rs.at[0], rs.at[1]]))
-    for side in range(2):
-        cur[:, 5 * side] = present(near, 2 + side, cur[:, 5 * side])
+    for k in range(2):
+        outside = pl.ds((BORDER + TILE) * k, BORDER)
+        cur[:, :, outside, :] = present(near, k, cur[:, :, outside, :])
+        cur[:, 5 * k] = present(near, 2 + k, cur[:, 5 * k])
     body = keep_gradients(grads, cur, amps, probe, (t0, t1), pos)
     _, before = groups_before()
     lax.fori_loop(0, before, body, 0)
@@ -416,46 +428,45 @@
                 lane = lanes(value.shape[0])
                 for block, mine in ((4 * side, lane >= 96), (4 * side + 1, lane < 32)):
                     cur[p, block, rows, :] += step * jnp.where(mine, value, 0.0)
+        for k in range(2):
+            outside = pl.ds((BORDER + TILE) * k, BORDER)
+            for block in (1, 4):
+                cur[p, block, outside, :] = present(near, k, cur[p, block, outside, :])
+                cur[p, 5 * (block // 4), outside, :] = present(near, k, cur[p, 5 * (block // 4), outside, :])
     lax.fori_loop(before, PMAX // GROUP, body, 0)
+    sums[:, 1:5] = acc[:, 1:5]
+    for p in range(2):
+        for side in range(2):
+            for rows, value in side_sums(near, rc, rm, side, p):
+                lane = lanes(value.shape[0])
+                sums[p, 1 + 3 * side, rows, :] += jnp.where(lane >= 96 if side else lane < 32, value, 0.0)
+    for k in range(2):
+        sums[:, 1:5, pl.ds((BORDER + TILE) * k, BORDER), :] = jnp.zeros((2, 4, BORDER, 128), f32)
+        sums[:, 5 * k] = jnp.zeros((2, ROWS, 128), f32)
     for wait in waits:
         wait()
 
 
 def second_kernel(
-    count, pos, acc_in, cur_in, rv, rs, rc, rm, grads, amps, probe, t0, t1, acc, cur, late, todo
+    count, pos, acc_in, cur_in, rv, rs, grads, amps, probe, t0, t1, acc, cur, late, todo
 ):
     near = neighbours()
     step = step_of(probe)
     del acc_in, cur_in
     early = GROUP * groups_before()[1]
-
-    def add(p, block, rows, value):
-        acc[p, block, rows, :] += value
-        cur[p, block, rows, :] += step * value
-
+    lane = lanes(64)
     for p in range(2):
         for ud in range(2):
             rows = pl.ds(TILE * ud, 64)
+            inner, at = pl.ds(BORDER + (TILE - 32) * ud, 32), slice(32 - 32 * ud, 64 - 32 * ud)
             for j in range(4):
-                add(p, j + 1, rows, present(near, ud, rv[ud, p, j]))
-            sides = present(near, ud, unpack_two(rs[ud, p]))
-            lane = lanes(64)
-            add(p, 0, rows, jnp.where(lane >= 96, sides, 0.0))
-            add(p, 5, rows, jnp.where(lane < 32, sides, 0.0))
-        for side in range(2):
-            block = 1 + 3 * side
-            for rows, value in side_sums(near, rc, rm, side, p):
-                lane = lanes(value.shape[0])
-                acc[p, block, rows, :] += jnp.where(lane >= 96 if side else lane < 32, value, 0.0)
-    for k in range(2):
-        rows = pl.ds((BORDER + TILE) * k, BORDER)
-        cur[:, :, rows, :] = present(near, k, cur[:, :, rows, :])
-        for p in range(2):
-            for r in range(2):
-                at = pl.ds((BORDER + TILE) * r, BORDER)
-                cur[p, 5 * k, at, :] = present(near, 2 + k, cur[p, 5 * k, at, :])
-        acc[:, :, rows, :] = jnp.zeros((2, BLOCKS, BORDER, 128), f32)
-        acc[:, 5 * k] = jnp.zeros((2, ROWS, 128), f32)
+                value = present(near, ud, rv[ud, p, j])
+                cur[p, j + 1, rows, :] += step * value
+                acc[p, j + 1, inner, :] += value[at]
+            value = step * present(near, ud, unpack_two(rs[ud, p]))
+            for side, mine in ((0, lane >= 96), (1, lane < 32)):
+                mine = jnp.logical_and(mine, near[2 + side][0])
+                cur[p, 5 * side, rows, :] += jnp.where(mine, value, 0.0)
     for k in range(LATE):
         late[k] = PMAX
 
@@ -469,7 +480,7 @@
 
         @pl.when(done)
         def _():
-            place(acc, (grads[s, 0], grads[s, 1]), *corner_of(pos, s))
+            place(acc, (grads[s, 0], grads[s, 1]), pos, s)
 
         @pl.when(hold)
         def _():
@@ -518,9 +529,8 @@
 
     def body(i, carry):
         slots = [jnp.minimum(late[i * GROUP + k], PMAX - 1) for k in range(GROUP)]
-        for k, (a, b) in enumerate(gradients(cur, amps, probe, (t0, t1), pos, slots)):
-            grads[i * GROUP + k, 0] = a
-            grads[i * GROUP + k, 1] = b
+        for k, grad in enumerate(gradients(cur, amps, probe, (t0, t1), pos, slots)):
+            grads[i * GROUP + k, 0], grads[i * GROUP + k, 1] = turned(grad, pos, slots[k])
         return carry
 
     lax.fori_loop(0, LATE // GROUP, body, 0)
@@ -538,34 +548,15 @@
 
         @pl.when(s < PMAX)
         def _():
-            place(acc, (grads[k, 0], grads[k, 1]), *corner_of(pos, s))
+            place(acc, (grads[k, 0], grads[k, 1]), pos, s)
 
         return carry
 
     lax.fori_loop(0, LATE, put, 0)
-    for p in range(2):
-        for side in range(2):
-            block, start = 1 + 3 * side, 96 * side
-
-            def mine(rows):
-                return lanes(rows) >= 96 if side else lanes(rows) < 32
-
-            for q, piece in enumerate(unpack(gc[side, p], start)):
-                at = BORDER + 128 * q
-                acc[p, block, at : at + 128, :] += jnp.where(mine(128), present(near, 2 + side, piece), 0.0)
-            for ud in range(2):
-                base = BORDER + (TILE - 32) * ud
-                for q, piece in enumerate(unpack(gd[2 * ud + side, p], start)):
-                    at = base + 8 * q
-                    piece = present(near, 4 + 2 * ud + side, piece)
-                    acc[p, block, at : at + 8, :] += jnp.where(mine(8), piece, 0.0)
-        for ud in range(2):
-            base = BORDER + (TILE - 32) * ud
-            for j in range(4):
-                acc[p, j + 1, base : base + 32, :] += present(near, ud, gv[ud, p, j])
+    inner = pl.ds(BORDER, TILE)
     stores = []
-    inner = pl.ds(BORDER, TILE)
-    for j in range(4):
+
+    def leave(j):
         out = pl.ds(128 * j, 128)
         acc[:, j + 1, inner, :] = step * acc[:, j + 1, inner, :]
         stores.append(pltpu.make_async_copy(acc.at[:, j + 1, inner, :], corr_out.at[:, :, out], sems.at[j]))
@@ -573,6 +564,29 @@
         est[:, j] = obj[:, :, 128 * j : 128 * j + 128] + acc[:, j + 1, inner, :]
         stores.append(pltpu.make_async_copy(est.at[:, j], est_out.at[:, :, out], sems.at[4 + j]))
         stores[-1].start()
+
+    for j in (1, 2, 0, 3):
+        for p in range(2):
+            for ud in range(2):
+                base = BORDER + (TILE - 32) * ud
+                acc[p, j + 1, base : base + 32, :] += present(near, ud, gv[ud, p, j])
+        if j in (0, 3):
+            side, block, start = j // 3, j + 1, 32 * j
+
+            def mine(rows):
+                return lanes(rows) >= 96 if side else lanes(rows) < 32
+
+            for p in range(2):
+                for q, piece in enumerate(unpack(gc[side, p], start)):
+                    at = BORDER + 128 * q
+                    acc[p, block, at : at + 128, :] += jnp.where(mine(128), present(near, 2 + side, piece), 0.0)
+                for ud in range(2):
+                    base = BORDER + (TILE - 32) * ud
+                    for q, piece in enumerate(unpack(gd[2 * ud + side, p], start)):
+                        at = base + 8 * q
+                        piece = present(near, 4 + 2 * ud + side, piece)
+                        acc[p, block, at : at + 8, :] += jnp.where(mine(8), piece, 0.0)
+        leave(j)
     for store in stores:
         store.wait()
 
@@ -601,12 +615,12 @@
     kept = shape(PMAX, 2, PROBE, PROBE)
     far = [
         pltpu.with_memory_space_constraint(x, pltpu.HBM)
-        for x in (object_field, amplitudes, probe_field, *tabs)
+        for x in (positions, object_field, amplitudes, probe_field, *tabs)
     ]
     cur, acc, grads, *shared = pl.pallas_call(
         halo_kernel,
         out_shape=[tile, tile, kept] + [jax.ShapeDtypeStruct(x.shape, x.dtype) for x in (amplitudes, probe_field, *tabs)],
-        in_specs=[SM] + [HBM] * 5,
+        in_specs=[HBM] * 6,
         out_specs=[VM] * 7,
         scratch_shapes=[
             pltpu.VMEM((2, 2, 32, TILE), f32),
@@ -614,13 +628,14 @@
             pltpu.VMEM((4, 2, 8, 128), f32),
             pltpu.VMEM((2, 2, 128, 128), f32),
             pltpu.VMEM((4, 2, 8, 128), f32),
+            pltpu.SMEM((1, 1, 2, PMAX), jnp.int32),
             dma((8,)),
             dma((8,)),
-            dma((8,)),
+            dma((9,)),
         ],
         compiler_params=remote_params(0),
         name="halo",
-    )(positions, *far)
+    )(*far)
     acc = pl.pallas_call(
         first_kernel,
         out_shape=tile,
@@ -632,11 +647,11 @@
         name="first",
     )(counts, positions, acc, cur, grads, *shared)
     strips = ((2, 2, 4, 64, 128), (2, 2, 32, 128), (2, 2, 2, 32, 128), (2, 2, 224, 128))
-    grads, cur, *got = pl.pallas_call(
+    grads, cur, sums, rv, rs, *_ = pl.pallas_call(
         strip_kernel,
-        out_shape=(kept, tile) + tuple(shape(*s) for s in strips),
+        out_shape=(kept, tile, tile) + tuple(shape(*s) for s in strips),
         in_specs=[SM] + [VM] * 6,
-        out_specs=[VM] * 6,
+        out_specs=[VM] * 7,
         scratch_shapes=[
             pltpu.VMEM((2, 2, 2, 64, 128), f32),
             pltpu.VMEM((2, 2, 32, 128), f32),
@@ -651,13 +666,13 @@
     acc, cur, late = pl.pallas_call(
         second_kernel,
         out_shape=(tile, tile, shape(LATE, dtype=jnp.int32)),
-        in_specs=[SM, SM] + [VM] * 11,
+        in_specs=[SM, SM] + [VM] * 9,
         out_specs=[VM, VM, SM],
         scratch_shapes=[pltpu.SMEM((PMAX,), jnp.int32)],
         input_output_aliases={2: 0, 3: 1},
         compiler_params=params(),
         name="second",
-    )(counts, positions, acc, cur, *got, grads, *shared)
+    )(counts, positions, sums, cur, rv, rs, grads, *shared)
     folds = ((2, 2, 4, 32, 128), (2, 2, 128, 128), (4, 2, 8, 128))
     grads, *got = pl.pallas_call(
         fold_kernel,

time: 60.8 us -> 57.7 us (0.949)
  Pallas kernels: 58.1 us -> 55.7 us
  local copies, waits for them, and re-layouts: 0.68 us -> 0.01 us
    pallas_call x1, Pallas kernels: 4.66 us -> 3.59 us  [on_device(): pl.pallas_call(second_kernel, out_shape=(tile, tile, shape(LATE, dtype=jn...]
    pallas_call x1, Pallas kernels: 3.7 us -> 2.71 us  [on_device(): pl.pallas_call(first_kernel, out_shape=tile, in_specs=[SM, SM] + [VM] * 7...]
    pallas_call x1, Pallas kernels: 20.8 us -> 21.6 us  [on_device(): pl.pallas_call(strip_kernel, out_shape=(kept, tile, tile) + tuple((shape(...]
    unnamed x4, local copies, waits for them, and re-layouts: 0.68 us -> 0.01 us
where the time goes in v6:
time: 57.7 us; the launch traced here: 57.3 us
  Pallas kernels  55.7 us (97%)
  between operations  1.54 us (3%)
    pallas_call x1, Pallas kernels, on_device(): pl.pallas_call(strip_kernel, out_shape=(kept, tile, tile) + tuple((shape(...  21.6 us
    pallas_call x1, Pallas kernels, on_device(): pl.pallas_call(halo_kernel, out_shape=[tile, tile, kept] + [jax.ShapeDtyp...  13 us
    pallas_call x1, Pallas kernels, on_device(): pl.pallas_call(fold_kernel, out_shape=(shape(LATE, 2, PROBE, PROBE),) + t...  11.9 us
    pallas_call x1, Pallas kernels, on_device(): pl.pallas_call(second_kernel, out_shape=(tile, tile, shape(LATE, dtype=jn...  3.59 us
    pallas_call x1, Pallas kernels, on_device(): pl.pallas_call(last_kernel, out_shape=(shape(2, TILE, TILE), shape(2, TIL...  2.97 us
    pallas_call x1, Pallas kernels, on_device(): pl.pallas_call(first_kernel, out_shape=tile, in_specs=[SM, SM] + [VM] * 7...  2.71 us

profile of v6, /device:TPU:8, one launch (start us, length us, event | category | flops | bytes accessed | tf_op | source)
XLA Modules:
  0.0 57.3 jit_solution(11880198917726323863)
XLA Ops:
  0.6 0.0 copy-start.1
  1.3 13.0 %halo.1 = (f32[2,6,576,128]{3,2,1,0:T(8,128)S(1)}, f32[2,6,576,128]{3,2,1,0:T(8,128)S(1)}, f32[24,2,128,128]{3,2,1,0:T(8,128)S(1)}, f32[24,128,128]{2,1,0:T(8,12...) custom-call(s32[1,1,2,24]{3,2,1,0:T(2,128)} %pos.9, ...), custom_call_target="tpu_custom_call" | custom-call | tf_op jit(solution)/shard_map/halo/pallas_call | solution.py:620
  14.3 0.0 copy-done.1
  14.3 2.7 %first.1.acc = f32[2,6,576,128]{3,2,1,0:T(8,128)S(1)} custom-call(s32[1,1]{1,0:T(1,128)S(6)} %copy.17.count, s32[1,1,2,24]{3,2,1,0:T(2,128)S(1)} %copy-done.1, f32[2,6,576,128]{3,2,1,0:T(8,128)S(1)} %get-tuple-element.23.acc_in, f32[2,6,576,128]{3,2,1,0:T(8,128)S(1)} %get-tuple-element.24.cur.cur_in, ...), custom_call_target="tpu_custom_call", output_to_operand_aliasing={{}: (2, {})} | custom-call | tf_op jit(solution)/shard_map/first/pallas_call | solution.py:639
  17.1 21.6 %strips.1 = (f32[24,2,128,128]{3,2,1,0:T(8,128)S(1)}, f32[2,6,576,128]{3,2,1,0:T(8,128)S(1)}, f32[2,6,576,128]{3,2,1,0:T(8,128)S(1)}, f32[2,2,4,64,128]{4,3,2,1,...) custom-call(s32[1,1,2,24]{3,2,1,0:T(2,128)S(1)} %copy-done.1, ...), custom_call_target="tpu_custom_call" | custom-call | tf_op jit(solution)/shard_map/strips/pallas_call | solution.py:650
  38.6 3.6 %second.1 = (f32[2,6,576,128]{3,2,1,0:T(8,128)S(1)}, f32[2,6,576,128]{3,2,1,0:T(8,128)S(1)}, s32[8]{0:T(128)S(1)}) custom-call(s32[1,1]{1,0:T(1,128)S(6)} %copy.17.count, s32[1,1,2,24]{3,2,1,0:T(2,128)S(1)} %copy-done.1, f32[2,6,576,128]{3,2,1,0:T(8,128)S(1)} %get-tuple-element.30.acc_in, ...), custom_call_target="tpu_custom_call", output_to_operand_aliasing={{0}: (2, {}), {1}: (3, {})} | custom-call | tf_op jit(solution)/shard_map/second/pallas_call | solution.py:666
  42.2 0.0 copy-start
  42.2 11.9 %folds.1 = (f32[8,2,128,128]{3,2,1,0:T(8,128)S(1)}, f32[2,2,4,32,128]{4,3,2,1,0:T(8,128)S(1)}, f32[2,2,128,128]{3,2,1,0:T(8,128)S(1)}, f32[4,2,8,128]{3,2,1,0:T(8,128)S(1)}) custom-call(s32[1,1,2,24]{3,2,1,0:T(2,128)S(1)} %copy-done.1, s32[8]{0:T(128)S(1)} %get-tuple-element.35.late, f32[2,6,576,128]{3,2,1,0:T(8,128)S(1)} %get-tuple-element.36.acc.acc_in, ...), custom_call_target="tpu_custom_call" | custom-call | tf_op jit(solution)/shard_map/folds/pallas_call | solution.py:677
  54.1 0.0 copy-done
  54.1 3.0 %last.1 = (f32[2,512,512]{2,1,0:T(8,128)}, f32[2,512,512]{2,1,0:T(8,128)}, f32[2,6,576,128]{3,2,1,0:T(8,128)S(1)}) custom-call(s32[1,1,2,24]{3,2,1,0:T(2,128)S(1)} %copy-done.1, s32[8]{0:T(128)S(1)} %get-tuple-element.35.late, f32[2,512,512]{2,1,0:T(8,128)S(1)} %copy-done, ...), custom_call_target="tpu_custom_call", output_to_operand_aliasing={{2}: (3, {})} | custom-call | tf_op jit(solution)/shard_map/last/pallas_call | solution.py:691
Async XLA Ops:
  0.6 13.7 %copy-start.1 = (s32[1,1,2,24]{3,2,1,0:T(2,128)S(1)}, s32[1,1,2,24]{3,2,1,0:T(2,128)}, u32[]{:S(2)}) copy-start(s32[1,1,2,24]{3,2,1,0:T(2,128)} %pos.9) | copy-start | bytes 580
  42.2 11.9 %copy-start = (f32[2,512,512]{2,1,0:T(8,128)S(1)}, f32[2,512,512]{2,1,0:T(8,128)}, u32[]{:S(2)}) copy-start(f32[2,512,512]{2,1,0:T(8,128)} %obj.3) | copy-start | bytes 6291460

commit v7 on v6

--- a/solution.py
+++ b/solution.py
@@ -22,8 +22,8 @@
 bf16 = jnp.bfloat16
 MESH = pl.DeviceIdType.MESH
 
-DIRS = ((-1, 0), (1, 0), (0, -1), (0, 1), (-1, -1), (-1, 1), (1, -1), (1, 1))
-OPP = (1, 0, 3, 2, 7, 6, 5, 4)
+DIRS = ((-1, 0), (1, 0), (0, -1), (0, 1))
+OPP = (1, 0, 3, 2)
 
 
 def tables():
@@ -306,17 +306,10 @@
             sc[side, p] = pack(
                 [cur[p, block, BORDER + 128 * q : BORDER + 128 * q + 128, :] for q in range(4)], start
             )
-            for ud in range(2):
-                base = BORDER + (TILE - 32) * ud
-                sd[2 * ud + side, p] = pack(
-                    [cur[p, block, base + 8 * q : base + 8 * q + 8, :] for q in range(4)], start
-                )
     greeted(near)
     post = Post(near, send, recv)
     sideways = post.pair(2, [sc.at[0], sc.at[1]], [hc.at[0], hc.at[1]])
     waits = [post.pair(0, [obj.at[:, pl.ds(0, 32), :], obj.at[:, pl.ds(TILE - 32, 32), :]], [hv.at[0], hv.at[1]])]
-    waits.append(post.pair(4, [sd.at[0], sd.at[3]], [hd.at[0], hd.at[3]]))
-    waits.append(post.pair(5, [sd.at[1], sd.at[2]], [hd.at[1], hd.at[2]]))
     for copy in [tile_at[1], tile_at[2]] + others:
         copy.wait()
     body = keep_gradients(grads, cur, amps, probe, (t0, t1), pos)
@@ -328,6 +321,10 @@
             for q, piece in enumerate(unpack(hc[side, p], 96 - 96 * side)):
                 at = BORDER + 128 * q
                 cur[p, 5 * side, at : at + 128, :] = present(near, 2 + side, piece)
+        for ud in range(2):
+            rows = pl.ds(BORDER + (TILE - BORDER) * ud, BORDER)
+            sd[ud, p] = pack_two(seam(cur[p, 0, rows, :], cur[p, 5, rows, :]))
+    waits.append(post.pair(0, [sd.at[0], sd.at[1]], [hd.at[0], hd.at[1]]))
     lax.fori_loop(before, PMAX // GROUP, body, 0)
     for wait in waits:
         wait()
@@ -336,9 +333,9 @@
             base = (BORDER + TILE) * k
             for j in range(4):
                 cur[p, j + 1, base : base + 32, :] = present(near, k, hv[k, p, :, 128 * j : 128 * j + 128])
+            beside = present(near, k, unpack_two(hd[k, p]))
             for side in range(2):
-                for q, piece in enumerate(unpack(hd[2 * k + side, p], 96 - 96 * side)):
-                    cur[p, 5 * side, base + 8 * q : base + 8 * q + 8, :] = present(near, 4 + 2 * k + side, piece)
+                cur[p, 5 * side, base : base + 32, :] = beside
 
 
 def first_kernel(count, pos, acc_in, cur, grads, amps, probe, t0, t1, acc, todo):
@@ -498,34 +495,45 @@
     listed_slots(amount, todo, pos, cur, acc, amps, probe, (t0, t1))
 
 
-def fold_kernel(pos, late, acc, cur, amps, probe, t0, t1, grads, gv, gc, gd, sc, sd, send, recv):
+def fold_kernel(pos, late, acc, cur, amps, probe, t0, t1, grads, gv, gc, gd, sc, sd, sv, send, recv):
     near = neighbours()
     greet(near)
     for p in range(2):
         for side in range(2):
-            start = 96 - 96 * side
             for ud in range(2):
                 base = (BORDER + TILE) * ud
-                sd[2 * ud + side, p] = pack(
-                    [acc[p, 5 * side, base + 8 * q : base + 8 * q + 8, :] for q in range(4)], start
+                sd[side, ud, p] = pack(
+                    [acc[p, 5 * side, base + 8 * q : base + 8 * q + 8, :] for q in range(4)], 96 - 96 * side
                 )
+    greeted(near)
+    post = Post(near, send, recv)
+    corners = post.pair(2, [sd.at[0], sd.at[1]], [gd.at[0], gd.at[1]])
+    waits = [
+        post.pair(
+            0,
+            [acc.at[:, pl.ds(2, 2), pl.ds((BORDER + TILE) * ud, BORDER), :] for ud in range(2)],
+            [gv.at[ud, :, pl.ds(1, 2)] for ud in range(2)],
+        )
+    ]
     for p in range(2):
         for side in range(2):
             sc[side, p] = pack(
                 [acc[p, 5 * side, BORDER + 128 * q : BORDER + 128 * q + 128, :] for q in range(4)], 96 - 96 * side
             )
-    greeted(near)
-    post = Post(near, send, recv)
-    waits = [post.pair(2, [sc.at[0], sc.at[1]], [gc.at[0], gc.at[1]])]
-    waits.append(
-        post.pair(
-            0,
-            [acc.at[:, pl.ds(1, 4), pl.ds((BORDER + TILE) * ud, BORDER), :] for ud in range(2)],
-            [gv.at[0], gv.at[1]],
+    waits.append(post.pair(2, [sc.at[0], sc.at[1]], [gc.at[0], gc.at[1]]))
+    corners()
+    lane = lanes(BORDER)
+    for p in range(2):
+        for ud in range(2):
+            rows = pl.ds((BORDER + TILE) * ud, BORDER)
+            for side in range(2):
+                beside = present(near, 2 + side, jnp.concatenate(unpack(gd[side, ud, p], 96 * side), 0))
+                mine = lane >= 96 if side else lane < 32
+                sv[ud, p, side] = acc[p, 1 + 3 * side, rows, :] + jnp.where(mine, beside, 0.0)
+    for side in range(2):
+        waits.append(
+            post.pair(0, [sv.at[ud, :, side] for ud in range(2)], [gv.at[ud, :, 3 * side] for ud in range(2)])
         )
-    )
-    waits.append(post.pair(4, [sd.at[0], sd.at[3]], [gd.at[0], gd.at[3]]))
-    waits.append(post.pair(5, [sd.at[1], sd.at[2]], [gd.at[1], gd.at[2]]))
 
     def body(i, carry):
         slots = [jnp.minimum(late[i * GROUP + k], PMAX - 1) for k in range(GROUP)]
@@ -538,7 +546,7 @@
         wait()
 
 
-def last_kernel(pos, late, obj, acc_in, gv, gc, gd, grads, probe, est_out, corr_out, acc, est, sems):
+def last_kernel(pos, late, obj, acc_in, gv, gc, grads, probe, est_out, corr_out, acc, est, sems):
     near = neighbours()
     del acc_in
     step = step_of(probe)
@@ -580,12 +588,6 @@
                 for q, piece in enumerate(unpack(gc[side, p], start)):
                     at = BORDER + 128 * q
                     acc[p, block, at : at + 128, :] += jnp.where(mine(128), present(near, 2 + side, piece), 0.0)
-                for ud in range(2):
-                    base = BORDER + (TILE - 32) * ud
-                    for q, piece in enumerate(unpack(gd[2 * ud + side, p], start)):
-                        at = base + 8 * q
-                        piece = present(near, 4 + 2 * ud + side, piece)
-                        acc[p, block, at : at + 8, :] += jnp.where(mine(8), piece, 0.0)
         leave(j)
     for store in stores:
         store.wait()
@@ -619,15 +621,16 @@
     ]
     cur, acc, grads, *shared = pl.pallas_call(
         halo_kernel,
-        out_shape=[tile, tile, kept] + [jax.ShapeDtypeStruct(x.shape, x.dtype) for x in (amplitudes, probe_field, *tabs)],
+        out_shape=[tile, tile, kept]
+        + [jax.ShapeDtypeStruct(x.shape, x.dtype) for x in (amplitudes, probe_field, *tabs)],
         in_specs=[HBM] * 6,
         out_specs=[VM] * 7,
         scratch_shapes=[
             pltpu.VMEM((2, 2, 32, TILE), f32),
             pltpu.VMEM((2, 2, 128, 128), f32),
-            pltpu.VMEM((4, 2, 8, 128), f32),
+            pltpu.VMEM((2, 2, 16, 128), f32),
             pltpu.VMEM((2, 2, 128, 128), f32),
-            pltpu.VMEM((4, 2, 8, 128), f32),
+            pltpu.VMEM((2, 2, 16, 128), f32),
             pltpu.SMEM((1, 1, 2, PMAX), jnp.int32),
             dma((8,)),
             dma((8,)),
@@ -673,17 +676,19 @@
         compiler_params=params(),
         name="second",
     )(counts, positions, sums, cur, rv, rs, grads, *shared)
-    folds = ((2, 2, 4, 32, 128), (2, 2, 128, 128), (4, 2, 8, 128))
-    grads, *got = pl.pallas_call(
+    folds = ((2, 2, 4, 32, 128), (2, 2, 128, 128))
+    grads, gv, gc = pl.pallas_call(
         fold_kernel,
         out_shape=(shape(LATE, 2, PROBE, PROBE),) + tuple(shape(*s) for s in folds),
         in_specs=[SM, SM] + [VM] * 6,
-        out_specs=[VM] * 4,
+        out_specs=[VM] * 3,
         scratch_shapes=[
+            pltpu.VMEM((2, 2, 2, 8, 128), f32),
             pltpu.VMEM((2, 2, 128, 128), f32),
-            pltpu.VMEM((4, 2, 8, 128), f32),
-            dma((8,)),
-            dma((8,)),
+            pltpu.VMEM((2, 2, 2, 8, 128), f32),
+            pltpu.VMEM((2, 2, 2, 32, 128), f32),
+            dma((10,)),
+            dma((10,)),
         ],
         compiler_params=remote_params(2),
         name="folds",
@@ -691,13 +696,13 @@
     return pl.pallas_call(
         last_kernel,
         out_shape=(shape(2, TILE, TILE), shape(2, TILE, TILE), tile),
-        in_specs=[SM, SM] + [VM] * 7,
+        in_specs=[SM, SM] + [VM] * 6,
         out_specs=[HBM, HBM, VM],
         scratch_shapes=[pltpu.VMEM((2, 4, TILE, 128), f32), dma((8,))],
         input_output_aliases={3: 2},
         compiler_params=params(),
         name="last",
-    )(positions, late, object_field, acc, *got, grads, shared[1])[:2]
+    )(positions, late, object_field, acc, gv, gc, grads, shared[1])[:2]
 
 
 def solution(mesh):

time: 57.7 us -> 57.1 us (0.990)
  Pallas kernels: 55.7 us -> 54.8 us
    pallas_call x1, Pallas kernels: 11.9 us -> 11.1 us  [on_device(): pl.pallas_call(fold_kernel, out_shape=(shape(LATE, 2, PROBE, PROBE),) + t...]
    pallas_call x1, Pallas kernels: 21.6 us -> 20.8 us  [on_device(): pl.pallas_call(strip_kernel, out_shape=(kept, tile, tile) + tuple((shape(...]
where the time goes in v7:
time: 57.1 us; the launch traced here: 56.4 us
  Pallas kernels  54.8 us (96%)
  between operations  1.54 us (3%)
    pallas_call x1, Pallas kernels, on_device(): pl.pallas_call(strip_kernel, out_shape=(kept, tile, tile) + tuple((shape(...  20.8 us
    pallas_call x1, Pallas kernels, on_device(): pl.pallas_call(halo_kernel, out_shape=[tile, tile, kept] + [jax.ShapeDtyp...  12.6 us
    pallas_call x1, Pallas kernels, on_device(): pl.pallas_call(fold_kernel, out_shape=(shape(LATE, 2, PROBE, PROBE),) + t...  11.1 us
    pallas_call x1, Pallas kernels, on_device(): pl.pallas_call(second_kernel, out_shape=(tile, tile, shape(LATE, dtype=jn...  4.05 us
    pallas_call x1, Pallas kernels, on_device(): pl.pallas_call(first_kernel, out_shape=tile, in_specs=[SM, SM] + [VM] * 7...  3.2 us
    pallas_call x1, Pallas kernels, on_device(): pl.pallas_call(last_kernel, out_shape=(shape(2, TILE, TILE), shape(2, TIL...  3.02 us

profile of v7, /device:TPU:8, one launch (start us, length us, event | category | flops | bytes accessed | tf_op | source)
XLA Modules:
  0.0 56.4 jit_solution(8914278044756393453)
XLA Ops:
  0.6 0.0 copy-start.1
  1.3 12.6 %halo.1 = (f32[2,6,576,128]{3,2,1,0:T(8,128)S(1)}, f32[2,6,576,128]{3,2,1,0:T(8,128)S(1)}, f32[24,2,128,128]{3,2,1,0:T(8,128)S(1)}, f32[24,128,128]{2,1,0:T(8,12...) custom-call(s32[1,1,2,24]{3,2,1,0:T(2,128)} %pos.9, ...), custom_call_target="tpu_custom_call" | custom-call | tf_op jit(solution)/shard_map/halo/pallas_call | solution.py:622
  13.9 0.0 copy-done.1
  13.9 3.2 %first.1.acc = f32[2,6,576,128]{3,2,1,0:T(8,128)S(1)} custom-call(s32[1,1]{1,0:T(1,128)S(6)} %copy.17.count, s32[1,1,2,24]{3,2,1,0:T(2,128)S(1)} %copy-done.1, f32[2,6,576,128]{3,2,1,0:T(8,128)S(1)} %get-tuple-element.22.acc_in, f32[2,6,576,128]{3,2,1,0:T(8,128)S(1)} %get-tuple-element.23.cur.cur_in, ...), custom_call_target="tpu_custom_call", output_to_operand_aliasing={{}: (2, {})} | custom-call | tf_op jit(solution)/shard_map/first/pallas_call | solution.py:642
  17.1 20.8 %strips.1 = (f32[24,2,128,128]{3,2,1,0:T(8,128)S(1)}, f32[2,6,576,128]{3,2,1,0:T(8,128)S(1)}, f32[2,6,576,128]{3,2,1,0:T(8,128)S(1)}, f32[2,2,4,64,128]{4,3,2,1,...) custom-call(s32[1,1,2,24]{3,2,1,0:T(2,128)S(1)} %copy-done.1, ...), custom_call_target="tpu_custom_call" | custom-call | tf_op jit(solution)/shard_map/strips/pallas_call | solution.py:653
  38.0 4.1 %second.1 = (f32[2,6,576,128]{3,2,1,0:T(8,128)S(1)}, f32[2,6,576,128]{3,2,1,0:T(8,128)S(1)}, s32[8]{0:T(128)S(1)}) custom-call(s32[1,1]{1,0:T(1,128)S(6)} %copy.17.count, s32[1,1,2,24]{3,2,1,0:T(2,128)S(1)} %copy-done.1, f32[2,6,576,128]{3,2,1,0:T(8,128)S(1)} %get-tuple-element.29.acc_in, ...), custom_call_target="tpu_custom_call", output_to_operand_aliasing={{0}: (2, {}), {1}: (3, {})} | custom-call | tf_op jit(solution)/shard_map/second/pallas_call | solution.py:669
  42.0 0.0 copy-start
  42.0 11.1 %folds.1 = (f32[8,2,128,128]{3,2,1,0:T(8,128)S(1)}, f32[2,2,4,32,128]{4,3,2,1,0:T(8,128)S(1)}, f32[2,2,128,128]{3,2,1,0:T(8,128)S(1)}) custom-call(s32[1,1,2,24]{3,2,1,0:T(2,128)S(1)} %copy-done.1, s32[8]{0:T(128)S(1)} %get-tuple-element.34.late, f32[2,6,576,128]{3,2,1,0:T(8,128)S(1)} %get-tuple-element.35.acc.acc_in, ...), custom_call_target="tpu_custom_call" | custom-call | tf_op jit(solution)/shard_map/folds/pallas_call | solution.py:680
  53.2 0.0 copy-done
  53.2 3.0 %last.1 = (f32[2,512,512]{2,1,0:T(8,128)}, f32[2,512,512]{2,1,0:T(8,128)}, f32[2,6,576,128]{3,2,1,0:T(8,128)S(1)}) custom-call(s32[1,1,2,24]{3,2,1,0:T(2,128)S(1)} %copy-done.1, s32[8]{0:T(128)S(1)} %get-tuple-element.34.late, f32[2,512,512]{2,1,0:T(8,128)S(1)} %copy-done, ...), custom_call_target="tpu_custom_call", output_to_operand_aliasing={{2}: (3, {})} | custom-call | tf_op jit(solution)/shard_map/last/pallas_call | solution.py:696
Async XLA Ops:
  0.6 13.3 %copy-start.1 = (s32[1,1,2,24]{3,2,1,0:T(2,128)S(1)}, s32[1,1,2,24]{3,2,1,0:T(2,128)}, u32[]{:S(2)}) copy-start(s32[1,1,2,24]{3,2,1,0:T(2,128)} %pos.9) | copy-start | bytes 580
  42.0 11.2 %copy-start = (f32[2,512,512]{2,1,0:T(8,128)S(1)}, f32[2,512,512]{2,1,0:T(8,128)}, u32[]{:S(2)}) copy-start(f32[2,512,512]{2,1,0:T(8,128)} %obj.3) | copy-start | bytes 6291460

commit v8 on v7

--- a/solution.py
+++ b/solution.py
@@ -262,6 +262,15 @@
 
 
 LATE = 8
+
+
+def second_rule(pos, s):
+    early = GROUP * groups_before()[1]
+    done = jnp.logical_and(
+        rows_within(pos, s, BORDER), jnp.logical_or(s >= early, columns_within(pos, s, BORDER))
+    )
+    inner = jnp.logical_and(rows_within(pos, s, 0), columns_within(pos, s, 0))
+    return done, jnp.logical_and(inner, jnp.logical_not(done))
 
 
 def keep_gradients(grads, cur, amps, probe, tabs, pos):
@@ -371,7 +380,7 @@
 
 
 def strip_kernel(
-    pos, acc, cur_in, amps, probe, t0, t1, grads, cur, sums, rv, rs, rc, rm, sv, ss, sc, sm, send, recv
+    pos, acc, cur_in, amps, probe, t0, t1, rate, grads, cur, sums, rv, rs, rc, rm, sv, ss, sc, sm, send, recv
 ):
     near = neighbours()
     greet(near)
@@ -395,6 +404,7 @@
         )
     ]
     step = step_of(probe)
+    rate[...] = jnp.full(rate.shape, step, f32)
     cur[...] = cur_in[...] + step * acc[...]
     corners()
     lane = lanes(64)
@@ -445,12 +455,11 @@
 
 
 def second_kernel(
-    count, pos, acc_in, cur_in, rv, rs, grads, amps, probe, t0, t1, acc, cur, late, todo
+    count, pos, acc_in, cur_in, rv, rs, rate, grads, amps, probe, t0, t1, acc, cur, todo
 ):
     near = neighbours()
-    step = step_of(probe)
+    step = rate[0:1, :]
     del acc_in, cur_in
-    early = GROUP * groups_before()[1]
     lane = lanes(64)
     for p in range(2):
         for ud in range(2):
@@ -464,25 +473,15 @@
             for side, mine in ((0, lane >= 96), (1, lane < 32)):
                 mine = jnp.logical_and(mine, near[2 + side][0])
                 cur[p, 5 * side, rows, :] += jnp.where(mine, value, 0.0)
-    for k in range(LATE):
-        late[k] = PMAX
-
     def sort(s, carry):
         amount, held = carry
-        done = jnp.logical_and(
-            rows_within(pos, s, BORDER), jnp.logical_or(s >= early, columns_within(pos, s, BORDER))
-        )
-        inner = jnp.logical_and(rows_within(pos, s, 0), columns_within(pos, s, 0))
-        hold = jnp.logical_and(jnp.logical_and(inner, held < LATE), jnp.logical_not(done))
+        done, hold = second_rule(pos, s)
+        hold = jnp.logical_and(hold, held < LATE)
 
         @pl.when(done)
         def _():
             place(acc, (grads[s, 0], grads[s, 1]), pos, s)
 
-        @pl.when(hold)
-        def _():
-            late[held] = s
-
         now = jnp.logical_not(jnp.logical_or(done, hold))
 
         @pl.when(now)
@@ -495,7 +494,9 @@
     listed_slots(amount, todo, pos, cur, acc, amps, probe, (t0, t1))
 
 
-def fold_kernel(pos, late, acc, cur, amps, probe, t0, t1, grads, gv, gc, gd, sc, sd, sv, send, recv):
+def fold_kernel(
+    count, pos, acc, cur, amps, probe, t0, t1, grads, gv, gc, gd, sc, sd, sv, late, follow, send, recv
+):
     near = neighbours()
     greet(near)
     for p in range(2):
@@ -535,6 +536,16 @@
             post.pair(0, [sv.at[ud, :, side] for ud in range(2)], [gv.at[ud, :, 3 * side] for ud in range(2)])
         )
 
+    coming = jnp.int32(PMAX)
+    follow[PMAX] = coming
+    for s in range(PMAX - 1, -1, -1):
+        hold = jnp.logical_and(s < count[0, 0], second_rule(pos, s)[1])
+        coming = jnp.where(hold, s, coming)
+        follow[s] = coming
+    for k in range(LATE):
+        late[k] = coming
+        coming = follow[jnp.minimum(coming + 1, PMAX)]
+
     def body(i, carry):
         slots = [jnp.minimum(late[i * GROUP + k], PMAX - 1) for k in range(GROUP)]
         for k, grad in enumerate(gradients(cur, amps, probe, (t0, t1), pos, slots)):
@@ -546,21 +557,21 @@
         wait()
 
 
-def last_kernel(pos, late, obj, acc_in, gv, gc, grads, probe, est_out, corr_out, acc, est, sems):
+def last_kernel(count, pos, obj, acc_in, gv, gc, grads, rate, est_out, corr_out, acc, est, sems):
     near = neighbours()
     del acc_in
-    step = step_of(probe)
-
-    def put(k, carry):
-        s = late[k]
-
-        @pl.when(s < PMAX)
+    step = rate[0:1, :]
+
+    def put(s, held):
+        hold = jnp.logical_and(second_rule(pos, s)[1], held < LATE)
+
+        @pl.when(hold)
         def _():
-            place(acc, (grads[k, 0], grads[k, 1]), pos, s)
-
-        return carry
-
-    lax.fori_loop(0, LATE, put, 0)
+            place(acc, (grads[held, 0], grads[held, 1]), pos, s)
+
+        return held + jnp.where(hold, 1, 0)
+
+    lax.fori_loop(0, count[0, 0], put, jnp.int32(0))
     inner = pl.ds(BORDER, TILE)
     stores = []
 
@@ -650,11 +661,11 @@
         name="first",
     )(counts, positions, acc, cur, grads, *shared)
     strips = ((2, 2, 4, 64, 128), (2, 2, 32, 128), (2, 2, 2, 32, 128), (2, 2, 224, 128))
-    grads, cur, sums, rv, rs, *_ = pl.pallas_call(
+    rate, grads, cur, sums, rv, rs, *_ = pl.pallas_call(
         strip_kernel,
-        out_shape=(kept, tile, tile) + tuple(shape(*s) for s in strips),
+        out_shape=(shape(8, 128), kept, tile, tile) + tuple(shape(*s) for s in strips),
         in_specs=[SM] + [VM] * 6,
-        out_specs=[VM] * 7,
+        out_specs=[VM] * 8,
         scratch_shapes=[
             pltpu.VMEM((2, 2, 2, 64, 128), f32),
             pltpu.VMEM((2, 2, 32, 128), f32),
@@ -666,16 +677,16 @@
         compiler_params=remote_params(1),
         name="strips",
     )(positions, acc, cur, *shared)
-    acc, cur, late = pl.pallas_call(
+    acc, cur = pl.pallas_call(
         second_kernel,
-        out_shape=(tile, tile, shape(LATE, dtype=jnp.int32)),
-        in_specs=[SM, SM] + [VM] * 9,
-        out_specs=[VM, VM, SM],
+        out_shape=(tile, tile),
+        in_specs=[SM, SM] + [VM] * 10,
+        out_specs=[VM, VM],
         scratch_shapes=[pltpu.SMEM((PMAX,), jnp.int32)],
         input_output_aliases={2: 0, 3: 1},
         compiler_params=params(),
         name="second",
-    )(counts, positions, sums, cur, rv, rs, grads, *shared)
+    )(counts, positions, sums, cur, rv, rs, rate, grads, *shared)
     folds = ((2, 2, 4, 32, 128), (2, 2, 128, 128))
     grads, gv, gc = pl.pallas_call(
         fold_kernel,
@@ -687,12 +698,14 @@
             pltpu.VMEM((2, 2, 128, 128), f32),
             pltpu.VMEM((2, 2, 2, 8, 128), f32),
             pltpu.VMEM((2, 2, 2, 32, 128), f32),
+            pltpu.SMEM((LATE,), jnp.int32),
+            pltpu.SMEM((PMAX + 1,), jnp.int32),
             dma((10,)),
             dma((10,)),
         ],
         compiler_params=remote_params(2),
         name="folds",
-    )(positions, late, acc, cur, *shared)
+    )(counts, positions, acc, cur, *shared)
     return pl.pallas_call(
         last_kernel,
         out_shape=(shape(2, TILE, TILE), shape(2, TILE, TILE), tile),
@@ -702,7 +715,7 @@
         input_output_aliases={3: 2},
         compiler_params=params(),
         name="last",
-    )(positions, late, object_field, acc, gv, gc, grads, shared[1])[:2]
+    )(counts, positions, object_field, acc, gv, gc, grads, rate)[:2]
 
 
 def solution(mesh):

time: 57.1 us -> 56.6 us (level)
  the two profiles are of different devices: /device:TPU:8 before, /device:TPU:104 now
where the time goes in v8:
time: 56.6 us; the launch traced here: 56.4 us
  Pallas kernels  54.9 us (97%)
  between operations  1.52 us (3%)
    pallas_call x1, Pallas kernels, on_device(): pl.pallas_call(strip_kernel, out_shape=(shape(8, 128), kept, tile, tile)...  19.9 us
    pallas_call x1, Pallas kernels, on_device(): pl.pallas_call(fold_kernel, out_shape=(shape(LATE, 2, PROBE, PROBE),) + t...  14.4 us
    pallas_call x1, Pallas kernels, on_device(): pl.pallas_call(halo_kernel, out_shape=[tile, tile, kept] + [jax.ShapeDtyp...  12.2 us
    pallas_call x1, Pallas kernels, on_device(): pl.pallas_call(last_kernel, out_shape=(shape(2, TILE, TILE), shape(2, TIL...  2.93 us
    pallas_call x1, Pallas kernels, on_device(): pl.pallas_call(second_kernel, out_shape=(tile, tile), in_specs=[SM, SM] +...  2.8 us
    pallas_call x1, Pallas kernels, on_device(): pl.pallas_call(first_kernel, out_shape=tile, in_specs=[SM, SM] + [VM] * 7...  2.69 us

profile of v8, /device:TPU:104, one launch (start us, length us, event | category | flops | bytes accessed | tf_op | source)
XLA Modules:
  0.0 56.4 jit_solution(893676706049778799)
XLA Ops:
  0.6 0.0 copy-start.1
  1.3 12.2 %halo.1 = (f32[2,6,576,128]{3,2,1,0:T(8,128)S(1)}, f32[2,6,576,128]{3,2,1,0:T(8,128)S(1)}, f32[24,2,128,128]{3,2,1,0:T(8,128)S(1)}, f32[24,128,128]{2,1,0:T(8,12...) custom-call(s32[1,1,2,24]{3,2,1,0:T(2,128)} %pos.9, ...), custom_call_target="tpu_custom_call" | custom-call | tf_op jit(solution)/shard_map/halo/pallas_call | solution.py:633
  13.5 0.0 copy-done.1
  13.5 2.7 %first.1.acc = f32[2,6,576,128]{3,2,1,0:T(8,128)S(1)} custom-call(s32[1,1]{1,0:T(1,128)S(6)} %copy.17.count, s32[1,1,2,24]{3,2,1,0:T(2,128)S(1)} %copy-done.1, f32[2,6,576,128]{3,2,1,0:T(8,128)S(1)} %get-tuple-element.22.acc_in, f32[2,6,576,128]{3,2,1,0:T(8,128)S(1)} %get-tuple-element.23.cur.cur_in, ...), custom_call_target="tpu_custom_call", output_to_operand_aliasing={{}: (2, {})} | custom-call | tf_op jit(solution)/shard_map/first/pallas_call | solution.py:653
  16.2 19.9 %strips.1 = (f32[8,128]{1,0:T(8,128)S(1)}, f32[24,2,128,128]{3,2,1,0:T(8,128)S(1)}, f32[2,6,576,128]{3,2,1,0:T(8,128)S(1)}, f32[2,6,576,128]{3,2,1,0:T(8,128)S(1...) custom-call(s32[1,1,2,24]{3,2,1,0:T(2,128)S(1)} %copy-done.1, ...), custom_call_target="tpu_custom_call" | custom-call | tf_op jit(solution)/shard_map/strips/pallas_call | solution.py:664
  36.1 2.8 %second.1 = (f32[2,6,576,128]{3,2,1,0:T(8,128)S(1)}, f32[2,6,576,128]{3,2,1,0:T(8,128)S(1)}) custom-call(s32[1,1]{1,0:T(1,128)S(6)} %copy.17.count, s32[1,1,2,24]{3,2,1,0:T(2,128)S(1)} %copy-done.1, f32[2,6,576,128]{3,2,1,0:T(8,128)S(1)} %get-tuple-element.29.acc_in, ...), custom_call_target="tpu_custom_call", output_to_operand_aliasing={{0}: (2, {}), {1}: (3, {})} | custom-call | tf_op jit(solution)/shard_map/second/pallas_call | solution.py:680
  38.9 0.0 copy-start
  38.9 14.4 %folds.1 = (f32[8,2,128,128]{3,2,1,0:T(8,128)S(1)}, f32[2,2,4,32,128]{4,3,2,1,0:T(8,128)S(1)}, f32[2,2,128,128]{3,2,1,0:T(8,128)S(1)}) custom-call(s32[1,1]{1,0:T(1,128)S(6)} %copy.17.count, s32[1,1,2,24]{3,2,1,0:T(2,128)S(1)} %copy-done.1, f32[2,6,576,128]{3,2,1,0:T(8,128)S(1)} %get-tuple-element.35.acc.acc_in, ...), custom_call_target="tpu_custom_call" | custom-call | tf_op jit(solution)/shard_map/folds/pallas_call | solution.py:691
  53.3 0.0 copy-done
  53.4 2.9 %last.1 = (f32[2,512,512]{2,1,0:T(8,128)}, f32[2,512,512]{2,1,0:T(8,128)}, f32[2,6,576,128]{3,2,1,0:T(8,128)S(1)}) custom-call(s32[1,1]{1,0:T(1,128)S(6)} %copy.17.count, s32[1,1,2,24]{3,2,1,0:T(2,128)S(1)} %copy-done.1, f32[2,512,512]{2,1,0:T(8,128)S(1)} %copy-done, ...), custom_call_target="tpu_custom_call", output_to_operand_aliasing={{2}: (3, {})} | custom-call | tf_op jit(solution)/shard_map/last/pallas_call | solution.py:709
Async XLA Ops:
  0.6 12.8 %copy-start.1 = (s32[1,1,2,24]{3,2,1,0:T(2,128)S(1)}, s32[1,1,2,24]{3,2,1,0:T(2,128)}, u32[]{:S(2)}) copy-start(s32[1,1,2,24]{3,2,1,0:T(2,128)} %pos.9) | copy-start | bytes 580
  38.9 14.4 %copy-start = (f32[2,512,512]{2,1,0:T(8,128)S(1)}, f32[2,512,512]{2,1,0:T(8,128)}, u32[]{:S(2)}) copy-start(f32[2,512,512]{2,1,0:T(8,128)} %obj.3) | copy-start | bytes 6291460

commit v9 on v8

--- a/solution.py
+++ b/solution.py
@@ -146,12 +146,14 @@
         some(i * GROUP, GROUP)
         return carry
 
-    full = lax.div(amount + GROUP // 2 - 1, GROUP)
+    full = lax.div(amount + 1, GROUP)
     lax.fori_loop(0, full, body, 0)
-
-    @pl.when(amount > full * GROUP)
-    def _():
-        some(full * GROUP, GROUP // 2)
+    rest = amount - full * GROUP
+    for least, size in ((1, 4), (5, 6)):
+
+        @pl.when(jnp.logical_and(rest >= least, rest <= size))
+        def _():
+            some(full * GROUP, size)
 
 
 def step_of(probe):

time: 56.6 us -> 56.1 us (level)
  the two profiles are of different devices: /device:TPU:104 before, /device:TPU:8 now
where the time goes in v9:
time: 56.1 us; the launch traced here: 55.5 us
  Pallas kernels  53.9 us (96%)
  between operations  1.54 us (3%)
    pallas_call x1, Pallas kernels, on_device(): pl.pallas_call(strip_kernel, out_shape=(shape(8, 128), kept, tile, tile)...  21.3 us
    pallas_call x1, Pallas kernels, on_device(): pl.pallas_call(halo_kernel, out_shape=[tile, tile, kept] + [jax.ShapeDtyp...  12.6 us
    pallas_call x1, Pallas kernels, on_device(): pl.pallas_call(fold_kernel, out_shape=(shape(LATE, 2, PROBE, PROBE),) + t...  11.6 us
    pallas_call x1, Pallas kernels, on_device(): pl.pallas_call(last_kernel, out_shape=(shape(2, TILE, TILE), shape(2, TIL...  2.91 us
    pallas_call x1, Pallas kernels, on_device(): pl.pallas_call(second_kernel, out_shape=(tile, tile), in_specs=[SM, SM] +...  2.81 us
    pallas_call x1, Pallas kernels, on_device(): pl.pallas_call(first_kernel, out_shape=tile, in_specs=[SM, SM] + [VM] * 7...  2.7 us

profile of v9, /device:TPU:8, one launch (start us, length us, event | category | flops | bytes accessed | tf_op | source)
XLA Modules:
  0.0 55.5 jit_solution(1349424102645905841)
XLA Ops:
  0.6 0.0 copy-start.1
  1.3 12.6 %halo.1 = (f32[2,6,576,128]{3,2,1,0:T(8,128)S(1)}, f32[2,6,576,128]{3,2,1,0:T(8,128)S(1)}, f32[24,2,128,128]{3,2,1,0:T(8,128)S(1)}, f32[24,128,128]{2,1,0:T(8,12...) custom-call(s32[1,1,2,24]{3,2,1,0:T(2,128)} %pos.9, ...), custom_call_target="tpu_custom_call" | custom-call | tf_op jit(solution)/shard_map/halo/pallas_call | solution.py:635
  13.9 0.0 copy-done.1
  13.9 2.7 %first.1.acc = f32[2,6,576,128]{3,2,1,0:T(8,128)S(1)} custom-call(s32[1,1]{1,0:T(1,128)S(6)} %copy.17.count, s32[1,1,2,24]{3,2,1,0:T(2,128)S(1)} %copy-done.1, f32[2,6,576,128]{3,2,1,0:T(8,128)S(1)} %get-tuple-element.22.acc_in, f32[2,6,576,128]{3,2,1,0:T(8,128)S(1)} %get-tuple-element.23.cur.cur_in, ...), custom_call_target="tpu_custom_call", output_to_operand_aliasing={{}: (2, {})} | custom-call | tf_op jit(solution)/shard_map/first/pallas_call | solution.py:655
  16.6 21.3 %strips.1 = (f32[8,128]{1,0:T(8,128)S(1)}, f32[24,2,128,128]{3,2,1,0:T(8,128)S(1)}, f32[2,6,576,128]{3,2,1,0:T(8,128)S(1)}, f32[2,6,576,128]{3,2,1,0:T(8,128)S(1...) custom-call(s32[1,1,2,24]{3,2,1,0:T(2,128)S(1)} %copy-done.1, ...), custom_call_target="tpu_custom_call" | custom-call | tf_op jit(solution)/shard_map/strips/pallas_call | solution.py:666
  37.9 2.8 %second.1 = (f32[2,6,576,128]{3,2,1,0:T(8,128)S(1)}, f32[2,6,576,128]{3,2,1,0:T(8,128)S(1)}) custom-call(s32[1,1]{1,0:T(1,128)S(6)} %copy.17.count, s32[1,1,2,24]{3,2,1,0:T(2,128)S(1)} %copy-done.1, f32[2,6,576,128]{3,2,1,0:T(8,128)S(1)} %get-tuple-element.29.acc_in, ...), custom_call_target="tpu_custom_call", output_to_operand_aliasing={{0}: (2, {}), {1}: (3, {})} | custom-call | tf_op jit(solution)/shard_map/second/pallas_call | solution.py:682
  40.8 0.0 copy-start
  40.8 11.6 %folds.1 = (f32[8,2,128,128]{3,2,1,0:T(8,128)S(1)}, f32[2,2,4,32,128]{4,3,2,1,0:T(8,128)S(1)}, f32[2,2,128,128]{3,2,1,0:T(8,128)S(1)}) custom-call(s32[1,1]{1,0:T(1,128)S(6)} %copy.17.count, s32[1,1,2,24]{3,2,1,0:T(2,128)S(1)} %copy-done.1, f32[2,6,576,128]{3,2,1,0:T(8,128)S(1)} %get-tuple-element.35.acc.acc_in, ...), custom_call_target="tpu_custom_call" | custom-call | tf_op jit(solution)/shard_map/folds/pallas_call | solution.py:693
  52.4 0.0 copy-done
  52.4 2.9 %last.1 = (f32[2,512,512]{2,1,0:T(8,128)}, f32[2,512,512]{2,1,0:T(8,128)}, f32[2,6,576,128]{3,2,1,0:T(8,128)S(1)}) custom-call(s32[1,1]{1,0:T(1,128)S(6)} %copy.17.count, s32[1,1,2,24]{3,2,1,0:T(2,128)S(1)} %copy-done.1, f32[2,512,512]{2,1,0:T(8,128)S(1)} %copy-done, ...), custom_call_target="tpu_custom_call", output_to_operand_aliasing={{2}: (3, {})} | custom-call | tf_op jit(solution)/shard_map/last/pallas_call | solution.py:711
Async XLA Ops:
  0.6 13.3 %copy-start.1 = (s32[1,1,2,24]{3,2,1,0:T(2,128)S(1)}, s32[1,1,2,24]{3,2,1,0:T(2,128)}, u32[]{:S(2)}) copy-start(s32[1,1,2,24]{3,2,1,0:T(2,128)} %pos.9) | copy-start | bytes 580
  40.8 11.6 %copy-start = (f32[2,512,512]{2,1,0:T(8,128)S(1)}, f32[2,512,512]{2,1,0:T(8,128)}, u32[]{:S(2)}) copy-start(f32[2,512,512]{2,1,0:T(8,128)} %obj.3) | copy-start | bytes 6291460

commit v10 on v9

--- a/solution.py
+++ b/solution.py
@@ -275,18 +275,47 @@
     return done, jnp.logical_and(inner, jnp.logical_not(done))
 
 
-def keep_gradients(grads, cur, amps, probe, tabs, pos):
+def inside(pos, s):
+    return jnp.logical_and(rows_within(pos, s, 0), columns_within(pos, s, 0))
+
+
+def early_order(pos, early, ahead, behind, follow, follow_other):
+    seen, taken = jnp.int32(0), []
+    for s in range(PMAX):
+        own = inside(pos, s)
+        taken.append((own, jnp.logical_and(own, seen < early)))
+        seen = seen + own.astype(jnp.int32)
+    last = jnp.int32(PMAX)
+    follow[PMAX], follow_other[PMAX] = last, last
+    coming, other = last, last
+    for s in range(PMAX - 1, -1, -1):
+        coming, other = jnp.where(taken[s][0], s, coming), jnp.where(taken[s][1], other, s)
+        follow[s], follow_other[s] = coming, other
+    for k in range(PMAX):
+        ahead[k], behind[k] = jnp.minimum(coming, PMAX - 1), jnp.minimum(other, PMAX - 1)
+        coming = follow[jnp.minimum(coming + 1, PMAX)]
+        other = follow_other[jnp.minimum(other + 1, PMAX)]
+
+    def slot_at(k):
+        return jnp.where(k < early, ahead[k], behind[jnp.maximum(k - early, 0)])
+
+    return slot_at
+
+
+def keep_gradients(grads, cur, amps, probe, tabs, pos, slot_at=lambda k: k):
     def body(i, carry):
-        slots = [i * GROUP + k for k in range(GROUP)]
-        for s, grad in zip(slots, gradients(cur, amps, probe, tabs, pos, slots)):
-            grads[s, 0], grads[s, 1] = turned(grad, pos, s)
+        places = [i * GROUP + k for k in range(GROUP)]
+        slots = [slot_at(k) for k in places]
+        for k, s, grad in zip(places, slots, gradients(cur, amps, probe, tabs, pos, slots)):
+            grads[k, 0], grads[k, 1] = turned(grad, pos, s)
         return carry
 
     return body
 
 
 def halo_kernel(
-    pos_far, obj, amps_far, probe_far, t0_far, t1_far, cur, acc, grads, amps, probe, t0, t1, hv, hc, hd, sc, sd, pos, send, recv, sems
+    pos_far, obj, amps_far, probe_far, t0_far, t1_far, cur, acc, grads, amps, probe, t0, t1, hv, hc, hd, sc, sd, pos,
+    ahead, behind, follow, follow_other, send, recv, sems
 ):
     near = neighbours()
     greet(near)
@@ -323,8 +352,9 @@
     waits = [post.pair(0, [obj.at[:, pl.ds(0, 32), :], obj.at[:, pl.ds(TILE - 32, 32), :]], [hv.at[0], hv.at[1]])]
     for copy in [tile_at[1], tile_at[2]] + others:
         copy.wait()
-    body = keep_gradients(grads, cur, amps, probe, (t0, t1), pos)
     before, _ = groups_before()
+    slot_at = early_order(pos, GROUP * before, ahead, behind, follow, follow_other)
+    body = keep_gradients(grads, cur, amps, probe, (t0, t1), pos, slot_at)
     lax.fori_loop(0, before, body, 0)
     sideways()
     for p in range(2):
@@ -353,22 +383,29 @@
     del acc_in
     early = GROUP * groups_before()[0]
 
-    def sort(s, amount):
-        done = jnp.logical_and(
-            rows_within(pos, s, 0), jnp.logical_or(s >= early, columns_within(pos, s, 0))
-        )
+    def sort(s, carry):
+        amount, seen, others = carry
+        own = inside(pos, s)
+        taken = jnp.logical_and(own, seen < early)
+        k = jnp.where(taken, seen, early + others)
+        done = jnp.logical_or(taken, jnp.logical_and(rows_within(pos, s, 0), k < PMAX))
 
         @pl.when(done)
         def _():
-            place(acc, (grads[s, 0], grads[s, 1]), pos, s)
+            place(acc, (grads[k, 0], grads[k, 1]), pos, s)
 
         @pl.when(jnp.logical_not(done))
         def _():
             todo[amount] = s
 
-        return amount + jnp.where(done, 0, 1)
-
-    amount = lax.fori_loop(0, count[0, 0], sort, jnp.int32(0))
+        return (
+            amount + jnp.where(done, 0, 1),
+            seen + jnp.where(own, 1, 0),
+            others + jnp.where(taken, 0, 1),
+        )
+
+    zero = jnp.int32(0)
+    amount, _, _ = lax.fori_loop(0, count[0, 0], sort, (zero, zero, zero))
     listed_slots(amount, todo, pos, cur, acc, amps, probe, (t0, t1))
 
 
@@ -645,6 +682,7 @@
             pltpu.VMEM((2, 2, 128, 128), f32),
             pltpu.VMEM((2, 2, 16, 128), f32),
             pltpu.SMEM((1, 1, 2, PMAX), jnp.int32),
+            *[pltpu.SMEM((n,), jnp.int32) for n in (PMAX, PMAX, PMAX + 1, PMAX + 1)],
             dma((8,)),
             dma((8,)),
             dma((9,)),

time: 56.1 us -> 55.8 us (level)
    pallas_call x1, Pallas kernels: 2.7 us -> 0.97 us  [on_device(): pl.pallas_call(first_kernel, out_shape=tile, in_specs=[SM, SM] + [VM] * 7...]
    pallas_call x1, Pallas kernels: 21.3 us -> 22.6 us  [on_device(): pl.pallas_call(strip_kernel, out_shape=(shape(8, 128), kept, tile, tile)...]
where the time goes in v10:
time: 55.8 us; the launch traced here: 55.2 us
  Pallas kernels  53.7 us (96%)
  between operations  1.54 us (3%)
    pallas_call x1, Pallas kernels, on_device(): pl.pallas_call(strip_kernel, out_shape=(shape(8, 128), kept, tile, tile)...  22.6 us
    pallas_call x1, Pallas kernels, on_device(): pl.pallas_call(halo_kernel, out_shape=[tile, tile, kept] + [jax.ShapeDtyp...  12.6 us
    pallas_call x1, Pallas kernels, on_device(): pl.pallas_call(fold_kernel, out_shape=(shape(LATE, 2, PROBE, PROBE),) + t...  11.7 us
    pallas_call x1, Pallas kernels, on_device(): pl.pallas_call(last_kernel, out_shape=(shape(2, TILE, TILE), shape(2, TIL...  2.86 us
    pallas_call x1, Pallas kernels, on_device(): pl.pallas_call(second_kernel, out_shape=(tile, tile), in_specs=[SM, SM] +...  2.85 us

profile of v10, /device:TPU:8, one launch (start us, length us, event | category | flops | bytes accessed | tf_op | source)
XLA Modules:
  0.0 55.2 jit_solution(1724180096162291310)
XLA Ops:
  0.6 0.0 copy-start.1
  1.3 12.6 %halo.1 = (f32[2,6,576,128]{3,2,1,0:T(8,128)S(1)}, f32[2,6,576,128]{3,2,1,0:T(8,128)S(1)}, f32[24,2,128,128]{3,2,1,0:T(8,128)S(1)}, f32[24,128,128]{2,1,0:T(8,12...) custom-call(s32[1,1,2,24]{3,2,1,0:T(2,128)} %pos.9, ...), custom_call_target="tpu_custom_call" | custom-call | tf_op jit(solution)/shard_map/halo/pallas_call | solution.py:672
  13.9 0.0 copy-done.1
  13.9 1.0 %first.1.acc = f32[2,6,576,128]{3,2,1,0:T(8,128)S(1)} custom-call(s32[1,1]{1,0:T(1,128)S(6)} %copy.17.count, s32[1,1,2,24]{3,2,1,0:T(2,128)S(1)} %copy-done.1, f32[2,6,576,128]{3,2,1,0:T(8,128)S(1)} %get-tuple-element.22.acc_in, f32[2,6,576,128]{3,2,1,0:T(8,128)S(1)} %get-tuple-element.23.cur.cur_in, ...), custom_call_target="tpu_custom_call", output_to_operand_aliasing={{}: (2, {})} | custom-call | tf_op jit(solution)/shard_map/first/pallas_call | solution.py:693
  14.9 22.6 %strips.1 = (f32[8,128]{1,0:T(8,128)S(1)}, f32[24,2,128,128]{3,2,1,0:T(8,128)S(1)}, f32[2,6,576,128]{3,2,1,0:T(8,128)S(1)}, f32[2,6,576,128]{3,2,1,0:T(8,128)S(1...) custom-call(s32[1,1,2,24]{3,2,1,0:T(2,128)S(1)} %copy-done.1, ...), custom_call_target="tpu_custom_call" | custom-call | tf_op jit(solution)/shard_map/strips/pallas_call | solution.py:704
  37.5 2.9 %second.1 = (f32[2,6,576,128]{3,2,1,0:T(8,128)S(1)}, f32[2,6,576,128]{3,2,1,0:T(8,128)S(1)}) custom-call(s32[1,1]{1,0:T(1,128)S(6)} %copy.17.count, s32[1,1,2,24]{3,2,1,0:T(2,128)S(1)} %copy-done.1, f32[2,6,576,128]{3,2,1,0:T(8,128)S(1)} %get-tuple-element.29.acc_in, ...), custom_call_target="tpu_custom_call", output_to_operand_aliasing={{0}: (2, {}), {1}: (3, {})} | custom-call | tf_op jit(solution)/shard_map/second/pallas_call | solution.py:720
  40.4 0.0 copy-start
  40.4 11.7 %folds.1 = (f32[8,2,128,128]{3,2,1,0:T(8,128)S(1)}, f32[2,2,4,32,128]{4,3,2,1,0:T(8,128)S(1)}, f32[2,2,128,128]{3,2,1,0:T(8,128)S(1)}) custom-call(s32[1,1]{1,0:T(1,128)S(6)} %copy.17.count, s32[1,1,2,24]{3,2,1,0:T(2,128)S(1)} %copy-done.1, f32[2,6,576,128]{3,2,1,0:T(8,128)S(1)} %get-tuple-element.35.acc.acc_in, ...), custom_call_target="tpu_custom_call" | custom-call | tf_op jit(solution)/shard_map/folds/pallas_call | solution.py:731
  52.2 0.0 copy-done
  52.2 2.9 %last.1 = (f32[2,512,512]{2,1,0:T(8,128)}, f32[2,512,512]{2,1,0:T(8,128)}, f32[2,6,576,128]{3,2,1,0:T(8,128)S(1)}) custom-call(s32[1,1]{1,0:T(1,128)S(6)} %copy.17.count, s32[1,1,2,24]{3,2,1,0:T(2,128)S(1)} %copy-done.1, f32[2,512,512]{2,1,0:T(8,128)S(1)} %copy-done, ...), custom_call_target="tpu_custom_call", output_to_operand_aliasing={{2}: (3, {})} | custom-call | tf_op jit(solution)/shard_map/last/pallas_call | solution.py:749
Async XLA Ops:
  0.6 13.3 %copy-start.1 = (s32[1,1,2,24]{3,2,1,0:T(2,128)S(1)}, s32[1,1,2,24]{3,2,1,0:T(2,128)}, u32[]{:S(2)}) copy-start(s32[1,1,2,24]{3,2,1,0:T(2,128)} %pos.9) | copy-start | bytes 580
  40.4 11.8 %copy-start = (f32[2,512,512]{2,1,0:T(8,128)S(1)}, f32[2,512,512]{2,1,0:T(8,128)}, u32[]{:S(2)}) copy-start(f32[2,512,512]{2,1,0:T(8,128)} %obj.3) | copy-start | bytes 6291460

commit v11 on v10

--- a/solution.py
+++ b/solution.py
@@ -149,7 +149,7 @@
     full = lax.div(amount + 1, GROUP)
     lax.fori_loop(0, full, body, 0)
     rest = amount - full * GROUP
-    for least, size in ((1, 4), (5, 6)):
+    for least, size in ((1, 2), (3, 4), (5, 6)):
 
         @pl.when(jnp.logical_and(rest >= least, rest <= size))
         def _():

time: 55.8 us -> 56.1 us (level)
  Pallas kernels: 53.7 us -> 54.3 us
    pallas_call x1, Pallas kernels: 0.97 us -> 2.93 us  [on_device(): pl.pallas_call(first_kernel, out_shape=tile, in_specs=[SM, SM] + [VM] * 7...]
    pallas_call x1, Pallas kernels: 22.6 us -> 21.4 us  [on_device(): pl.pallas_call(strip_kernel, out_shape=(shape(8, 128), kept, tile, tile)...]
where the time goes in v11:
time: 56.1 us; the launch traced here: 55.9 us
  Pallas kernels  54.3 us (97%)
  between operations  1.54 us (3%)
    pallas_call x1, Pallas kernels, on_device(): pl.pallas_call(strip_kernel, out_shape=(shape(8, 128), kept, tile, tile)...  21.4 us
    pallas_call x1, Pallas kernels, on_device(): pl.pallas_call(halo_kernel, out_shape=[tile, tile, kept] + [jax.ShapeDtyp...  12.6 us
    pallas_call x1, Pallas kernels, on_device(): pl.pallas_call(fold_kernel, out_shape=(shape(LATE, 2, PROBE, PROBE),) + t...  11.3 us
    pallas_call x1, Pallas kernels, on_device(): pl.pallas_call(last_kernel, out_shape=(shape(2, TILE, TILE), shape(2, TIL...  3.07 us
    pallas_call x1, Pallas kernels, on_device(): pl.pallas_call(second_kernel, out_shape=(tile, tile), in_specs=[SM, SM] +...  3.04 us
    pallas_call x1, Pallas kernels, on_device(): pl.pallas_call(first_kernel, out_shape=tile, in_specs=[SM, SM] + [VM] * 7...  2.93 us

profile of v11, /device:TPU:8, one launch (start us, length us, event | category | flops | bytes accessed | tf_op | source)
XLA Modules:
  0.0 55.9 jit_solution(11918823589905713246)
XLA Ops:
  0.6 0.0 copy-start.1
  1.3 12.6 %halo.1 = (f32[2,6,576,128]{3,2,1,0:T(8,128)S(1)}, f32[2,6,576,128]{3,2,1,0:T(8,128)S(1)}, f32[24,2,128,128]{3,2,1,0:T(8,128)S(1)}, f32[24,128,128]{2,1,0:T(8,12...) custom-call(s32[1,1,2,24]{3,2,1,0:T(2,128)} %pos.9, ...), custom_call_target="tpu_custom_call" | custom-call | tf_op jit(solution)/shard_map/halo/pallas_call | solution.py:672
  13.9 0.0 copy-done.1
  13.9 2.9 %first.1.acc = f32[2,6,576,128]{3,2,1,0:T(8,128)S(1)} custom-call(s32[1,1]{1,0:T(1,128)S(6)} %copy.17.count, s32[1,1,2,24]{3,2,1,0:T(2,128)S(1)} %copy-done.1, f32[2,6,576,128]{3,2,1,0:T(8,128)S(1)} %get-tuple-element.22.acc_in, f32[2,6,576,128]{3,2,1,0:T(8,128)S(1)} %get-tuple-element.23.cur.cur_in, ...), custom_call_target="tpu_custom_call", output_to_operand_aliasing={{}: (2, {})} | custom-call | tf_op jit(solution)/shard_map/first/pallas_call | solution.py:693
  16.9 21.4 %strips.1 = (f32[8,128]{1,0:T(8,128)S(1)}, f32[24,2,128,128]{3,2,1,0:T(8,128)S(1)}, f32[2,6,576,128]{3,2,1,0:T(8,128)S(1)}, f32[2,6,576,128]{3,2,1,0:T(8,128)S(1...) custom-call(s32[1,1,2,24]{3,2,1,0:T(2,128)S(1)} %copy-done.1, ...), custom_call_target="tpu_custom_call" | custom-call | tf_op jit(solution)/shard_map/strips/pallas_call | solution.py:704
  38.3 3.0 %second.1 = (f32[2,6,576,128]{3,2,1,0:T(8,128)S(1)}, f32[2,6,576,128]{3,2,1,0:T(8,128)S(1)}) custom-call(s32[1,1]{1,0:T(1,128)S(6)} %copy.17.count, s32[1,1,2,24]{3,2,1,0:T(2,128)S(1)} %copy-done.1, f32[2,6,576,128]{3,2,1,0:T(8,128)S(1)} %get-tuple-element.29.acc_in, ...), custom_call_target="tpu_custom_call", output_to_operand_aliasing={{0}: (2, {}), {1}: (3, {})} | custom-call | tf_op jit(solution)/shard_map/second/pallas_call | solution.py:720
  41.3 0.0 copy-start
  41.3 11.3 %folds.1 = (f32[8,2,128,128]{3,2,1,0:T(8,128)S(1)}, f32[2,2,4,32,128]{4,3,2,1,0:T(8,128)S(1)}, f32[2,2,128,128]{3,2,1,0:T(8,128)S(1)}) custom-call(s32[1,1]{1,0:T(1,128)S(6)} %copy.17.count, s32[1,1,2,24]{3,2,1,0:T(2,128)S(1)} %copy-done.1, f32[2,6,576,128]{3,2,1,0:T(8,128)S(1)} %get-tuple-element.35.acc.acc_in, ...), custom_call_target="tpu_custom_call" | custom-call | tf_op jit(solution)/shard_map/folds/pallas_call | solution.py:731
  52.6 0.0 copy-done
  52.6 3.1 %last.1 = (f32[2,512,512]{2,1,0:T(8,128)}, f32[2,512,512]{2,1,0:T(8,128)}, f32[2,6,576,128]{3,2,1,0:T(8,128)S(1)}) custom-call(s32[1,1]{1,0:T(1,128)S(6)} %copy.17.count, s32[1,1,2,24]{3,2,1,0:T(2,128)S(1)} %copy-done.1, f32[2,512,512]{2,1,0:T(8,128)S(1)} %copy-done, ...), custom_call_target="tpu_custom_call", output_to_operand_aliasing={{2}: (3, {})} | custom-call | tf_op jit(solution)/shard_map/last/pallas_call | solution.py:749
Async XLA Ops:
  0.6 13.3 %copy-start.1 = (s32[1,1,2,24]{3,2,1,0:T(2,128)S(1)}, s32[1,1,2,24]{3,2,1,0:T(2,128)}, u32[]{:S(2)}) copy-start(s32[1,1,2,24]{3,2,1,0:T(2,128)} %pos.9) | copy-start | bytes 580
  41.3 11.3 %copy-start = (f32[2,512,512]{2,1,0:T(8,128)S(1)}, f32[2,512,512]{2,1,0:T(8,128)}, u32[]{:S(2)}) copy-start(f32[2,512,512]{2,1,0:T(8,128)} %obj.3) | copy-start | bytes 6291460
